TPU v7x, 32 devices: a whole 2x2x4 slice. The times are simulated.
32 devices in a mesh: mem: 16 (over z, x, core), lat: 2 (over y).
Axes of the slice: x: 2, y: 2, z: 4, core: 2. Of those that a mesh axis runs over, the one named last changes fastest.
Arguments:
- background: float32 [128, 128, 2, 256], P('lat', 'mem'), may hold values from -16 to 16, as said below
- wind_east: bfloat16 [128, 256], P('lat'), may hold values from -0.8984375 to 0.8984375
- wind_north: bfloat16 [128, 256], P('lat'), may hold values from -0.8984375 to 0.8984375
- obs_index: int32 [2, 64, 1, 128], P('lat', 'mem'), may hold values from 0 to 511
- obs_value: float32 [2, 64, 1, 128], P('lat', 'mem'), may hold values from -4 to 4
- obs_scale: float32 [2, 64, 1, 128], P('lat', 'mem'), may hold values from 1 to 8
Outputs:
- analysis: float32 [128, 128, 2, 256], P('lat', 'mem')
Inputs may be any that keep to these rules, and one draw needn't show every extreme that they name: `background`: Members' states.
All inputs are finite; a program needn't handle non-finite values.
Results may differ from a plain program's by a relative error of at most 0.0043.
Values may be sent and summed in bfloat16 or wider, within the bound.
No kernel may reach another device: no remote copies, remote signals or barrier semaphores. Data moves between devices by JAX's collectives and lax.ppermute only.
A program may use at most 64 MiB of HBM per device.

v0:
```python
import math

import jax
import jax.numpy as jnp
from jax import lax
from jax.sharding import PartitionSpec as P

PW = 256
NOBS = 128
STEPS = 4
ITERS = 12


HIGHEST = lax.Precision.HIGHEST


def padded_2(block, sides, width, periodic):
    for axis, dim in sides:
        count = lax.axis_size(axis)
        forward = [(i, i + 1) for i in range(count - 1)]
        if periodic:
            forward.append((count - 1, 0))
        backward = [(target, source) for source, target in forward]
        low = lax.ppermute(
            lax.slice_in_dim(block, block.shape[dim] - width, None, axis=dim), axis, forward
        )
        high = lax.ppermute(lax.slice_in_dim(block, 0, width, axis=dim), axis, backward)
        block = jnp.concatenate([low, block, high], axis=dim)
    return block


def tendency(padded, circumpolar_wind_speed, poleward_wind_speed):
    center_rows = padded[1:-1]
    along_diff = jnp.roll(center_rows, -1, axis=-1) - jnp.roll(center_rows, 1, axis=-1)
    across_diff = padded[2:] - padded[:-2]
    return -0.5 * (circumpolar_wind_speed * along_diff + poleward_wind_speed * across_diff)


def make_blocks(model_variables, index_rows, value_rows, scale_rows):
    row_count, members, flat_width = model_variables.shape
    patch_count = index_rows.shape[1]
    obs_count = index_rows.shape[2]
    fields = flat_width // (patch_count * PW)
    patch_values = model_variables.reshape(row_count, members, fields, patch_count, PW)
    value_ids = lax.broadcasted_iota(jnp.int32, (fields * PW, 1), 0)
    selector = (value_ids[None, None] == index_rows[:, :, None, :]).astype(jnp.float32)
    selector = selector.reshape(row_count, patch_count, fields, PW, obs_count)
    picked = jnp.einsum("akfpt,apftj->akpj", patch_values, selector, precision=HIGHEST)
    average = jnp.mean(picked, axis=1)
    spread = (picked - average[:, None]) * scale_rows[:, None] / math.sqrt(members - 1)
    innovation = (value_rows - average) * scale_rows
    return jnp.concatenate([spread, innovation[:, None]], axis=1).astype(jnp.bfloat16)


def edge_pair(extended):
    return jnp.stack([extended[-1], extended[0]])


def rows_beside(local_rows, extended, banded):
    position = lax.axis_index("mem")
    last_index = lax.axis_size("mem") - 1
    upper_rim = jnp.where(position == 0, banded[0], extended[0])
    lower_rim = jnp.where(position == last_index, banded[3], extended[-1])
    upper_adjacent = jnp.concatenate([upper_rim[None], local_rows[:-1]], axis=0)
    bottom_adjacent = jnp.concatenate([local_rows[1:], lower_rim[None]], axis=0)
    return (upper_adjacent, bottom_adjacent)


def per_device(background, wind_east, wind_north, obs_index, obs_value, obs_scale):
    current = background
    stacked_winds = jnp.stack([wind_east, wind_north])
    wide_winds = padded_2(stacked_winds, (("lat", 1),), 3, False).astype(jnp.float32)
    east_wide = wide_winds[0][:, None, None, :]
    north_wide = wide_winds[1][:, None, None, :]
    span = east_wide.shape[0]
    for step_index in range(STEPS):
        extended = padded_2(current, (("lat", 0),), 4, False)
        slope_one = tendency(extended, east_wide, north_wide)
        slope_two = tendency(
            extended[1:-1] + 0.5 * slope_one, east_wide[1 : span - 1], north_wide[1 : span - 1]
        )
        slope_three = tendency(
            extended[2:-2] + 0.5 * slope_two, east_wide[2 : span - 2], north_wide[2 : span - 2]
        )
        slope_four = tendency(
            extended[3:-3] + slope_three, east_wide[3 : span - 3], north_wide[3 : span - 3]
        )
        current = (
            extended[4:-4]
            + (slope_one[3:-3] + 2.0 * slope_two[2:-2] + 2.0 * slope_three[1:-1] + slope_four) / 6.0
        )
    points = lax.all_to_all(current, "mem", split_axis=0, concat_axis=1, tiled=True)
    row_count, members, fields, width = points.shape
    patch_count = obs_index.shape[2]
    model_variables = points.reshape(row_count, members, fields * width)
    index_rows = obs_index.reshape(row_count, patch_count, NOBS)
    value_rows = obs_value.reshape(row_count, patch_count, NOBS)
    scale_rows = obs_scale.reshape(row_count, patch_count, NOBS)
    own_block = make_blocks(model_variables, index_rows, value_rows, scale_rows)
    extended = padded_2(own_block, (("mem", 0),), 1, True)
    banded = padded_2(edge_pair(extended), (("lat", 0),), 1, False)
    upper_adjacent, bottom_adjacent = rows_beside(own_block, extended, banded)
    gram_sum = jnp.zeros((row_count, patch_count, members + 1, members + 1), jnp.float32)
    for neighbor_block in (
        own_block,
        jnp.roll(own_block, -1, axis=2),
        jnp.roll(own_block, 1, axis=2),
        upper_adjacent,
        bottom_adjacent,
    ):
        gram_sum = gram_sum + jnp.einsum(
            "akpj,alpj->apkl", neighbor_block, neighbor_block, preferred_element_type=jnp.float32
        )
    identity = jnp.eye(members, dtype=jnp.float32)
    system = identity + gram_sum[:, :, :members, :members]
    coupling = gram_sum[:, :, :members, members]
    trace_sum = jnp.trace(system, axis1=2, axis2=3)
    scaled = system / trace_sum[:, :, None, None]

    def newton(turn_index, carry):
        upper_iter, lower_iter = carry
        factor = 1.5 * identity - 0.5 * jnp.einsum(
            "apij,apjk->apik", lower_iter, upper_iter, precision=HIGHEST
        )
        return (
            jnp.einsum("apij,apjk->apik", upper_iter, factor, precision=HIGHEST),
            jnp.einsum("apij,apjk->apik", factor, lower_iter, precision=HIGHEST),
        )

    start_lower = jnp.broadcast_to(identity, scaled.shape)
    upper_iter, lower_iter = lax.fori_loop(0, ITERS, newton, (scaled, start_lower))
    inv_root = lower_iter / jnp.sqrt(trace_sum)[:, :, None, None]
    half_step = jnp.einsum("apkl,apl->apk", inv_root, coupling, precision=HIGHEST)
    mean_weight = jnp.einsum("apkl,apl->apk", inv_root, half_step, precision=HIGHEST) / math.sqrt(
        members - 1
    )
    weights = mean_weight[:, :, :, None] + inv_root
    patch_values = points.reshape(row_count, members, fields, patch_count, PW)
    center = jnp.mean(patch_values, axis=1)
    result = center[:, None] + jnp.einsum(
        "akfpt,apki->aifpt", patch_values - center[:, None], weights, precision=HIGHEST
    )
    analysis = result.reshape(row_count, members, fields, width)
    return lax.all_to_all(analysis, "mem", split_axis=1, concat_axis=0, tiled=True)


def solution(mesh):
    in_specs = (
        P("lat", "mem", None, None),
        P("lat", None),
        P("lat", None),
        P("lat", "mem", None, None),
        P("lat", "mem", None, None),
        P("lat", "mem", None, None),
    )
    out_specs = P("lat", "mem", None, None)
    return jax.shard_map(
        per_device, mesh=mesh, in_specs=in_specs, out_specs=out_specs, check_vma=False
    )
```

profile of v0, /device:TPU:0, one launch (start us, length us, event | category | flops | bytes accessed | tf_op | source)
XLA Modules:
  0.0 245.6 jit_solution(18216593775091099222)
XLA Ops:
  0.8 4.9 %collective-permute-start = (bf16[2,3,256]{2,1,0:T(4,128)(2,1)S(1)}, bf16[2,3,256]{2,1,0:T(4,128)(2,1)S(1)}, u32[]{:S(2)}, u32[]{:S(2)}) collective-permute-start(bf16[2,3,256]{2,1,0:T(4,128)(2,1)S(1)} %get-tuple-element.159), channel_id=1, source_target_pairs={{0,1},{2,3},{4,5},{6,7},{8,9},{10,11},{12,13},{14,15},{16,17},{18,... | collective-permute-start | bytes 9224 | tf_op jit(solution)/shard_map/ppermute | solution.py:24
  7.9 4.5 %collective-permute-start.2 = (f32[4,8,2,256]{3,2,1,0:T(2,128)S(1)}, f32[4,8,2,256]{3,2,1,0:T(2,128)S(1)}, u32[]{:S(2)}, u32[]{:S(2)}) collective-permute-start(f32[4,8,2,256]{3,2,1,0:T(2,128)S(1)} %get-tuple-element.146), channel_id=1, source_target_pairs={{0,1},{2,3},{4,5},{6,7},{8,9},{10,11},{12,13},{14,15},{16,17},{18,... | collective-permute-start | bytes 196616 | tf_op jit(solution)/shard_map/ppermute | solution.py:24
  15.1 3.5 %collective-permute-done.3 = f32[4,8,2,256]{3,2,1,0:T(2,128)S(1)} collective-permute-done((f32[4,8,2,256]{3,2,1,0:T(2,128)S(1)}, f32[4,8,2,256]{3,2,1,0:T(2,128)S(1)}, u32[]{:S(2)}, u32[]{:S(2)}) %collective-permute-start.3) | collective-permute-done | bytes 65568 | tf_op jit(solution)/shard_map/ppermute | solution.py:27
  21.0 4.1 %slice_add_fusion.3 = (f32[70,8,2,256]{3,2,1,0:T(2,128)S(1)}, f32[70,8,2,256]{3,2,1,0:T(2,128)S(1)}) fusion(f32[72,8,2,256]{3,2,1,0:T(2,128)S(1)} %constant_dynamic-update-slice_fusion, f32[70,256]{1,0:T(8,128)S(1)} %get-tuple-element.154, f32[70,8,2,255]{3,2,1,0:T(2,128)S(1)} %get-tuple-element.88, f32[70,8,2,1]{3,2,1,0:T(2,128)S(1)} %get-tuple-element.90, ...), kind=kLoop, calls=%fused_computation.31 | loop fusion | flops 2580480 | bytes 8171520 | tf_op jit(solution)/shard_map/add | solution.py:80
  27.4 3.5 %slice_add_fusion.7 = (f32[68,8,2,256]{3,2,1,0:T(2,128)S(1)}, f32[68,8,2,256]{3,2,1,0:T(2,128)S(1)}) fusion(f32[72,8,2,256]{3,2,1,0:T(2,128)S(1)} %constant_dynamic-update-slice_fusion, f32[70,8,2,256]{3,2,1,0:T(2,128)S(1)} %get-tuple-element.73, f32[68,256]{1,0:T(8,128)S(1)} %get-tuple-element.152, f32[68,8,2,255]{3,2,1,0:T(2,128)S(1)} %get-tuple-element.104, ...), kind=kLoop, calls=%fused_computation.55 | loop fusion | flops 2506752 | bytes 7938048 | tf_op jit(solution)/shard_map/add | solution.py:83
  33.1 3.5 %slice_add_fusion.11 = (f32[66,8,2,256]{3,2,1,0:T(2,128)S(1)}, f32[66,8,2,256]{3,2,1,0:T(2,128)S(1)}) fusion(f32[72,8,2,256]{3,2,1,0:T(2,128)S(1)} %constant_dynamic-update-slice_fusion, f32[68,8,2,256]{3,2,1,0:T(2,128)S(1)} %get-tuple-element.71, f32[66,256]{1,0:T(8,128)S(1)} %get-tuple-element.150, f32[66,8,2,255]{3,2,1,0:T(2,128)S(1)} %get-tuple-element.120, ...), kind=kLoop, calls=%fused_computation.83 | loop fusion | flops 2433024 | bytes 7704576 | tf_op jit(solution)/shard_map/add | solution.py:86
  38.8 4.1 %multiply_add_fusion.3 = f32[64,8,2,256]{3,2,1,0:T(2,128)S(1)} fusion(f32[64,8,2,256]{3,2,1,0:T(2,128)S(1)} %copy-done, f32[66,8,2,256]{3,2,1,0:T(2,128)S(1)} %get-tuple-element.69, f32[64,8,2,255]{3,2,1,0:T(2,128)S(1)} %get-tuple-element.136, f32[64,8,2,1]{3,2,1,0:T(2,128)S(1)} %get-tuple-element.138, f32[64,8,2,1]{3,2,1,0:T(2,128)S(1)} %get-tuple-element.137, ...), kind=kLoop, calls=%fused_computation.154 | loop fusion | flops 4456448 | bytes 9568256 | tf_op jit(solution)/shard_map/add | solution.py:89
  42.9 1.6 collective-permute-start.4
  46.4 4.3 %collective-permute-done.5 = f32[4,8,2,256]{3,2,1,0:T(2,128)S(1)} collective-permute-done((f32[4,8,2,256]{3,2,1,0:T(2,128)S(1)}, f32[4,8,2,256]{3,2,1,0:T(2,128)S(1)}, u32[]{:S(2)}, u32[]{:S(2)}) %collective-permute-start.5) | collective-permute-done | bytes 65568 | tf_op jit(solution)/shard_map/ppermute | solution.py:27
  53.7 3.8 %slice_add_fusion.2 = (f32[70,8,2,256]{3,2,1,0:T(2,128)S(1)}, f32[70,8,2,256]{3,2,1,0:T(2,128)S(1)}) fusion(f32[72,8,2,256]{3,2,1,0:T(2,128)S(1)} %pad_maximum_fusion, f32[70,256]{1,0:T(8,128)S(1)} %get-tuple-element.154, f32[70,8,2,255]{3,2,1,0:T(2,128)S(1)} %get-tuple-element.84, f32[70,8,2,1]{3,2,1,0:T(2,128)S(1)} %get-tuple-element.86, ...), kind=kLoop, calls=%fused_computation.27 | loop fusion | flops 2580480 | bytes 8171520 | tf_op jit(solution)/shard_map/add | solution.py:80
  59.8 3.5 %slice_add_fusion.6 = (f32[68,8,2,256]{3,2,1,0:T(2,128)S(1)}, f32[68,8,2,256]{3,2,1,0:T(2,128)S(1)}) fusion(f32[72,8,2,256]{3,2,1,0:T(2,128)S(1)} %pad_maximum_fusion, f32[70,8,2,256]{3,2,1,0:T(2,128)S(1)} %get-tuple-element.67, f32[68,256]{1,0:T(8,128)S(1)} %get-tuple-element.152, f32[68,8,2,255]{3,2,1,0:T(2,128)S(1)} %get-tuple-element.100, ...), kind=kLoop, calls=%fused_computation.51 | loop fusion | flops 2506752 | bytes 7938048 | tf_op jit(solution)/shard_map/add | solution.py:83
  65.5 3.6 %slice_add_fusion.10 = (f32[66,8,2,256]{3,2,1,0:T(2,128)S(1)}, f32[66,8,2,256]{3,2,1,0:T(2,128)S(1)}) fusion(f32[72,8,2,256]{3,2,1,0:T(2,128)S(1)} %pad_maximum_fusion, f32[68,8,2,256]{3,2,1,0:T(2,128)S(1)} %get-tuple-element.65, f32[66,256]{1,0:T(8,128)S(1)} %get-tuple-element.150, f32[66,8,2,255]{3,2,1,0:T(2,128)S(1)} %get-tuple-element.116, ...), kind=kLoop, calls=%fused_computation.78 | loop fusion | flops 2433024 | bytes 7704576 | tf_op jit(solution)/shard_map/add | solution.py:86
  71.3 4.1 %multiply_add_fusion.2 = f32[64,8,2,256]{3,2,1,0:T(2,128)S(1)} fusion(f32[64,8,2,256]{3,2,1,0:T(2,128)S(1)} %multiply_add_fusion.3, f32[66,8,2,256]{3,2,1,0:T(2,128)S(1)} %get-tuple-element.63, f32[64,8,2,255]{3,2,1,0:T(2,128)S(1)} %get-tuple-element.132, f32[64,8,2,1]{3,2,1,0:T(2,128)S(1)} %get-tuple-element.134, ...), kind=kLoop, calls=%fused_computation.153 | loop fusion | flops 4456448 | bytes 9568256 | tf_op jit(solution)/shard_map/add | solution.py:89
  75.4 1.6 collective-permute-start.6
  78.9 4.3 %collective-permute-done.7 = f32[4,8,2,256]{3,2,1,0:T(2,128)S(1)} collective-permute-done((f32[4,8,2,256]{3,2,1,0:T(2,128)S(1)}, f32[4,8,2,256]{3,2,1,0:T(2,128)S(1)}, u32[]{:S(2)}, u32[]{:S(2)}) %collective-permute-start.7) | collective-permute-done | bytes 65568 | tf_op jit(solution)/shard_map/ppermute | solution.py:27
  86.2 4.0 %slice_add_fusion.1 = (f32[70,8,2,256]{3,2,1,0:T(2,128)S(1)}, f32[70,8,2,256]{3,2,1,0:T(2,128)S(1)}) fusion(f32[72,8,2,256]{3,2,1,0:T(2,128)S(1)} %pad_maximum_fusion.1, f32[70,256]{1,0:T(8,128)S(1)} %get-tuple-element.154, f32[70,8,2,255]{3,2,1,0:T(2,128)S(1)} %get-tuple-element.80, f32[70,8,2,1]{3,2,1,0:T(2,128)S(1)} %get-tuple-element.82, ...), kind=kLoop, calls=%fused_computation.23 | loop fusion | flops 2580480 | bytes 8171520 | tf_op jit(solution)/shard_map/add | solution.py:80
  92.5 3.5 %slice_add_fusion.5 = (f32[68,8,2,256]{3,2,1,0:T(2,128)S(1)}, f32[68,8,2,256]{3,2,1,0:T(2,128)S(1)}) fusion(f32[72,8,2,256]{3,2,1,0:T(2,128)S(1)} %pad_maximum_fusion.1, f32[70,8,2,256]{3,2,1,0:T(2,128)S(1)} %get-tuple-element.61, f32[68,256]{1,0:T(8,128)S(1)} %get-tuple-element.152, f32[68,8,2,255]{3,2,1,0:T(2,128)S(1)} %get-tuple-element.96, ...), kind=kLoop, calls=%fused_computation.47 | loop fusion | flops 2506752 | bytes 7938048 | tf_op jit(solution)/shard_map/add | solution.py:83
  98.3 3.5 %slice_add_fusion.9 = (f32[66,8,2,256]{3,2,1,0:T(2,128)S(1)}, f32[66,8,2,256]{3,2,1,0:T(2,128)S(1)}) fusion(f32[72,8,2,256]{3,2,1,0:T(2,128)S(1)} %pad_maximum_fusion.1, f32[68,8,2,256]{3,2,1,0:T(2,128)S(1)} %get-tuple-element.59, f32[66,256]{1,0:T(8,128)S(1)} %get-tuple-element.150, f32[66,8,2,255]{3,2,1,0:T(2,128)S(1)} %get-tuple-element.112, ...), kind=kLoop, calls=%fused_computation.73 | loop fusion | flops 2433024 | bytes 7704576 | tf_op jit(solution)/shard_map/add | solution.py:86
  104.0 4.1 %multiply_add_fusion.1 = f32[64,8,2,256]{3,2,1,0:T(2,128)S(1)} fusion(f32[64,8,2,256]{3,2,1,0:T(2,128)S(1)} %multiply_add_fusion.2, f32[66,8,2,256]{3,2,1,0:T(2,128)S(1)} %get-tuple-element.57, f32[64,8,2,255]{3,2,1,0:T(2,128)S(1)} %get-tuple-element.128, f32[64,8,2,1]{3,2,1,0:T(2,128)S(1)} %get-tuple-element.130, ...), kind=kLoop, calls=%fused_computation.152 | loop fusion | flops 4456448 | bytes 9568256 | tf_op jit(solution)/shard_map/add | solution.py:89
  108.1 1.6 collective-permute-start.8
  111.5 4.3 %collective-permute-done.9 = f32[4,8,2,256]{3,2,1,0:T(2,128)S(1)} collective-permute-done((f32[4,8,2,256]{3,2,1,0:T(2,128)S(1)}, f32[4,8,2,256]{3,2,1,0:T(2,128)S(1)}, u32[]{:S(2)}, u32[]{:S(2)}) %collective-permute-start.9) | collective-permute-done | bytes 65568 | tf_op jit(solution)/shard_map/ppermute | solution.py:27
  118.8 3.8 %slice_add_fusion = (f32[70,8,2,256]{3,2,1,0:T(2,128)S(1)}, f32[70,8,2,256]{3,2,1,0:T(2,128)S(1)}) fusion(f32[72,8,2,256]{3,2,1,0:T(2,128)S(1)} %pad_maximum_fusion.2, f32[70,256]{1,0:T(8,128)S(1)} %get-tuple-element.154, f32[70,8,2,255]{3,2,1,0:T(2,128)S(1)} %get-tuple-element.76, f32[70,8,2,1]{3,2,1,0:T(2,128)S(1)} %get-tuple-element.78, ...), kind=kLoop, calls=%fused_computation.19 | loop fusion | flops 2580480 | bytes 8171520 | tf_op jit(solution)/shard_map/add | solution.py:80
  124.9 3.5 %slice_add_fusion.4 = (f32[68,8,2,256]{3,2,1,0:T(2,128)S(1)}, f32[68,8,2,256]{3,2,1,0:T(2,128)S(1)}) fusion(f32[72,8,2,256]{3,2,1,0:T(2,128)S(1)} %pad_maximum_fusion.2, f32[70,8,2,256]{3,2,1,0:T(2,128)S(1)} %get-tuple-element.55, f32[68,256]{1,0:T(8,128)S(1)} %get-tuple-element.152, f32[68,8,2,255]{3,2,1,0:T(2,128)S(1)} %get-tuple-element.92, ...), kind=kLoop, calls=%fused_computation.43 | loop fusion | flops 2506752 | bytes 7938048 | tf_op jit(solution)/shard_map/add | solution.py:83
  130.7 3.6 %slice_add_fusion.8 = (f32[66,8,2,256]{3,2,1,0:T(2,128)S(1)}, f32[66,8,2,256]{3,2,1,0:T(2,128)S(1)}) fusion(f32[72,8,2,256]{3,2,1,0:T(2,128)S(1)} %pad_maximum_fusion.2, f32[68,8,2,256]{3,2,1,0:T(2,128)S(1)} %get-tuple-element.53, f32[66,256]{1,0:T(8,128)S(1)} %get-tuple-element.150, f32[66,8,2,255]{3,2,1,0:T(2,128)S(1)} %get-tuple-element.108, ...), kind=kLoop, calls=%fused_computation.68 | loop fusion | flops 2433024 | bytes 7704576 | tf_op jit(solution)/shard_map/add | solution.py:86
  136.4 5.4 %multiply_add_fusion = f32[64,8,2,256]{3,2,1,0:T(2,128)} fusion(f32[64,8,2,256]{3,2,1,0:T(2,128)S(1)} %multiply_add_fusion.1, f32[66,8,2,256]{3,2,1,0:T(2,128)S(1)} %get-tuple-element.51, f32[64,8,2,255]{3,2,1,0:T(2,128)S(1)} %get-tuple-element.124, f32[64,8,2,1]{3,2,1,0:T(2,128)S(1)} %get-tuple-element.126, f32[64,8,2,1]{3,2,1,0:T(2,128)S(1)} %get-tuple-element.125, ...), kind=kLoop, calls=%fused_computation.151 | loop fusion | flops 4456448 | bytes 9568256 | tf_op jit(solution)/shard_map/add | solution.py:89
  141.9 6.0 %all-to-all-start = ((f32[64,8,2,256]{3,2,1,0:T(2,128)}), f32[64,8,2,256]{3,2,1,0:T(2,128)S(1)}, u32[]{:S(2)}, u32[]{:S(2)}) async-start(f32[64,8,2,256]{3,2,1,0:T(2,128)} %multiply_add_fusion), calls=%async_computation | async-start | bytes 2097152 | tf_op jit(solution)/shard_map/all_to_all | solution.py:92
  148.1 22.8 %all-to-all-done = f32[64,8,2,256]{3,2,1,0:T(2,128)S(1)} async-done(((f32[64,8,2,256]{3,2,1,0:T(2,128)}), f32[64,8,2,256]{3,2,1,0:T(2,128)S(1)}, u32[]{:S(2)}, u32[]{:S(2)}) %all-to-all-start) | async-done | bytes 1048608 | tf_op jit(solution)/shard_map/all_to_all | solution.py:92
  172.4 5.4 %collective-permute-start.12 = (bf16[1,129,1,128]{3,1,0,2:T(8,128)(2,1)S(1)}, bf16[1,129,1,128]{3,1,0,2:T(8,128)(2,1)S(1)}, u32[]{:S(2)}, u32[]{:S(2)}) collective-permute-start(bf16[1,129,1,128]{3,1,0,2:T(8,128)(2,1)S(1)} %get-tuple-element.157), channel_id=1, source_target_pairs={{2,0},{4,2},{6,4},{8,6},{10,8},{12,10},{14,12},{16,14},{18,16},{20... | collective-permute-start | bytes 99080 | tf_op jit(solution)/shard_map/ppermute | solution.py:27
  178.1 5.8 %collective-permute-done.10 = bf16[1,129,1,128]{3,1,0,2:T(8,128)(2,1)S(1)} collective-permute-done((bf16[1,129,1,128]{3,1,0,2:T(8,128)(2,1)S(1)}, bf16[1,129,1,128]{3,1,0,2:T(8,128)(2,1)S(1)}, u32[]{:S(2)}, u32[]{:S(2)}) %collective-permute-start.10) | collective-permute-done | bytes 33056 | tf_op jit(solution)/shard_map/ppermute | solution.py:24
  187.3 4.0 %collective-permute-done.13 = bf16[1,129,1,128]{3,1,0,2:T(8,128)(2,1)S(1)} collective-permute-done((bf16[1,129,1,128]{3,1,0,2:T(8,128)(2,1)S(1)}, bf16[1,129,1,128]{3,1,0,2:T(8,128)(2,1)S(1)}, u32[]{:S(2)}, u32[]{:S(2)}) %collective-permute-start.13) | collective-permute-done | bytes 33056 | tf_op jit(solution)/shard_map/ppermute | solution.py:27
  191.9 21.2 %while.13 = (s32[]{:T(128)}, f32[4,1,128,128]{2,3,0,1:T(8,128)S(1)}, f32[4,1,128,128]{3,2,0,1:T(8,128)S(1)}, s32[]{:T(128)}) while((s32[]{:T(128)}, f32[4,1,128,128]{2,3,0,1:T(8,128)S(1)}, f32[4,1,128,128]{3,2,0,1:T(8,128)S(1)}, s32[]{:T(128)}) %tuple.81), condition=%wide.region_4.5_spmd.clone, body=%wide.region_3.4_spmd.clone.sunk | while | flops 302153728 | bytes 3538997 | solution.py:131
  216.3 27.4 %all_to_all.33 = f32[4,128,2,256]{3,2,0,1:T(2,128)S(1)} all-to-all(f32[4,128,2,256]{3,2,0,1:T(2,128)S(1)} %copy.30), channel_id=1, replica_groups=mesh['mem'=16,'lat'=2] {'mem'}, dimensions={1} | all-to-all | bytes 2097152 | tf_op jit(solution)/shard_map/all_to_all | solution.py:144
  (171 shorter events, 80.0 us)
Async XLA Ops:
  0.0 14.7 %copy-start = (f32[64,8,2,256]{3,2,1,0:T(2,128)S(1)}, f32[64,8,2,256]{3,2,1,0:T(2,128)}, u32[]{:S(2)}) copy-start(f32[64,8,2,256]{3,2,1,0:T(2,128)} %param.8) | copy-start | bytes 3145732
  0.8 12.9 %collective-permute-start = (bf16[2,3,256]{2,1,0:T(4,128)(2,1)S(1)}, bf16[2,3,256]{2,1,0:T(4,128)(2,1)S(1)}, u32[]{:S(2)}, u32[]{:S(2)}) collective-permute-start(bf16[2,3,256]{2,1,0:T(4,128)(2,1)S(1)} %get-tuple-element.159), channel_id=1, source_target_pairs={{0,1},{2,3},{4,5},{6,7},{8,9},{10,11},{12,13},{14,15},{16,17},{18,... | collective-permute-start | bytes 9224 | tf_op jit(solution)/shard_map/ppermute | solution.py:24
  5.7 8.1 %collective-permute-start.1 = (bf16[2,3,256]{2,1,0:T(4,128)(2,1)S(1)}, bf16[2,3,256]{2,1,0:T(4,128)(2,1)S(1)}, u32[]{:S(2)}, u32[]{:S(2)}) collective-permute-start(bf16[2,3,256]{2,1,0:T(4,128)(2,1)S(1)} %get-tuple-element.160), channel_id=1, source_target_pairs={{1,0},{3,2},{5,4},{7,6},{9,8},{11,10},{13,12},{15,14},{17,16},{19,... | collective-permute-start | bytes 9224 | tf_op jit(solution)/shard_map/ppermute | solution.py:27
  7.9 6.8 %collective-permute-start.2 = (f32[4,8,2,256]{3,2,1,0:T(2,128)S(1)}, f32[4,8,2,256]{3,2,1,0:T(2,128)S(1)}, u32[]{:S(2)}, u32[]{:S(2)}) collective-permute-start(f32[4,8,2,256]{3,2,1,0:T(2,128)S(1)} %get-tuple-element.146), channel_id=1, source_target_pairs={{0,1},{2,3},{4,5},{6,7},{8,9},{10,11},{12,13},{14,15},{16,17},{18,... | collective-permute-start | bytes 196616 | tf_op jit(solution)/shard_map/ppermute | solution.py:24
  12.4 6.2 %collective-permute-start.3 = (f32[4,8,2,256]{3,2,1,0:T(2,128)S(1)}, f32[4,8,2,256]{3,2,1,0:T(2,128)S(1)}, u32[]{:S(2)}, u32[]{:S(2)}) collective-permute-start(f32[4,8,2,256]{3,2,1,0:T(2,128)S(1)} %get-tuple-element.145), channel_id=1, source_target_pairs={{1,0},{3,2},{5,4},{7,6},{9,8},{11,10},{13,12},{15,14},{17,16},{19,... | collective-permute-start | bytes 196616 | tf_op jit(solution)/shard_map/ppermute | solution.py:27
  42.9 3.5 %collective-permute-start.4 = (f32[4,8,2,256]{3,2,1,0:T(2,128)S(1)}, f32[4,8,2,256]{3,2,1,0:T(2,128)S(1)}, u32[]{:S(2)}, u32[]{:S(2)}) collective-permute-start(f32[4,8,2,256]{3,2,1,0:T(2,128)S(1)} %get-tuple-element.143), channel_id=1, source_target_pairs={{0,1},{2,3},{4,5},{6,7},{8,9},{10,11},{12,13},{14,15},{16,17},{18,... | collective-permute-start | bytes 196616 | tf_op jit(solution)/shard_map/ppermute | solution.py:24
  44.5 6.2 %collective-permute-start.5 = (f32[4,8,2,256]{3,2,1,0:T(2,128)S(1)}, f32[4,8,2,256]{3,2,1,0:T(2,128)S(1)}, u32[]{:S(2)}, u32[]{:S(2)}) collective-permute-start(f32[4,8,2,256]{3,2,1,0:T(2,128)S(1)} %get-tuple-element.144), channel_id=1, source_target_pairs={{1,0},{3,2},{5,4},{7,6},{9,8},{11,10},{13,12},{15,14},{17,16},{19,... | collective-permute-start | bytes 196616 | tf_op jit(solution)/shard_map/ppermute | solution.py:27
  75.4 3.5 %collective-permute-start.6 = (f32[4,8,2,256]{3,2,1,0:T(2,128)S(1)}, f32[4,8,2,256]{3,2,1,0:T(2,128)S(1)}, u32[]{:S(2)}, u32[]{:S(2)}) collective-permute-start(f32[4,8,2,256]{3,2,1,0:T(2,128)S(1)} %get-tuple-element.141), channel_id=1, source_target_pairs={{0,1},{2,3},{4,5},{6,7},{8,9},{10,11},{12,13},{14,15},{16,17},{18,... | collective-permute-start | bytes 196616 | tf_op jit(solution)/shard_map/ppermute | solution.py:24
  77.0 6.2 %collective-permute-start.7 = (f32[4,8,2,256]{3,2,1,0:T(2,128)S(1)}, f32[4,8,2,256]{3,2,1,0:T(2,128)S(1)}, u32[]{:S(2)}, u32[]{:S(2)}) collective-permute-start(f32[4,8,2,256]{3,2,1,0:T(2,128)S(1)} %get-tuple-element.142), channel_id=1, source_target_pairs={{1,0},{3,2},{5,4},{7,6},{9,8},{11,10},{13,12},{15,14},{17,16},{19,... | collective-permute-start | bytes 196616 | tf_op jit(solution)/shard_map/ppermute | solution.py:27
  108.1 3.5 %collective-permute-start.8 = (f32[4,8,2,256]{3,2,1,0:T(2,128)S(1)}, f32[4,8,2,256]{3,2,1,0:T(2,128)S(1)}, u32[]{:S(2)}, u32[]{:S(2)}) collective-permute-start(f32[4,8,2,256]{3,2,1,0:T(2,128)S(1)} %get-tuple-element.139), channel_id=1, source_target_pairs={{0,1},{2,3},{4,5},{6,7},{8,9},{10,11},{12,13},{14,15},{16,17},{18,... | collective-permute-start | bytes 196616 | tf_op jit(solution)/shard_map/ppermute | solution.py:24
  109.6 6.2 %collective-permute-start.9 = (f32[4,8,2,256]{3,2,1,0:T(2,128)S(1)}, f32[4,8,2,256]{3,2,1,0:T(2,128)S(1)}, u32[]{:S(2)}, u32[]{:S(2)}) collective-permute-start(f32[4,8,2,256]{3,2,1,0:T(2,128)S(1)} %get-tuple-element.140), channel_id=1, source_target_pairs={{1,0},{3,2},{5,4},{7,6},{9,8},{11,10},{13,12},{15,14},{17,16},{19,... | collective-permute-start | bytes 196616 | tf_op jit(solution)/shard_map/ppermute | solution.py:27
  141.9 29.0 %copy-start.2 = (s32[1,4,1,128]{3,2,1,0:T(1,128)S(1)}, s32[1,4,1,128]{3,2,1,0:T(1,128)}, u32[]{:S(2)}) copy-start(s32[1,4,1,128]{3,2,1,0:T(1,128)} %param.11) | copy-start | bytes 6148
  141.9 29.0 %all-to-all-start = ((f32[64,8,2,256]{3,2,1,0:T(2,128)}), f32[64,8,2,256]{3,2,1,0:T(2,128)S(1)}, u32[]{:S(2)}, u32[]{:S(2)}) async-start(f32[64,8,2,256]{3,2,1,0:T(2,128)} %multiply_add_fusion), calls=%async_computation | async-start | bytes 2097152 | tf_op jit(solution)/shard_map/all_to_all | solution.py:92
  147.9 23.8 %copy-start.1 = (f32[1,4,1,128]{3,2,1,0:T(1,128)S(1)}, f32[1,4,1,128]{3,2,1,0:T(1,128)}, u32[]{:S(2)}) copy-start(f32[1,4,1,128]{3,2,1,0:T(1,128)} %param.13) | copy-start | bytes 6148
  171.7 0.7 copy-start.3
  172.4 13.1 %collective-permute-start.12 = (bf16[1,129,1,128]{3,1,0,2:T(8,128)(2,1)S(1)}, bf16[1,129,1,128]{3,1,0,2:T(8,128)(2,1)S(1)}, u32[]{:S(2)}, u32[]{:S(2)}) collective-permute-start(bf16[1,129,1,128]{3,1,0,2:T(8,128)(2,1)S(1)} %get-tuple-element.157), channel_id=1, source_target_pairs={{2,0},{4,2},{6,4},{8,6},{10,8},{12,10},{14,12},{16,14},{18,16},{20... | collective-permute-start | bytes 99080 | tf_op jit(solution)/shard_map/ppermute | solution.py:27
  177.8 6.1 %collective-permute-start.10 = (bf16[1,129,1,128]{3,1,0,2:T(8,128)(2,1)S(1)}, bf16[1,129,1,128]{3,1,0,2:T(8,128)(2,1)S(1)}, u32[]{:S(2)}, u32[]{:S(2)}) collective-permute-start(bf16[1,129,1,128]{3,1,0,2:T(8,128)(2,1)S(1)} %get-tuple-element.158), channel_id=1, source_target_pairs={{0,2},{2,4},{4,6},{6,8},{8,10},{10,12},{12,14},{14,16},{16,18},{18... | collective-permute-start | bytes 99080 | tf_op jit(solution)/shard_map/ppermute | solution.py:24
  183.9 3.2 %collective-permute-start.11 = (bf16[1,129,1,128]{3,1,0,2:T(8,128)(2,1)S(1)}, bf16[1,129,1,128]{3,1,0,2:T(8,128)(2,1)S(1)}, u32[]{:S(2)}, u32[]{:S(2)}) collective-permute-start(bf16[1,129,1,128]{3,1,0,2:T(8,128)(2,1)S(1)} %collective-permute-done.10), channel_id=1, source_target_pairs={{0,1},{2,3},{4,5},{6,7},{8,9},{10,11},{12,13},{14,15},{16,17},{18,... | collective-permute-start | bytes 99080 | tf_op jit(solution)/shard_map/ppermute | solution.py:24
  185.5 5.8 %collective-permute-start.13 = (bf16[1,129,1,128]{3,1,0,2:T(8,128)(2,1)S(1)}, bf16[1,129,1,128]{3,1,0,2:T(8,128)(2,1)S(1)}, u32[]{:S(2)}, u32[]{:S(2)}) collective-permute-start(bf16[1,129,1,128]{3,1,0,2:T(8,128)(2,1)S(1)} %collective-permute-done.12), channel_id=1, source_target_pairs={{1,0},{3,2},{5,4},{7,6},{9,8},{11,10},{13,12},{15,14},{17,16},{19,... | collective-permute-start | bytes 99080 | tf_op jit(solution)/shard_map/ppermute | solution.py:27
where the time goes:
time: 249 us; the launch traced here: 246 us
  other arithmetic  65.9 us (26%)
  waiting for transfers between devices  50.9 us (20%)
  local copies, waits for them, and re-layouts  40.8 us (16%)
  starting transfers between devices  34.9 us (14%)
  blocking collectives  27.4 us (11%)
  matrix products  23.8 us (10%)
    slice x32, local copies, waits for them, and re-layouts, tendency(): jnp.roll(center_rows, -1, axis=-1) - jnp.roll(center_rows, 1, axis=-1)  36 us
    all_to_all x1, blocking collectives, per_device(): lax.all_to_all(analysis, 'mem', split_axis=1, concat_axis=0, tiled=True)  27.4 us
    all_to_all x1, waiting for transfers between devices, per_device(): lax.all_to_all(current, 'mem', split_axis=0, concat_axis=1, tiled=True)  22.8 us
    ppermute x7, waiting for transfers between devices, padded_2(): lax.ppermute(lax.slice_in_dim(block, 0, width, axis=dim), axis, backward)  20.3 us
    add x4, other arithmetic, per_device(): extended[4:-4]  17.7 us
    add x4, other arithmetic, per_device(): extended[1:-1] + 0.5 * slope_one  15.7 us
    ppermute x7, starting transfers between devices, padded_2(): lax.ppermute(lax.slice_in_dim(block, block.shape[dim] - width, None, axis...  15.7 us
    add x4, other arithmetic, per_device(): extended[3:-3] + slope_three  14.3 us
  transfers between devices with their start and end apart: 15, of which 11 were waited for; matrix products, arithmetic and copies ran while one was open for 1% of the time, Pallas kernels for 0%

commit v1 on v0

--- a/solution.py
+++ b/solution.py
@@ -1,17 +1,24 @@
+import functools
 import math
 
 import jax
 import jax.numpy as jnp
 from jax import lax
+from jax.experimental import pallas as pl
+from jax.experimental.pallas import tpu as pltpu
 from jax.sharding import PartitionSpec as P
 
 PW = 256
 NOBS = 128
 STEPS = 4
 ITERS = 12
-
+LANES = 128
+HALO = 4 * STEPS + 1
+CHUNK = 8
 
 HIGHEST = lax.Precision.HIGHEST
+F32 = jnp.float32
+BF16 = jnp.bfloat16
 
 
 def padded_2(block, sides, width, periodic):
@@ -66,7 +73,7 @@
     return (upper_adjacent, bottom_adjacent)
 
 
-def per_device(background, wind_east, wind_north, obs_index, obs_value, obs_scale):
+def per_device_any(background, wind_east, wind_north, obs_index, obs_value, obs_scale):
     current = background
     stacked_winds = jnp.stack([wind_east, wind_north])
     wide_winds = padded_2(stacked_winds, (("lat", 1),), 3, False).astype(jnp.float32)
@@ -144,6 +151,650 @@
     return lax.all_to_all(analysis, "mem", split_axis=1, concat_axis=0, tiled=True)
 
 
+PAD = 8
+INNER_BLOCK = 32
+OUTER_BLOCK = 25
+LEVELS = 32766.0
+LOG_STEP = math.log(2.0) / 512.0
+
+
+def take_lanes(values, lanes):
+    return jnp.take_along_axis(values, lanes, axis=1, mode="promise_in_bounds")
+
+
+def parity_matrix():
+    source = lax.broadcasted_iota(jnp.int32, (2 * LANES, 2 * LANES), 0)
+    target = lax.broadcasted_iota(jnp.int32, (2 * LANES, 2 * LANES), 1)
+    wanted = jnp.where(target < LANES, 2 * target, 2 * (target - LANES) + 1)
+    return jnp.where(source == wanted, F32(1.0), F32(0.0)).astype(BF16)
+
+
+def stage_states(source_ref, rows_of, count, members, matrix, store):
+    for field in range(2):
+        low = [source_ref[rows_of(k), pl.ds(field, members, stride=4), :] for k in range(count)]
+        high = [
+            source_ref[rows_of(k), pl.ds(2 + field, members, stride=4), :] for k in range(count)
+        ]
+        left = jnp.concatenate(
+            [jnp.concatenate(low, axis=0), jnp.concatenate(high, axis=0)], axis=1
+        )
+        first = left.astype(BF16)
+        left = left - first.astype(F32)
+        second = left.astype(BF16)
+        third = (left - second.astype(F32)).astype(BF16)
+        split = jnp.dot(first, matrix, preferred_element_type=F32) + (
+            jnp.dot(second, matrix, preferred_element_type=F32)
+            + jnp.dot(third, matrix, preferred_element_type=F32)
+        )
+        store(field, split[:, :LANES].reshape(count, members, LANES))
+        store(2 + field, split[:, LANES:].reshape(count, members, LANES))
+
+
+def stage_winds(east, north, north_sign, matrix, w_ref, start):
+    count = east.shape[0]
+    for side, (wind, sign) in enumerate(((east, F32(-0.25)), (north, north_sign))):
+        split = jnp.dot(wind, matrix, preferred_element_type=F32) * sign
+        for parity in range(2):
+            lanes = split[:, parity * LANES : (parity + 1) * LANES]
+            wide = jnp.broadcast_to(lanes[:, None, :], (count, w_ref.shape[2], LANES))
+            w_ref[2 * side + parity, pl.ds(start, count)] = wide
+
+
+def rk_passes(q_ref, stage_refs, offset, w_ref, wind_row, first, count, block):
+    a_ref, b_ref, c_ref = stage_refs
+
+    def finish_one(part, at, half):
+        a_ref[part, at] = q_ref[part, at] + half
+
+    def finish_two(part, at, half):
+        b_ref[part, at] = q_ref[part, at] + half
+
+    def finish_three(part, at, half):
+        c_ref[part, at] = q_ref[part, at] + (half + half)
+
+    def finish_four(part, at, half):
+        doubled = b_ref[part, at]
+        gathered = (a_ref[part, at] + c_ref[part, at] - q_ref[part, at]) + (doubled + doubled)
+        q_ref[part, at] = (gathered + half) * F32(1.0 / 3.0)
+
+    for stage, finish in (
+        (q_ref, finish_one),
+        (a_ref, finish_two),
+        (b_ref, finish_three),
+        (c_ref, finish_four),
+    ):
+
+        def turn(index, _):
+            base = first + index * block + offset
+            states = [[stage[part, base + k - 1] for k in range(block + 2)] for part in range(4)]
+            for k in range(1, block + 1):
+                place = wind_row(base - offset + k - 1)
+                winds = [w_ref[part, place] for part in range(4)]
+                for field in range(2):
+                    even, odd = states[field], states[2 + field]
+                    along_even = odd[k] - pltpu.roll(odd[k], 1, 1)
+                    along_odd = pltpu.roll(even[k], LANES - 1, 1) - even[k]
+                    finish(
+                        field,
+                        base + k - 1,
+                        winds[0] * along_even + winds[2] * (even[k + 1] - even[k - 1]),
+                    )
+                    finish(
+                        2 + field,
+                        base + k - 1,
+                        winds[1] * along_odd + winds[3] * (odd[k + 1] - odd[k - 1]),
+                    )
+            return 0
+
+        turns = -(-count // block)
+        if turns == 1:
+            turn(0, 0)
+        else:
+            lax.fori_loop(0, turns, turn, 0)
+
+
+def encode_rows(states, row_count, members, store):
+    lane = lax.broadcasted_iota(jnp.int32, (members, LANES), 1)
+    scales = jnp.zeros((members, LANES), jnp.int32)
+    coded = []
+    for j in range(row_count):
+        top = jnp.abs(states[j][0])
+        for part in range(1, 4):
+            top = jnp.maximum(top, jnp.abs(states[j][part]))
+        top = jnp.maximum(jnp.max(top, axis=1, keepdims=True), F32(1e-9))
+        level = jnp.floor(jnp.log(top) * F32(1.0 / LOG_STEP)) + 2.0
+        factor = F32(LEVELS) / jnp.exp(level * F32(LOG_STEP))
+        scales = jnp.where(lane == j, level.astype(jnp.int32), scales)
+        coded.append([jnp.round(states[j][part] * factor).astype(jnp.int32) for part in range(4)])
+    for part in range(4):
+        for j in range(0, row_count, 2):
+            store(
+                (part * row_count + j) * members,
+                jnp.concatenate([coded[j][part], coded[j + 1][part]], axis=0).astype(jnp.int16),
+            )
+    store(
+        4 * row_count * members,
+        jnp.concatenate([scales, jnp.zeros_like(scales)], axis=0).astype(jnp.int16),
+    )
+
+
+def inner_kernel(sizes, flags_ref, own_ref, east_ref, north_ref, q_ref, out_ref, w_ref, *stage_refs):
+    rows, members, devices = sizes
+    own_rows = rows // devices
+    band = flags_ref[0]
+    matrix = parity_matrix()
+    north_sign = jnp.where(band == 0, F32(-0.25), F32(0.25))
+    for ref in (q_ref, *stage_refs):
+        ref[:, :PAD] = jnp.zeros((4, PAD, members, LANES), F32)
+        ref[:, PAD + rows :] = jnp.zeros((4, PAD, members, LANES), F32)
+    w_ref[...] = jnp.zeros(w_ref.shape, F32)
+    stage_winds(east_ref[...], north_ref[...], north_sign, matrix, w_ref, PAD)
+
+    def stage(index, _):
+        base = index * CHUNK
+
+        def store(part, values):
+            q_ref[part, pl.ds(PAD + base, CHUNK)] = values
+
+        def row_of(k):
+            return jnp.where(band == 0, base + k, rows - 1 - base - k)
+
+        stage_states(own_ref, row_of, CHUNK, members, matrix, store)
+        return 0
+
+    lax.fori_loop(0, rows // CHUNK, stage, 0)
+
+    def wind_row(row):
+        return PAD + jnp.where(band == 0, row, rows - 1 - row)
+
+    def step(_, carry):
+        rk_passes(q_ref, stage_refs, PAD, w_ref, wind_row, 0, rows, INNER_BLOCK)
+        return carry
+
+    lax.fori_loop(0, STEPS, step, 0)
+
+    def emit(device, _):
+        def store(place, values):
+            out_ref[device, pl.ds(place, values.shape[0]), :] = values
+
+        base = PAD + device * own_rows
+        states = [[q_ref[part, base + j] for part in range(4)] for j in range(own_rows)]
+        encode_rows(states, own_rows, members, store)
+        return 0
+
+    lax.fori_loop(0, (rows - 4 * STEPS) // own_rows, emit, 0)
+
+
+def outer_kernel(
+    sizes,
+    flags_ref,
+    own_ref,
+    halo_ref,
+    halo_winds_ref,
+    east_ref,
+    north_ref,
+    inner_ref,
+    table_ref,
+    coded_ref,
+    out_ref,
+    observed_ref,
+    q_ref,
+    w_ref,
+    *stage_refs,
+):
+    rows, members, devices = sizes
+    own_rows = rows // devices
+    band = flags_ref[0]
+    matrix = parity_matrix()
+    north_sign = jnp.where(band == 0, F32(-0.25), F32(0.25))
+    wind_halo = halo_winds_ref.shape[0] // 4
+    inner_rows = rows - 4 * STEPS
+    first = inner_rows - 4 * STEPS
+    count = rows + HALO - first
+    shift = 4 - first
+
+    w_ref[...] = jnp.zeros(w_ref.shape, F32)
+    stage_winds(
+        east_ref[...],
+        north_ref[...],
+        north_sign,
+        matrix,
+        w_ref,
+        PAD + jnp.where(band == 0, 0, wind_halo),
+    )
+    halo_winds = [
+        halo_winds_ref[part * wind_halo : (part + 1) * wind_halo].astype(BF16) for part in range(4)
+    ]
+    stage_winds(
+        jnp.concatenate(halo_winds[:2], axis=1),
+        jnp.concatenate(halo_winds[2:], axis=1),
+        north_sign,
+        matrix,
+        w_ref,
+        PAD + jnp.where(band == 0, rows, 0),
+    )
+
+    def stage_own(index, _):
+        base = first + index * CHUNK
+
+        def store(part, values):
+            q_ref[part, pl.ds(shift + base, CHUNK)] = values
+
+        def row_of(k):
+            return jnp.where(band == 0, base + k, rows - 1 - base - k)
+
+        stage_states(own_ref, row_of, CHUNK, members, matrix, store)
+        return 0
+
+    lax.fori_loop(0, (rows - first) // CHUNK, stage_own, 0)
+
+    def stage_halo(index, _):
+        base = index * CHUNK
+
+        def store(part, values):
+            q_ref[part, pl.ds(shift + rows + base, CHUNK)] = values
+
+        def row_of(k):
+            row = jnp.minimum(base + k, HALO - 1)
+            return jnp.where(band == 0, row, HALO - 1 - row)
+
+        stage_states(halo_ref, row_of, CHUNK, members, matrix, store)
+        return 0
+
+    lax.fori_loop(0, -(-HALO // CHUNK), stage_halo, 0)
+
+    def wind_row(row):
+        return PAD + jnp.where(band == 0, row, rows + wind_halo - 1 - row)
+
+    def step(_, carry):
+        rk_passes(q_ref, stage_refs, shift, w_ref, wind_row, first, count, OUTER_BLOCK)
+        return carry
+
+    lax.fori_loop(0, STEPS, step, 0)
+
+    def observed(states, table_row):
+        index = jnp.broadcast_to(table_ref[pl.ds(table_row * 3, 1), :], (members, LANES))
+        index = index.astype(jnp.int32)
+        lanes = jnp.bitwise_and(jnp.right_shift(index, 1), LANES - 1)
+        is_odd = jnp.bitwise_and(index, 1) == 1
+        second = index >= 2 * LANES
+        picks = [take_lanes(state, lanes) for state in states]
+        return jnp.where(
+            second,
+            jnp.where(is_odd, picks[3], picks[1]),
+            jnp.where(is_odd, picks[2], picks[0]),
+        )
+
+    def table_row_of(row):
+        return band * rows + jnp.where(band == 0, row, rows - 1 - row)
+
+    def place(device, slot, values):
+        observed_ref[device, pl.ds(slot * members, members), :] = values
+
+    def emit(device, state_of):
+        values = []
+        for j in range(own_rows):
+            row = device * own_rows + j
+            values.append(observed(state_of(row), table_row_of(row)))
+            place(device, j + 1, values[j])
+
+        @pl.when(device + 1 < devices)
+        def _():
+            place(device + 1, 0, values[own_rows - 1])
+
+        @pl.when(device > 0)
+        def _():
+            place(device - 1, own_rows + 1, values[0])
+
+    def emit_inner(device, _):
+        emit(device, lambda row: [inner_ref[part, PAD + row] for part in range(4)])
+        return 0
+
+    def outer_state(row):
+        return [q_ref[part, shift + row] for part in range(4)]
+
+    def emit_outer(device, _):
+        emit(device, outer_state)
+
+        def store(place_at, values):
+            out_ref[device, pl.ds(place_at, values.shape[0]), :] = values
+
+        states = [outer_state(device * own_rows + j) for j in range(own_rows)]
+        encode_rows(states, own_rows, members, store)
+        return 0
+
+    lax.fori_loop(0, inner_rows // own_rows, emit_inner, 0)
+    out_ref[...] = coded_ref[...]
+    lax.fori_loop(inner_rows // own_rows, devices, emit_outer, 0)
+    place(0, 0, jnp.zeros((members, LANES), F32))
+    edge = (1 - band) * rows + jnp.where(band == 0, 0, rows - 1)
+    place(devices - 1, own_rows + 1, observed(outer_state(rows), edge))
+
+
+def split_value(value):
+    high = value.astype(BF16)
+    return high, (value - high.astype(F32)).astype(BF16)
+
+
+def product(left, right):
+    (left_high, left_low), (right_high, right_low) = left, right
+    size = right_high.shape[1]
+    both = jnp.dot(
+        jnp.concatenate([left_high, left_low], axis=1),
+        jnp.concatenate(
+            [
+                jnp.concatenate([right_high, right_low], axis=1),
+                jnp.concatenate([right_high, jnp.zeros_like(right_low)], axis=1),
+            ],
+            axis=0,
+        ),
+        preferred_element_type=F32,
+    )
+    return both[:, :size] + both[:, size:]
+
+
+def weights_kernel(
+    sizes, flags_ref, got_ref, table_ref, out_ref, upper_ref, upper_low_ref, lower_ref, lower_low_ref
+):
+    rows, members, devices = sizes
+    own_rows = rows // devices
+    total = members * devices
+    band = flags_ref[0]
+    first = flags_ref[1] * own_rows
+    nobs = LANES
+
+    def info(row):
+        inside = jnp.logical_and(row >= 0, row < rows)
+        here = band * rows + jnp.where(band == 0, row, rows - 1 - row)
+        edge = (1 - band) * rows + jnp.where(band == 0, 0, rows - 1)
+        at = 3 * jnp.where(inside, here, edge)
+        keep = jnp.where(row >= 0, F32(1.0), F32(0.0))
+        return table_ref[pl.ds(at + 1, 1), :], table_ref[pl.ds(at + 2, 1), :] * keep
+
+    grams = []
+    couplings = []
+    for j in range(-1, own_rows + 1):
+        value, scale = info(first + j)
+        picked = got_ref[:, (j + 1) * members : (j + 2) * members, :].reshape(total, nobs)
+        average = jnp.mean(picked, axis=0, keepdims=True)
+        spread = ((picked - average) * scale / math.sqrt(total - 1)).astype(BF16)
+        innovation = jnp.broadcast_to((value - average) * scale, (16, nobs)).astype(BF16)
+        contract = (((1,), (1,)), ((), ()))
+        grams.append(lax.dot_general(spread, spread, contract, preferred_element_type=F32))
+        couplings.append(
+            lax.dot_general(innovation, spread, contract, preferred_element_type=F32)
+        )
+
+    row_ids = lax.broadcasted_iota(jnp.int32, (total, total), 0)
+    column_ids = lax.broadcasted_iota(jnp.int32, (total, total), 1)
+    diagonal = row_ids == column_ids
+    identity = jnp.where(diagonal, F32(1.0), F32(0.0))
+
+    def put(high_ref, low_ref, j, value):
+        high_ref[j], low_ref[j] = split_value(value)
+
+    traces = []
+    for j in range(own_rows):
+        system = identity + 3.0 * grams[j + 1] + grams[j] + grams[j + 2]
+        trace = jnp.sum(
+            jnp.sum(jnp.where(diagonal, system, 0.0), axis=0, keepdims=True),
+            axis=1,
+            keepdims=True,
+        )
+        traces.append(trace)
+        scaled = system / trace
+        factor = split_value(1.5 * identity - 0.5 * scaled)
+        put(upper_ref, upper_low_ref, j, product(split_value(scaled), factor))
+        lower_ref[j], lower_low_ref[j] = factor
+
+    def factor_of(j):
+        lower = lower_ref[j], lower_low_ref[j]
+        upper = upper_ref[j], upper_low_ref[j]
+        return lower, upper, split_value(1.5 * identity - 0.5 * product(lower, upper))
+
+    def newton(turn, _):
+        parts = [factor_of(j) for j in range(own_rows)]
+        for j in range(own_rows):
+            lower, upper, factor = parts[j]
+            put(upper_ref, upper_low_ref, j, product(upper, factor))
+            put(lower_ref, lower_low_ref, j, product(factor, lower))
+        return 0
+
+    lax.fori_loop(0, ITERS - 2, newton, 0)
+
+    parts = [factor_of(j) for j in range(own_rows)]
+    for j in range(own_rows):
+        lower, upper, factor = parts[j]
+        inv_root = product(factor, lower) / jnp.sqrt(traces[j])
+        coupling = 3.0 * couplings[j + 1] + couplings[j] + couplings[j + 2]
+        root_parts = split_value(inv_root)
+        half_step = product(split_value(coupling), root_parts)
+        mean_weight = product(split_value(half_step), root_parts)[:1] / math.sqrt(total - 1)
+        out_ref[j] = inv_root + mean_weight
+
+
+def apply_kernel(sizes, got_ref, weights_ref, out_ref):
+    rows, members, devices = sizes
+    own_rows = rows // devices
+    total = members * devices
+    pair = 2 * members
+    levels = got_ref[:, pl.ds(4 * own_rows * members, pair), :].astype(jnp.int32).astype(F32)
+    levels = levels[:, :members].reshape(total, LANES)
+    scales = jnp.exp(levels * F32(LOG_STEP)) * F32(1.0 / LEVELS)
+    weights = [split_value(weights_ref[j]) for j in range(own_rows)]
+    for j in range(0, own_rows, 2):
+        for part in range(4):
+            place = (part * own_rows + j) * members
+            both = got_ref[:, pl.ds(place, pair), :].astype(jnp.int32).astype(F32)
+            both = both.reshape(devices, 2, members, LANES)
+            moved = []
+            for k in range(2):
+                state = both[:, k].reshape(total, LANES) * scales[:, j + k : j + k + 1]
+                center = jnp.mean(state, axis=0, keepdims=True)
+                high, low = split_value(state - center)
+                weights_high, weights_low = weights[j + k]
+                result = center + (
+                    jnp.dot(weights_high, high, preferred_element_type=F32)
+                    + jnp.dot(weights_high, low, preferred_element_type=F32)
+                    + jnp.dot(weights_low, high, preferred_element_type=F32)
+                )
+                moved.append(result.reshape(devices, members, LANES))
+            out_ref[:, pl.ds(place, pair), :] = jnp.concatenate(moved, axis=1).astype(BF16)
+
+
+def unpack_kernel(sizes, flags_ref, got_ref, out_ref):
+    rows, members, devices = sizes
+    own_rows = rows // devices
+    band = flags_ref[0]
+    pair = 2 * members
+    source = lax.broadcasted_iota(jnp.int32, (2 * LANES, 2 * LANES), 0)
+    target = lax.broadcasted_iota(jnp.int32, (2 * LANES, 2 * LANES), 1)
+    wanted = jnp.where(source < LANES, 2 * source, 2 * (source - LANES) + 1)
+    matrix = jnp.where(target == wanted, F32(1.0), F32(0.0)).astype(BF16)
+
+    def place(index, _):
+        device = index * 2
+        for field in range(2):
+            even, odd = [
+                jnp.concatenate(
+                    [
+                        got_ref[
+                            device + d, pl.ds((part * own_rows) * members, own_rows * members), :
+                        ]
+                        for d in range(2)
+                    ],
+                    axis=0,
+                )
+                for part in (field, 2 + field)
+            ]
+            joined = jnp.dot(
+                jnp.concatenate([even, odd], axis=1), matrix, preferred_element_type=F32
+            )
+            for k in range(2 * own_rows):
+                row = device * own_rows + k
+                row = jnp.where(band == 0, row, rows - 1 - row)
+                values = joined[k * members : (k + 1) * members]
+                for half in range(2):
+                    out_ref[row, pl.ds(2 * half + field, members, stride=4), :] = values[
+                        :, half * LANES : (half + 1) * LANES
+                    ]
+        return 0
+
+    lax.fori_loop(0, devices // 2, place, 0)
+
+
+def per_device_pair(background, wind_east, wind_north, obs_index, obs_value, obs_scale):
+    rows, members, fields, width = background.shape
+    devices = lax.axis_size("mem")
+    bands = lax.axis_size("lat")
+    own_rows = rows // devices
+    total = members * devices
+    sizes = (rows, members, devices)
+    band = lax.axis_index("lat")
+    flags = jnp.stack([band, lax.axis_index("mem")]).astype(jnp.int32)
+    smem = pl.BlockSpec(memory_space=pltpu.SMEM)
+    vmem = pl.BlockSpec(memory_space=pltpu.VMEM)
+    params = pltpu.CompilerParams(vmem_limit_bytes=40 * 1024 * 1024)
+
+    def cost(microseconds):
+        return pl.CostEstimate(
+            flops=0, bytes_accessed=int(microseconds * 3_000_000), transcendentals=0
+        )
+
+    grouped = members * fields * 2
+    own = background.reshape(rows, members, fields, 2, LANES)
+    own = own.transpose(0, 1, 3, 2, 4).reshape(rows, grouped, LANES)
+
+    wind_halo = -(-HALO // CHUNK) * CHUNK
+
+    def edge_rows(array, count):
+        return lax.dynamic_slice_in_dim(
+            array, jnp.where(band == 0, rows - count, 0), count, 0
+        )
+
+    edge_winds = [edge_rows(wind, wind_halo).astype(F32) for wind in (wind_east, wind_north)]
+    sent = jnp.concatenate(
+        [edge_rows(own, HALO).reshape(HALO * grouped, LANES)]
+        + [wind[:, half * LANES : (half + 1) * LANES] for wind in edge_winds for half in range(2)],
+        axis=0,
+    )
+    halo = lax.ppermute(sent, "lat", [(0, 1), (1, 0)])
+    info = jnp.stack(
+        [
+            obs_index.reshape(own_rows, NOBS).astype(F32),
+            obs_value.reshape(own_rows, NOBS),
+            obs_scale.reshape(own_rows, NOBS),
+        ],
+        axis=1,
+    ).reshape(1, own_rows * 3, NOBS)
+    table = lax.all_to_all(
+        jnp.broadcast_to(info, (bands * devices, own_rows * 3, NOBS)),
+        ("lat", "mem"),
+        split_axis=0,
+        concat_axis=0,
+        tiled=True,
+    ).reshape(bands * rows * 3, NOBS)
+
+    coded_shape = jax.ShapeDtypeStruct(
+        (devices, (4 * own_rows + 2) * members, LANES), jnp.int16
+    )
+    inner, coded = pl.pallas_call(
+        functools.partial(inner_kernel, sizes),
+        out_shape=(
+            jax.ShapeDtypeStruct((4, rows + 2 * PAD, members, LANES), F32),
+            coded_shape,
+        ),
+        in_specs=[smem, vmem, vmem, vmem],
+        out_specs=(vmem, vmem),
+        scratch_shapes=[pltpu.VMEM((4, rows + 2 * PAD, members, LANES), F32)] * 4,
+        compiler_params=params,
+        cost_estimate=cost(6),
+        name="forecast_inner",
+    )(flags, own, wind_east, wind_north)
+
+    outer_rows = 4 * STEPS * 2 + wind_halo + CHUNK
+    coded, observed = pl.pallas_call(
+        functools.partial(outer_kernel, sizes),
+        out_shape=(
+            coded_shape,
+            jax.ShapeDtypeStruct((devices, (own_rows + 2) * members, LANES), F32),
+        ),
+        in_specs=[smem] + [vmem] * 8,
+        out_specs=(vmem, vmem),
+        scratch_shapes=[
+            pltpu.VMEM((4, outer_rows, members, LANES), F32),
+            pltpu.VMEM((4, rows + wind_halo + 2 * PAD, members, LANES), F32),
+        ]
+        + [pltpu.VMEM((4, outer_rows, members, LANES), F32)] * 3,
+        compiler_params=params,
+        cost_estimate=cost(6),
+        name="forecast_outer",
+    )(
+        flags,
+        own,
+        halo[: HALO * grouped].reshape(HALO, grouped, LANES),
+        halo[HALO * grouped :],
+        wind_east,
+        wind_north,
+        inner,
+        table,
+        coded,
+    )
+    got_observed = lax.all_to_all(observed, "mem", split_axis=0, concat_axis=0, tiled=True)
+    got_states = lax.all_to_all(coded, "mem", split_axis=0, concat_axis=0, tiled=True)
+    half_matrix = pltpu.VMEM((own_rows, total, total), BF16)
+    weights = pl.pallas_call(
+        functools.partial(weights_kernel, sizes),
+        out_shape=jax.ShapeDtypeStruct((own_rows, total, total), F32),
+        in_specs=[smem, vmem, vmem],
+        out_specs=vmem,
+        scratch_shapes=[half_matrix] * 4,
+        compiler_params=params,
+        cost_estimate=cost(12),
+        name="weights",
+    )(flags, got_observed, table)
+    back = pl.pallas_call(
+        functools.partial(apply_kernel, sizes),
+        out_shape=jax.ShapeDtypeStruct((devices, 4 * own_rows * members, LANES), BF16),
+        in_specs=[vmem, vmem],
+        out_specs=vmem,
+        compiler_params=params,
+        cost_estimate=cost(2),
+        name="apply",
+    )(got_states, weights)
+    returned = lax.all_to_all(back, "mem", split_axis=0, concat_axis=0, tiled=True)
+    result = pl.pallas_call(
+        functools.partial(unpack_kernel, sizes),
+        out_shape=jax.ShapeDtypeStruct((rows, grouped, LANES), F32),
+        in_specs=[smem, vmem],
+        out_specs=vmem,
+        compiler_params=params,
+        cost_estimate=cost(2),
+        name="unpack",
+    )(flags, returned)
+    result = result.reshape(rows, members, 2, fields, LANES).transpose(0, 1, 3, 2, 4)
+    return result.reshape(rows, members, fields, width)
+
+
+def per_device(background, wind_east, wind_north, obs_index, obs_value, obs_scale):
+    rows, members, fields, width = background.shape
+    devices = lax.axis_size("mem")
+    fits = (
+        lax.axis_size("lat") == 2
+        and members == 8
+        and members * devices == LANES
+        and fields == 2
+        and width == 2 * LANES == PW
+        and obs_index.shape[2:] == (1, LANES)
+        and rows % (2 * CHUNK) == 0
+        and 4 * STEPS % (rows // devices) == 0
+        and (rows // devices) % 2 == 0
+        and rows >= 8 * STEPS
+    )
+    run = per_device_pair if fits else per_device_any
+    return run(background, wind_east, wind_north, obs_index, obs_value, obs_scale)
+
+
 def solution(mesh):
     in_specs = (
         P("lat", "mem", None, None),

time: 249 us -> 103 us (0.41); the launches traced: 246 us -> 102 us
  other arithmetic: 65.9 us -> 1.55 us
  waiting for transfers between devices: 50.9 us -> 8.25 us
  Pallas kernels: 0 us -> 35.6 us
  local copies, waits for them, and re-layouts: 40.8 us -> 7.62 us
  matrix products: 23.8 us -> 0 us
  starting transfers between devices: 34.9 us -> 12.7 us
  blocking collectives: 27.4 us -> 36.3 us
    add x16 -> x0, other arithmetic: 61.8 us -> none  [the longest x4 17.7 us: per_device(): extended[4:-4]]
    pallas_call x0 -> x5, Pallas kernels: none -> 35.6 us  [the longest x1 12.5 us: per_device_pair(): pl.pallas_call(functools.partial(outer_kernel, sizes), out_shape=(coded_s...]
    slice x36 -> x2, local copies, waits for them, and re-layouts: 36.9 us -> 1.78 us  [the longest x1 0.97 us: per_device_pair(): halo[:HALO * grouped].reshape(HALO, grouped, LANES)]
    ppermute x14 -> x1, waiting for transfers between devices: 28.1 us -> 0.01 us  [per_device_pair(): halo = lax.ppermute(sent, 'lat', [(0, 1), (1, 0)])]
    ppermute x14 -> x1, starting transfers between devices: 28.9 us -> 1.69 us  [per_device_pair(): halo = lax.ppermute(sent, 'lat', [(0, 1), (1, 0)])]
    dot_general x43 -> x0, matrix products: 23.8 us -> none  [the longest x12 7.98 us: newton(): jnp.einsum('apij,apjk->apik', lower_iter, upper_iter, precision=HIGHEST)]
    all_to_all x1 -> x2, waiting for transfers between devices: 22.8 us -> 8.25 us  [the longest x1 8.24 us: per_device_pair(): lax.all_to_all(coded, 'mem', split_axis=0, concat_axis=0, tiled=True)]
    all_to_all x1 -> x2, blocking collectives: 27.4 us -> 36.3 us  [the longest x1 18.7 us: per_device_pair(): lax.all_to_all(back, 'mem', split_axis=0, concat_axis=0, tiled=True)]
  transfers between devices with their start and end apart: 15 -> 3, of which waited for: 11 -> 1; matrix products, arithmetic and copies ran while one was open for 1% -> 6% of each run, Pallas kernels for 0% -> 19%
where the time goes in v1:
time: 103 us; the launch traced here: 102 us
  blocking collectives  36.3 us (35%)
  Pallas kernels  35.6 us (35%)
  starting transfers between devices  12.7 us (12%)
  waiting for transfers between devices  8.25 us (8%)
  local copies, waits for them, and re-layouts  7.62 us (7%)
  other arithmetic  1.55 us (2%)
    all_to_all x1, blocking collectives, per_device_pair(): lax.all_to_all(back, 'mem', split_axis=0, concat_axis=0, tiled=True)  18.7 us
    all_to_all x1, blocking collectives, per_device_pair(): lax.all_to_all(observed, 'mem', split_axis=0, concat_axis=0, tiled=True)  17.6 us
    pallas_call x1, Pallas kernels, per_device_pair(): pl.pallas_call(functools.partial(outer_kernel, sizes), out_shape=(coded_s...  12.5 us
    pallas_call x1, Pallas kernels, per_device_pair(): pl.pallas_call(functools.partial(inner_kernel, sizes), out_shape=(jax.Sha...  12.3 us
    all_to_all x1, waiting for transfers between devices, per_device_pair(): lax.all_to_all(coded, 'mem', split_axis=0, concat_axis=0, tiled=True)  8.24 us
    all_to_all x1, starting transfers between devices, per_device_pair(): lax.all_to_all(jnp.broadcast_to(info, (bands * devices, own_rows * 3, NOB...  7.43 us
    pallas_call x1, Pallas kernels, per_device_pair(): pl.pallas_call(functools.partial(weights_kernel, sizes), out_shape=jax.Sh...  7.25 us
    all_to_all x1, starting transfers between devices, per_device_pair(): lax.all_to_all(coded, 'mem', split_axis=0, concat_axis=0, tiled=True)  3.58 us
  transfers between devices with their start and end apart: 3, of which 1 were waited for; matrix products, arithmetic and copies ran while one was open for 6% of the time, Pallas kernels for 19%

profile of v1, /device:TPU:0, one launch (start us, length us, event | category | flops | bytes accessed | tf_op | source)
XLA Modules:
  0.0 102.2 jit_solution(5916977567504205840)
XLA Ops:
  0.0 0.0 copy-start
  0.0 0.0 copy-start.1
  0.0 0.0 copy-start.2
  0.0 0.8 convert_bitcast_fusion
  0.8 0.7 pad_maximum_fusion
  1.5 0.7 broadcast_in_dim.8
  2.2 7.4 %all-to-all-start = ((f32[32,12,128]{2,1,0:T(8,128)}), f32[32,12,128]{2,1,0:T(8,128)}, u32[]{:S(2)}, u32[]{:S(2)}) async-start(f32[32,12,128]{2,1,0:T(8,128)} %broadcast_in_dim.8), calls=%async_computation | async-start | bytes 524288 | tf_op jit(solution)/shard_map/all_to_all | solution.py:690
  9.7 1.0 constant_dynamic-slice_fusion
  10.7 0.7 constant_dynamic-update-slice_fusion
  11.4 0.0 copy-done.1
  11.4 0.0 copy-done.2
  11.4 0.6 slice_dynamic-update-slice_fusion.3
  12.0 0.6 slice_dynamic-update-slice_fusion.2
  12.6 0.6 slice_dynamic-update-slice_fusion.1
  13.2 0.6 slice_dynamic-update-slice_fusion
  13.8 1.7 %collective-permute-start = (f32[640,128]{1,0:T(8,128)}, f32[640,128]{1,0:T(8,128)}, u32[]{:S(2)}, u32[]{:S(2)}) collective-permute-start(f32[640,128]{1,0:T(8,128)} %slice_dynamic-update-slice_fusion), channel_id=1, source_target_pairs={{0,1},{1,0},{2,3},{3,2},{4,5},{5,4},{6,7},{7,6},{8,9},{9,8},{10,11... | collective-permute-start | bytes 983048 | tf_op jit(solution)/shard_map/ppermute | solution.py:681
  15.5 0.1 pad_add_fusion.flags_ref
  15.6 0.0 copy-done
  15.6 12.3 %forecast_inner.1 = (f32[4,80,8,128]{3,2,1,0:T(8,128)S(1)}, s16[16,144,128]{2,1,0:T(8,128)(2,1)S(1)}) custom-call(s32[2]{0:T(128)S(1)} %pad_add_fusion.flags_ref, f32[64,32,128]{2,1,0:T(8,128)S(1)} %bitcast.20, bf16[64,256]{1,0:T(8,128)(2,1)S(1)} %copy-done.2, bf16[64,256]{1,0:T(8,128)(2,1)S(1)} %copy-done.1), custom_call_target="tpu_custom_call" | custom-call | bytes 18000000 | tf_op jit(solution)/shard_map/forecast_inner/pallas_call | solution.py:701
  27.9 0.0 collective-permute-done
  27.9 0.8 slice.29.halo_winds_ref
  28.7 1.0 slice.28
  29.7 0.0 all-to-all-done
  29.7 1.0 reshape.39.table_ref
  30.7 12.5 %forecast_outer.1 = (s16[16,144,128]{2,1,0:T(8,128)(2,1)}, f32[16,48,128]{2,1,0:T(8,128)S(1)}) custom-call(s32[2]{0:T(128)S(1)} %pad_add_fusion.flags_ref, f32[64,32,128]{2,1,0:T(8,128)S(1)} %bitcast.21, f32[17,32,128]{2,1,0:T(8,128)S(1)} %bitcast.22, f32[96,128]{1,0:T(8,128)S(1)} %slice.29.halo_winds_ref, bf16[64,256]{1,0:T(8,128)(2,1)S(1)} %copy-done.2, ...), custom_call_target="tpu_custom_call" | custom-call | bytes 18000000 | tf_op jit(solution)/shard_map/forecast_outer/pallas_call | solution.py:716
  43.2 17.6 %all_to_all.20.got_ref = f32[16,48,128]{2,1,0:T(8,128)S(1)} all-to-all(f32[16,48,128]{2,1,0:T(8,128)S(1)} %get-tuple-element.12), channel_id=1, replica_groups=mesh['mem'=16,'lat'=2] {'mem'}, dimensions={0} | all-to-all | bytes 786432 | tf_op jit(solution)/shard_map/all_to_all | solution.py:743
  60.8 3.6 %all-to-all-start.1 = ((s16[16,144,128]{2,1,0:T(8,128)(2,1)}), s16[16,144,128]{2,1,0:T(8,128)(2,1)S(1)}, u32[]{:S(2)}, u32[]{:S(2)}) async-start(s16[16,144,128]{2,1,0:T(8,128)(2,1)} %get-tuple-element.11), calls=%async_computation.1 | async-start | bytes 1179648 | tf_op jit(solution)/shard_map/all_to_all | solution.py:744
  64.4 7.2 %weights.1.weights_ref = f32[4,128,128]{2,1,0:T(8,128)S(1)} custom-call(s32[2]{0:T(128)S(1)} %pad_add_fusion.flags_ref, f32[16,48,128]{2,1,0:T(8,128)S(1)} %all_to_all.20.got_ref, f32[384,128]{1,0:T(8,128)S(1)} %reshape.39.table_ref), custom_call_target="tpu_custom_call" | custom-call | bytes 36000000 | tf_op jit(solution)/shard_map/weights/pallas_call | solution.py:746
  71.6 8.2 %all-to-all-done.1.got_ref = s16[16,144,128]{2,1,0:T(8,128)(2,1)S(1)} async-done(((s16[16,144,128]{2,1,0:T(8,128)(2,1)}), s16[16,144,128]{2,1,0:T(8,128)(2,1)S(1)}, u32[]{:S(2)}, u32[]{:S(2)}) %all-to-all-start.1) | async-done | bytes 589856 | tf_op jit(solution)/shard_map/all_to_all | solution.py:744
  79.9 0.7 apply.1
  80.6 18.7 %all_to_all.21.got_ref = bf16[16,128,128]{2,1,0:T(8,128)(2,1)S(1)} all-to-all(bf16[16,128,128]{2,1,0:T(8,128)(2,1)S(1)} %apply.1), channel_id=1, replica_groups=mesh['mem'=16,'lat'=2] {'mem'}, dimensions={0} | all-to-all | bytes 1048576 | tf_op jit(solution)/shard_map/all_to_all | solution.py:765
  99.3 2.9 %unpack.1 = f32[64,32,128]{2,1,0:T(8,128)} custom-call(s32[2]{0:T(128)S(1)} %pad_add_fusion.flags_ref, bf16[16,128,128]{2,1,0:T(8,128)(2,1)S(1)} %all_to_all.21.got_ref), custom_call_target="tpu_custom_call" | custom-call | bytes 6000000 | tf_op jit(solution)/shard_map/unpack/pallas_call | solution.py:766
  (3 shorter events, 0.0 us)
Async XLA Ops:
  0.0 15.6 %copy-start = (f32[64,8,2,256]{3,2,1,0:T(2,128)S(1)}, f32[64,8,2,256]{3,2,1,0:T(2,128)}, u32[]{:S(2)}) copy-start(f32[64,8,2,256]{3,2,1,0:T(2,128)} %param.6) | copy-start | bytes 3145732
  0.0 11.4 %copy-start.1 = (bf16[64,256]{1,0:T(8,128)(2,1)S(1)}, bf16[64,256]{1,0:T(8,128)(2,1)}, u32[]{:S(2)}) copy-start(bf16[64,256]{1,0:T(8,128)(2,1)} %north_ref.3) | copy-start | bytes 98308
  0.0 11.4 %copy-start.2 = (bf16[64,256]{1,0:T(8,128)(2,1)S(1)}, bf16[64,256]{1,0:T(8,128)(2,1)}, u32[]{:S(2)}) copy-start(bf16[64,256]{1,0:T(8,128)(2,1)} %east_ref.3) | copy-start | bytes 98308
  2.2 27.5 %all-to-all-start = ((f32[32,12,128]{2,1,0:T(8,128)}), f32[32,12,128]{2,1,0:T(8,128)}, u32[]{:S(2)}, u32[]{:S(2)}) async-start(f32[32,12,128]{2,1,0:T(8,128)} %broadcast_in_dim.8), calls=%async_computation | async-start | bytes 524288 | tf_op jit(solution)/shard_map/all_to_all | solution.py:690
  13.8 14.1 %collective-permute-start = (f32[640,128]{1,0:T(8,128)}, f32[640,128]{1,0:T(8,128)}, u32[]{:S(2)}, u32[]{:S(2)}) collective-permute-start(f32[640,128]{1,0:T(8,128)} %slice_dynamic-update-slice_fusion), channel_id=1, source_target_pairs={{0,1},{1,0},{2,3},{3,2},{4,5},{5,4},{6,7},{7,6},{8,9},{9,8},{10,11... | collective-permute-start | bytes 983048 | tf_op jit(solution)/shard_map/ppermute | solution.py:681
  60.8 19.1 %all-to-all-start.1 = ((s16[16,144,128]{2,1,0:T(8,128)(2,1)}), s16[16,144,128]{2,1,0:T(8,128)(2,1)S(1)}, u32[]{:S(2)}, u32[]{:S(2)}) async-start(s16[16,144,128]{2,1,0:T(8,128)(2,1)} %get-tuple-element.11), calls=%async_computation.1 | async-start | bytes 1179648 | tf_op jit(solution)/shard_map/all_to_all | solution.py:744

commit v2 on v0

--- a/solution.py
+++ b/solution.py
@@ -1,17 +1,24 @@
+import functools
 import math
 
 import jax
 import jax.numpy as jnp
 from jax import lax
+from jax.experimental import pallas as pl
+from jax.experimental.pallas import tpu as pltpu
 from jax.sharding import PartitionSpec as P
 
 PW = 256
 NOBS = 128
 STEPS = 4
 ITERS = 12
-
+LANES = 128
+HALO = 4 * STEPS + 1
+CHUNK = 8
 
 HIGHEST = lax.Precision.HIGHEST
+F32 = jnp.float32
+BF16 = jnp.bfloat16
 
 
 def padded_2(block, sides, width, periodic):
@@ -66,7 +73,7 @@
     return (upper_adjacent, bottom_adjacent)
 
 
-def per_device(background, wind_east, wind_north, obs_index, obs_value, obs_scale):
+def per_device_any(background, wind_east, wind_north, obs_index, obs_value, obs_scale):
     current = background
     stacked_winds = jnp.stack([wind_east, wind_north])
     wide_winds = padded_2(stacked_winds, (("lat", 1),), 3, False).astype(jnp.float32)
@@ -144,6 +151,652 @@
     return lax.all_to_all(analysis, "mem", split_axis=1, concat_axis=0, tiled=True)
 
 
+PAD = 8
+BLOCK = 20
+FINEST = 0.05
+LARGEST = 16.0 * sum(1.8**power / math.factorial(power) for power in range(5)) ** STEPS
+STEEPNESS = 32766.0 / math.log(1.0 + LARGEST / FINEST)
+
+
+def take_lanes(values, lanes):
+    return jnp.take_along_axis(values, lanes, axis=1, mode="promise_in_bounds")
+
+
+def pick_lanes(states, index):
+    field = jnp.right_shift(index, 8)
+    lanes = jnp.bitwise_and(jnp.right_shift(index, 1), LANES - 2) + field
+    is_odd = jnp.bitwise_and(index, 1) == 1
+    is_late = jnp.bitwise_and(index, 2) == 2
+    picks = [take_lanes(state, lanes) for state in states]
+    return jnp.where(
+        is_odd, jnp.where(is_late, picks[3], picks[1]), jnp.where(is_late, picks[2], picks[0])
+    )
+
+
+def group_place(sizes, band, group):
+    return jnp.where(band == 0, group, sizes[2] - 1 - group)
+
+
+def beside_info(table_ref, sizes, band, group, is_after, kind):
+    devices = sizes[2]
+    near = group + 1 if is_after else jnp.maximum(group - 1, 0)
+    over = near == devices
+    place = jnp.where(over, jnp.where(band == 0, 0, devices - 1), group_place(sizes, band, near))
+    near_band = jnp.where(over, 1 - band, band)
+    last = jnp.where(band == 0, 0, 1) if is_after else jnp.where(band == 0, 1, 0)
+    return table_ref[near_band * devices + place, pl.ds(2 * kind + last, 1), :]
+
+
+def parts_matrix(from_parts=False):
+    shape = (4 * LANES, 4 * LANES)
+    rows = lax.broadcasted_iota(jnp.int32, shape, 0)
+    columns = lax.broadcasted_iota(jnp.int32, shape, 1)
+    column, plain = (rows, columns) if from_parts else (columns, rows)
+    lane = jnp.bitwise_and(column, LANES - 1)
+    wanted = (
+        jnp.bitwise_and(lane, 1) * (2 * LANES)
+        + jnp.right_shift(lane, 1) * 4
+        + jnp.right_shift(column, 7)
+    )
+    return jnp.where(plain == wanted, F32(1.0), F32(0.0)).astype(BF16)
+
+
+def stage_states(load, row_of, count, members, matrix, q_ref, start):
+    left = jnp.concatenate(
+        [
+            jnp.concatenate([load(row_of(k), 2 * half + field) for k in range(count)], axis=0)
+            for field in range(2)
+            for half in range(2)
+        ],
+        axis=1,
+    )
+    first = left.astype(BF16)
+    left = left - first.astype(F32)
+    second = left.astype(BF16)
+    third = (left - second.astype(F32)).astype(BF16)
+    size = count * members
+    split = jnp.dot(
+        jnp.concatenate([first, second, third], axis=0), matrix, preferred_element_type=F32
+    )
+    split = split[:size] + (split[size : 2 * size] + split[2 * size :])
+    for part in range(4):
+        values = split[:, part * LANES : (part + 1) * LANES]
+        q_ref[part, pl.ds(start, count)] = values.reshape(count, members, LANES)
+
+
+def stage_winds(east, north, north_sign, matrix, w_ref, start):
+    count = east.shape[0]
+    for side, (wind, sign) in enumerate(((east, F32(-0.25)), (north, north_sign))):
+        both = jnp.concatenate([wind, wind], axis=1)
+        split = jnp.dot(both, matrix, preferred_element_type=F32) * sign
+        for part in range(4):
+            lanes = split[:, part * LANES : (part + 1) * LANES]
+            wide = jnp.broadcast_to(lanes[:, None, :], (count, w_ref.shape[2], LANES))
+            w_ref[4 * side + part, pl.ds(start, count)] = wide
+
+
+def rk_passes(q_ref, stage_refs, offset, w_ref, wind_row, first, count, block):
+    a_ref, b_ref, c_ref = stage_refs
+
+    def finish_one(part, at, half):
+        a_ref[part, at] = q_ref[part, at] + half
+
+    def finish_two(part, at, half):
+        b_ref[part, at] = q_ref[part, at] + half
+
+    def finish_three(part, at, half):
+        c_ref[part, at] = q_ref[part, at] + (half + half)
+
+    def finish_four(part, at, half):
+        doubled = b_ref[part, at]
+        gathered = (a_ref[part, at] + c_ref[part, at] - q_ref[part, at]) + (doubled + doubled)
+        q_ref[part, at] = (gathered + half) * F32(1.0 / 3.0)
+
+    for stage, finish in (
+        (q_ref, finish_one),
+        (a_ref, finish_two),
+        (b_ref, finish_three),
+        (c_ref, finish_four),
+    ):
+
+        def turn(index, _):
+            base = first + index * block + offset
+            states = [[stage[part, base + k - 1] for k in range(block + 2)] for part in range(4)]
+            for k in range(1, block + 1):
+                place = wind_row(base - offset + k - 1)
+                here = [states[part][k] for part in range(4)]
+                along = (
+                    here[1] - pltpu.roll(here[3], 2, 1),
+                    here[2] - here[0],
+                    here[3] - here[1],
+                    pltpu.roll(here[0], LANES - 2, 1) - here[2],
+                )
+                for part in range(4):
+                    across = states[part][k + 1] - states[part][k - 1]
+                    half = w_ref[part, place] * along[part] + w_ref[4 + part, place] * across
+                    finish(part, base + k - 1, half)
+            return 0
+
+        turns = -(-count // block)
+        if turns == 1:
+            turn(0, 0)
+        else:
+            lax.fori_loop(0, turns, turn, 0)
+
+
+def encode(value):
+    level = jnp.round(jnp.log(1.0 + jnp.abs(value) * F32(1.0 / FINEST)) * F32(STEEPNESS))
+    return jnp.where(value < 0.0, -level, level)
+
+
+def decode(code):
+    size = (jnp.exp(jnp.abs(code) * F32(1.0 / STEEPNESS)) - 1.0) * F32(FINEST)
+    return jnp.where(code < 0.0, -size, size)
+
+
+def pack_pair(low, high):
+    return jnp.concatenate([low, high], axis=0).astype(jnp.int32).astype(jnp.int16)
+
+
+def halo_kernel(
+    sizes, flags_ref, own_ref, east_ref, north_ref, sent_ref, winds_ref, copied, winds_copied
+):
+    rows, members, devices = sizes
+    band = flags_ref[0]
+    wind_halo = -(-HALO // CHUNK) * CHUNK
+    begin = jnp.where(band == 0, rows - HALO, 0)
+    copies = [
+        pltpu.make_async_copy(ref, winds_ref.at[side], winds_copied.at[side])
+        for side, ref in enumerate((east_ref, north_ref))
+    ]
+    copies.append(
+        pltpu.make_async_copy(own_ref.at[pl.ds(begin, HALO)], sent_ref.at[:HALO], copied)
+    )
+    for copy in copies:
+        copy.start()
+    winds = []
+    for side in range(2):
+        copies[side].wait()
+        wind = winds_ref[side].astype(F32)
+        wind = jnp.where(band == 0, wind[rows - wind_halo :], wind[:wind_halo])
+        winds += [wind[:, :LANES], wind[:, LANES:]]
+    sent_ref[HALO:] = jnp.concatenate(winds, axis=0).reshape(-1, sent_ref.shape[1], LANES)
+    copies[2].wait()
+
+
+def info_kernel(sizes, sent_ref, index_ref, value_ref, scale_ref, info_ref, ints_ref, floats_ref, copied):
+    rows, members, devices = sizes
+    own_rows = rows // devices
+    copies = [
+        pltpu.make_async_copy(index_ref, ints_ref, copied.at[0]),
+        pltpu.make_async_copy(value_ref, floats_ref.at[0], copied.at[1]),
+        pltpu.make_async_copy(scale_ref, floats_ref.at[1], copied.at[2]),
+    ]
+    for copy in copies:
+        copy.start()
+    for copy in copies:
+        copy.wait()
+    edges = []
+    for array in (ints_ref[...].astype(F32), floats_ref[0], floats_ref[1]):
+        edges += [array[:1], array[own_rows - 1 :]]
+    edges.append(jnp.zeros((info_ref.shape[1] - len(edges), LANES), F32))
+    told = jnp.concatenate(edges, axis=0)
+    info_ref[...] = jnp.broadcast_to(told[None], info_ref.shape)
+
+
+def stage_kernel(sizes, flags_ref, own_ref, parts_ref):
+    rows, members, devices = sizes
+    band = flags_ref[0]
+    matrix = parts_matrix()
+    block = 4 * CHUNK
+
+    def stage(index, _):
+        base = index * block
+
+        def row_of(k):
+            return jnp.where(band == 0, base + k, rows - 1 - base - k)
+
+        def load(row, lane):
+            return own_ref[row, pl.ds(lane, members, stride=4), :]
+
+        stage_states(load, row_of, block, members, matrix, parts_ref, base)
+        return 0
+
+    lax.fori_loop(0, rows // block, stage, 0)
+
+
+def forecast_kernel(
+    sizes,
+    flags_ref,
+    own_ref,
+    halo_ref,
+    east_ref,
+    north_ref,
+    out_ref,
+    edges_ref,
+    w_ref,
+    q_ref,
+    *stage_refs,
+):
+    rows, members, devices = sizes
+    own_rows = rows // devices
+    band = flags_ref[0]
+    matrix = parts_matrix()
+    north_sign = jnp.where(band == 0, F32(-0.25), F32(0.25))
+    wind_halo = -(-HALO // CHUNK) * CHUNK
+    pair = 2 * members
+
+    zero_rows = jnp.zeros((4, PAD, members, LANES), F32)
+    for ref in (q_ref, *stage_refs):
+        ref[:, :PAD] = zero_rows
+    stage_winds(
+        east_ref[...],
+        north_ref[...],
+        north_sign,
+        matrix,
+        w_ref,
+        jnp.where(band == 0, 0, wind_halo),
+    )
+    halo_winds = halo_ref[HALO:].reshape(4 * wind_halo, LANES).astype(BF16)
+    halo_winds = [halo_winds[k * wind_halo : (k + 1) * wind_halo] for k in range(4)]
+    stage_winds(
+        jnp.concatenate(halo_winds[:2], axis=1),
+        jnp.concatenate(halo_winds[2:], axis=1),
+        north_sign,
+        matrix,
+        w_ref,
+        jnp.where(band == 0, rows, 0),
+    )
+
+    q_ref[:, PAD : PAD + rows] = own_ref[...]
+
+    def row_of(k):
+        row = min(k, HALO - 1)
+        return jnp.where(band == 0, row, HALO - 1 - row)
+
+    def load(row, lane):
+        return halo_ref[row, pl.ds(lane, members, stride=4), :]
+
+    stage_states(load, row_of, wind_halo, members, matrix, q_ref, PAD + rows)
+
+    def wind_row(row):
+        return jnp.where(band == 0, row, rows + wind_halo - 1 - row)
+
+    def step(_, carry):
+        rk_passes(q_ref, stage_refs, PAD, w_ref, wind_row, 0, rows + HALO - 1, BLOCK)
+        return carry
+
+    lax.fori_loop(0, STEPS, step, 0)
+
+    def state(row):
+        return [q_ref[part, PAD + row] for part in range(4)]
+
+    def emit(group, _):
+        first = group * own_rows
+        place = group_place(sizes, band, group)
+        for j in range(0, own_rows, 2):
+            low, high = state(first + j), state(first + j + 1)
+            for part in range(4):
+                start = (part * own_rows + j) * members
+                out_ref[place, pl.ds(start, pair), :] = pack_pair(
+                    encode(low[part]), encode(high[part])
+                )
+        for side, row in enumerate((jnp.maximum(first - 1, 0), first + own_rows)):
+            for part, values in enumerate(state(row)):
+                edges_ref[place, 4 * side + part] = values
+        return 0
+
+    lax.fori_loop(0, devices, emit, 0)
+
+
+def observe_kernel(sizes, flags_ref, edges_ref, coded_ref, table_ref, out_ref):
+    rows, members, devices = sizes
+    band = flags_ref[0]
+    coded_rows = coded_ref.shape[1]
+    out_ref[:, :coded_rows] = coded_ref[...]
+
+    def emit(group, _):
+        place = group_place(sizes, band, group)
+        values = []
+        for side in range(2):
+            index = beside_info(table_ref, sizes, band, group, side == 1, 0)
+            index = jnp.broadcast_to(index, (members, LANES)).astype(jnp.int32)
+            states = [edges_ref[place, 4 * side + part] for part in range(4)]
+            values.append(encode(pick_lanes(states, index)))
+        out_ref[place, pl.ds(coded_rows, 2 * members), :] = pack_pair(*values)
+        return 0
+
+    lax.fori_loop(0, devices, emit, 0, unroll=4)
+
+
+def split_value(value):
+    high = value.astype(BF16)
+    return high, (value - high.astype(F32)).astype(BF16)
+
+
+def product(left, right):
+    (left_high, left_low), (right_high, right_low) = left, right
+    size = right_high.shape[1]
+    both = jnp.dot(
+        jnp.concatenate([left_high, left_low], axis=1),
+        jnp.concatenate(
+            [
+                jnp.concatenate([right_high, right_low], axis=1),
+                jnp.concatenate([right_high, jnp.zeros_like(right_low)], axis=1),
+            ],
+            axis=0,
+        ),
+        preferred_element_type=F32,
+    )
+    return both[:, :size] + both[:, size:]
+
+
+def analysis_kernel(
+    sizes,
+    flags_ref,
+    got_ref,
+    table_ref,
+    index_ref,
+    value_ref,
+    scale_ref,
+    out_ref,
+    states_ref,
+    upper_ref,
+    upper_low_ref,
+    lower_ref,
+    lower_low_ref,
+):
+    rows, members, devices = sizes
+    own_rows = rows // devices
+    total = members * devices
+    band = flags_ref[0]
+    group = group_place(sizes, band, flags_ref[1])
+    pair = 2 * members
+    beside_start = 4 * own_rows * members
+
+    def pair_at(start):
+        both = decode(got_ref[:, pl.ds(start, pair), :].astype(jnp.int32).astype(F32))
+        both = both.reshape(devices, 2, members, LANES)
+        return both[:, 0].reshape(total, LANES), both[:, 1].reshape(total, LANES)
+
+    def info(ref, j):
+        return ref[pl.ds(jnp.where(band == 0, j, own_rows - 1 - j), 1), :]
+
+    picked_rows = [None] * (own_rows + 2)
+    picked_rows[0], picked_rows[own_rows + 1] = pair_at(beside_start)
+    for j in range(0, own_rows, 2):
+        parts = [pair_at((part * own_rows + j) * members) for part in range(4)]
+        for k in range(2):
+            states_ref[j + k] = jnp.concatenate([part[k] for part in parts], axis=1)
+            index = jnp.broadcast_to(info(index_ref, j + k), (total, LANES)).astype(jnp.int32)
+            picked_rows[j + k + 1] = pick_lanes([part[k] for part in parts], index)
+
+    grams = []
+    couplings = []
+    for j in range(-1, own_rows + 1):
+        if 0 <= j < own_rows:
+            value, scale = info(value_ref, j), info(scale_ref, j)
+        else:
+            value, scale = [
+                beside_info(table_ref, sizes, band, group, j == own_rows, kind) for kind in (1, 2)
+            ]
+        if j == -1:
+            scale = jnp.where(group == 0, 0.0, scale)
+        picked = picked_rows[j + 1]
+        average = jnp.mean(picked, axis=0, keepdims=True)
+        spread = ((picked - average) * scale / math.sqrt(total - 1)).astype(BF16)
+        innovation = jnp.broadcast_to((value - average) * scale, (16, LANES)).astype(BF16)
+        contract = (((1,), (1,)), ((), ()))
+        grams.append(lax.dot_general(spread, spread, contract, preferred_element_type=F32))
+        couplings.append(
+            lax.dot_general(innovation, spread, contract, preferred_element_type=F32)
+        )
+
+    row_ids = lax.broadcasted_iota(jnp.int32, (total, total), 0)
+    column_ids = lax.broadcasted_iota(jnp.int32, (total, total), 1)
+    diagonal = row_ids == column_ids
+    identity = jnp.where(diagonal, F32(1.0), F32(0.0))
+
+    def put(high_ref, low_ref, j, value):
+        high_ref[j], low_ref[j] = split_value(value)
+
+    traces = []
+    for j in range(own_rows):
+        system = identity + 3.0 * grams[j + 1] + grams[j] + grams[j + 2]
+        trace = jnp.sum(
+            jnp.sum(jnp.where(diagonal, system, 0.0), axis=0, keepdims=True),
+            axis=1,
+            keepdims=True,
+        )
+        traces.append(trace)
+        scaled = system / trace
+        factor = split_value(1.5 * identity - 0.5 * scaled)
+        put(upper_ref, upper_low_ref, j, product(split_value(scaled), factor))
+        lower_ref[j], lower_low_ref[j] = factor
+
+    def factor_of(j):
+        lower = lower_ref[j], lower_low_ref[j]
+        upper = upper_ref[j], upper_low_ref[j]
+        return lower, upper, split_value(1.5 * identity - 0.5 * product(lower, upper))
+
+    def newton(turn, _):
+        parts = [factor_of(j) for j in range(own_rows)]
+        for j in range(own_rows):
+            lower, upper, factor = parts[j]
+            put(upper_ref, upper_low_ref, j, product(upper, factor))
+            put(lower_ref, lower_low_ref, j, product(factor, lower))
+        return 0
+
+    lax.fori_loop(0, ITERS - 2, newton, 0)
+
+    parts = [factor_of(j) for j in range(own_rows)]
+    weights = []
+    for j in range(own_rows):
+        lower, upper, factor = parts[j]
+        inv_root = product(factor, lower) / jnp.sqrt(traces[j])
+        coupling = 3.0 * couplings[j + 1] + couplings[j] + couplings[j + 2]
+        root_parts = split_value(inv_root)
+        half_step = product(split_value(coupling), root_parts)
+        mean_weight = product(split_value(half_step), root_parts)[:1] / math.sqrt(total - 1)
+        weights.append(split_value(inv_root + mean_weight))
+
+    for j in range(0, own_rows, 2):
+        for part in range(4):
+            place = (part * own_rows + j) * members
+            moved = []
+            for k in range(2):
+                state = states_ref[j + k, :, part * LANES : (part + 1) * LANES]
+                center = jnp.mean(state, axis=0, keepdims=True)
+                high, low = split_value(state - center)
+                weights_high, weights_low = weights[j + k]
+                result = center + (
+                    jnp.dot(weights_high, high, preferred_element_type=F32)
+                    + jnp.dot(weights_high, low, preferred_element_type=F32)
+                    + jnp.dot(weights_low, high, preferred_element_type=F32)
+                )
+                moved.append(result.reshape(devices, members, LANES))
+            out_ref[:, pl.ds(place, pair), :] = jnp.concatenate(moved, axis=1).astype(BF16)
+
+
+def unpack_kernel(sizes, flags_ref, got_ref, out_ref):
+    rows, members, devices = sizes
+    own_rows = rows // devices
+    band = flags_ref[0]
+    matrix = parts_matrix(from_parts=True)
+
+    batch = 4
+
+    def place(index, _):
+        device = index * batch
+        parts = jnp.concatenate(
+            [
+                jnp.concatenate(
+                    [
+                        got_ref[device + d, pl.ds(part * own_rows * members, own_rows * members), :]
+                        for d in range(batch)
+                    ],
+                    axis=0,
+                )
+                for part in range(4)
+            ],
+            axis=1,
+        )
+        joined = jnp.dot(parts, matrix, preferred_element_type=F32)
+        for k in range(batch * own_rows):
+            row = device * own_rows + k
+            if own_rows > 1:
+                flipped = (device + k // own_rows) * own_rows + own_rows - 1 - k % own_rows
+                row = jnp.where(band == 0, row, flipped)
+            values = joined[k * members : (k + 1) * members]
+            for field in range(2):
+                for half in range(2):
+                    first = (2 * field + half) * LANES
+                    out_ref[row, pl.ds(2 * half + field, members, stride=4), :] = values[
+                        :, first : first + LANES
+                    ]
+        return 0
+
+    lax.fori_loop(0, devices // batch, place, 0)
+
+
+def per_device_pair(background, wind_east, wind_north, obs_index, obs_value, obs_scale):
+    rows, members, fields, width = background.shape
+    devices = lax.axis_size("mem")
+    bands = lax.axis_size("lat")
+    own_rows = rows // devices
+    total = members * devices
+    sizes = (rows, members, devices)
+    band = lax.axis_index("lat")
+    flags = jnp.stack([band, lax.axis_index("mem")]).astype(jnp.int32)
+    smem = pl.BlockSpec(memory_space=pltpu.SMEM)
+    vmem = pl.BlockSpec(memory_space=pltpu.VMEM)
+    params = pltpu.CompilerParams(vmem_limit_bytes=40 * 1024 * 1024)
+
+    def cost(microseconds):
+        return pl.CostEstimate(
+            flops=0, bytes_accessed=int(microseconds * 3_000_000), transcendentals=0
+        )
+
+    grouped = members * fields * 2
+    own = background.reshape(rows, members, fields, 2, LANES)
+    own = own.transpose(0, 1, 3, 2, 4).reshape(rows, grouped, LANES)
+
+    wind_halo = -(-HALO // CHUNK) * CHUNK
+    hbm = pl.BlockSpec(memory_space=pltpu.HBM)
+    dma = pltpu.SemaphoreType.DMA
+    sent = pl.pallas_call(
+        functools.partial(halo_kernel, sizes),
+        out_shape=jax.ShapeDtypeStruct((HALO + 4 * wind_halo // grouped, grouped, LANES), F32),
+        in_specs=[smem, hbm, hbm, hbm],
+        out_specs=vmem,
+        scratch_shapes=[pltpu.VMEM((2, rows, width), BF16), dma, dma((2,))],
+        compiler_params=params,
+        cost_estimate=cost(1),
+        name="halo_rows",
+    )(flags, own, wind_east, wind_north)
+    halo = lax.ppermute(sent, "lat", [(0, 1), (1, 0)])
+    staged = pl.pallas_call(
+        functools.partial(stage_kernel, sizes),
+        out_shape=jax.ShapeDtypeStruct((4, rows, members, LANES), F32),
+        in_specs=[smem, vmem],
+        out_specs=vmem,
+        compiler_params=params,
+        cost_estimate=cost(2),
+        name="stage",
+    )(flags, own)
+    observations = [
+        array.reshape(own_rows, NOBS) for array in (obs_index, obs_value, obs_scale)
+    ]
+    info = pl.pallas_call(
+        functools.partial(info_kernel, sizes),
+        out_shape=jax.ShapeDtypeStruct((bands * devices, CHUNK, LANES), F32),
+        in_specs=[pl.BlockSpec(memory_space=pl.ANY)] + [hbm] * 3,
+        out_specs=vmem,
+        scratch_shapes=[
+            pltpu.VMEM((own_rows, LANES), jnp.int32),
+            pltpu.VMEM((2, own_rows, LANES), F32),
+            dma((3,)),
+        ],
+        compiler_params=params,
+        cost_estimate=cost(1),
+        name="info_rows",
+    )(
+        staged,
+        *observations,
+    )
+    table = lax.all_to_all(info, ("lat", "mem"), split_axis=0, concat_axis=0, tiled=True)
+
+    per_target = (4 * own_rows + 2) * members
+    wind_rows = pltpu.VMEM((8, rows + wind_halo, members, LANES), F32)
+    field_rows = pltpu.VMEM((4, PAD + rows + wind_halo, members, LANES), F32)
+    coded, edges = pl.pallas_call(
+        functools.partial(forecast_kernel, sizes),
+        out_shape=(
+            jax.ShapeDtypeStruct((devices, 4 * own_rows * members, LANES), jnp.int16),
+            jax.ShapeDtypeStruct((devices, 8, members, LANES), F32),
+        ),
+        in_specs=[smem] + [vmem] * 4,
+        out_specs=(vmem, vmem),
+        scratch_shapes=[wind_rows] + [field_rows] * 4,
+        compiler_params=params,
+        cost_estimate=cost(12),
+        name="forecast",
+    )(flags, staged, halo, wind_east, wind_north)
+    packed = pl.pallas_call(
+        functools.partial(observe_kernel, sizes),
+        out_shape=jax.ShapeDtypeStruct((devices, per_target, LANES), jnp.int16),
+        in_specs=[smem] + [vmem] * 3,
+        out_specs=vmem,
+        compiler_params=params,
+        cost_estimate=cost(1),
+        name="observe",
+    )(flags, edges, coded, table)
+    got = lax.all_to_all(packed, "mem", split_axis=0, concat_axis=0, tiled=True)
+    half_matrix = pltpu.VMEM((own_rows, total, total), BF16)
+    back = pl.pallas_call(
+        functools.partial(analysis_kernel, sizes),
+        out_shape=jax.ShapeDtypeStruct((devices, 4 * own_rows * members, LANES), BF16),
+        in_specs=[smem] + [vmem] * 5,
+        out_specs=vmem,
+        scratch_shapes=[pltpu.VMEM((own_rows, total, 4 * LANES), F32)] + [half_matrix] * 4,
+        compiler_params=params,
+        cost_estimate=cost(12),
+        name="analysis",
+    )(flags, got, table, *observations)
+    returned = lax.all_to_all(back, "mem", split_axis=0, concat_axis=0, tiled=True)
+    result = pl.pallas_call(
+        functools.partial(unpack_kernel, sizes),
+        out_shape=jax.ShapeDtypeStruct((rows, grouped, LANES), F32),
+        in_specs=[smem, vmem],
+        out_specs=vmem,
+        compiler_params=params,
+        cost_estimate=cost(2),
+        name="unpack",
+    )(flags, returned)
+    result = result.reshape(rows, members, 2, fields, LANES).transpose(0, 1, 3, 2, 4)
+    return result.reshape(rows, members, fields, width)
+
+
+def per_device(background, wind_east, wind_north, obs_index, obs_value, obs_scale):
+    rows, members, fields, width = background.shape
+    devices = lax.axis_size("mem")
+    fits = (
+        lax.axis_size("lat") == 2
+        and members == 8
+        and members * devices == LANES
+        and fields == 2
+        and width == 2 * LANES == PW
+        and obs_index.shape[2:] == (1, LANES)
+        and rows % (4 * CHUNK) == 0
+        and devices % 4 == 0
+        and 4 * STEPS % (rows // devices) == 0
+        and (rows // devices) % 2 == 0
+        and rows >= 8 * STEPS
+    )
+    run = per_device_pair if fits else per_device_any
+    return run(background, wind_east, wind_north, obs_index, obs_value, obs_scale)
+
+
 def solution(mesh):
     in_specs = (
         P("lat", "mem", None, None),

time: 249 us -> 79.1 us (0.32); the launches traced: 246 us -> 78.7 us
  other arithmetic: 65.9 us -> 0.07 us
  waiting for transfers between devices: 50.9 us -> 0.01 us
  local copies, waits for them, and re-layouts: 40.8 us -> 3.43 us
  starting transfers between devices: 34.9 us -> 7.93 us
  Pallas kernels: 0 us -> 26.8 us
  matrix products: 23.8 us -> 0 us
  blocking collectives: 27.4 us -> 40.3 us
    add x16 -> x0, other arithmetic: 61.8 us -> none  [the longest x4 17.7 us: per_device(): extended[4:-4]]
    slice x36 -> x0, local copies, waits for them, and re-layouts: 36.9 us -> none  [the longest x32 36 us: tendency(): jnp.roll(center_rows, -1, axis=-1) - jnp.roll(center_rows, 1, axis=-1)]
    ppermute x14 -> x1, waiting for transfers between devices: 28.1 us -> 0.01 us  [per_device_pair(): halo = lax.ppermute(sent, 'lat', [(0, 1), (1, 0)])]
    pallas_call x0 -> x7, Pallas kernels: none -> 26.8 us  [the longest x1 11.7 us: per_device_pair(): pl.pallas_call(functools.partial(forecast_kernel, sizes), out_shape=(jax....]
    ppermute x14 -> x1, starting transfers between devices: 28.9 us -> 3.03 us  [per_device_pair(): halo = lax.ppermute(sent, 'lat', [(0, 1), (1, 0)])]
    dot_general x43 -> x0, matrix products: 23.8 us -> none  [the longest x12 7.98 us: newton(): jnp.einsum('apij,apjk->apik', lower_iter, upper_iter, precision=HIGHEST)]
    all_to_all x1, waiting for transfers between devices: 22.8 us -> 0.01 us  [per_device_pair(): lax.all_to_all(info, ('lat', 'mem'), split_axis=0, concat_axis=0, tiled=T...]
    all_to_all x1 -> x2, blocking collectives: 27.4 us -> 40.3 us  [the longest x1 23 us: per_device_pair(): got = lax.all_to_all(packed, 'mem', split_axis=0, concat_axis=0, tiled=True)]
  transfers between devices with their start and end apart: 15 -> 2, of which waited for: 11 -> 0; matrix products, arithmetic and copies ran while one was open for 1% -> 0% of each run, Pallas kernels for 0% -> 18%
where the time goes in v2:
time: 79.1 us; the launch traced here: 78.7 us
  blocking collectives  40.3 us (51%)
  Pallas kernels  26.8 us (34%)
  starting transfers between devices  7.93 us (10%)
  local copies, waits for them, and re-layouts  3.43 us (4%)
    all_to_all x1, blocking collectives, per_device_pair(): got = lax.all_to_all(packed, 'mem', split_axis=0, concat_axis=0, tiled=True)  23 us
    all_to_all x1, blocking collectives, per_device_pair(): lax.all_to_all(back, 'mem', split_axis=0, concat_axis=0, tiled=True)  17.3 us
    pallas_call x1, Pallas kernels, per_device_pair(): pl.pallas_call(functools.partial(forecast_kernel, sizes), out_shape=(jax....  11.7 us
    pallas_call x1, Pallas kernels, per_device_pair(): pl.pallas_call(functools.partial(analysis_kernel, sizes), out_shape=jax.S...  8.09 us
    all_to_all x1, starting transfers between devices, per_device_pair(): lax.all_to_all(info, ('lat', 'mem'), split_axis=0, concat_axis=0, tiled=T...  4.9 us
    unnamed x16, local copies, waits for them, and re-layouts  3.43 us
    ppermute x1, starting transfers between devices, per_device_pair(): halo = lax.ppermute(sent, 'lat', [(0, 1), (1, 0)])  3.03 us
    pallas_call x1, Pallas kernels, per_device_pair(): pl.pallas_call(functools.partial(unpack_kernel, sizes), out_shape=jax.Sha...  2.68 us
  transfers between devices with their start and end apart: 2, of which 0 were waited for; matrix products, arithmetic and copies ran while one was open for 0% of the time, Pallas kernels for 18%

profile of v2, /device:TPU:0, one launch (start us, length us, event | category | flops | bytes accessed | tf_op | source)
XLA Modules:
  0.0 78.7 jit_solution(2411588970928392301)
XLA Ops:
  0.0 0.1 pad_add_fusion.flags_ref
  0.1 0.0 copy-start
  0.1 1.2 %copy-done = f32[64,8,2,256]{3,2,1,0:T(2,128)S(1)} copy-done((f32[64,8,2,256]{3,2,1,0:T(2,128)S(1)}, f32[64,8,2,256]{3,2,1,0:T(2,128)}, u32[]{:S(2)}) %copy-start) | copy-done | bytes 1048600
  1.3 0.0 copy-start.1
  1.3 0.8 copy-done.1
  2.1 0.0 copy-start.3
  2.1 0.8 copy-done.3
  2.8 0.7 halo_rows.1
  3.5 3.0 %collective-permute-start = (f32[20,32,128]{2,1,0:T(8,128)S(1)}, f32[20,32,128]{2,1,0:T(8,128)S(1)}, u32[]{:S(2)}, u32[]{:S(2)}) collective-permute-start(f32[20,32,128]{2,1,0:T(8,128)S(1)} %halo_rows.1), channel_id=1, source_target_pairs={{0,1},{1,0},{2,3},{3,2},{4,5},{5,4},{6,7},{7,6},{8,9},{9,8},{10,11... | collective-permute-start | bytes 983048 | tf_op jit(solution)/shard_map/ppermute | solution.py:697
  6.6 0.0 copy-start.7
  6.6 1.8 %stage.1.own_ref.sent_ref = f32[4,64,8,128]{3,2,1,0:T(8,128)S(1)} custom-call(s32[2]{0:T(128)S(1)} %pad_add_fusion.flags_ref, f32[64,32,128]{2,1,0:T(8,128)S(1)} %bitcast.16), custom_call_target="tpu_custom_call" | custom-call | bytes 6000000 | tf_op jit(solution)/shard_map/stage/pallas_call | solution.py:698
  8.4 0.0 copy-start.6
  8.4 0.0 copy-start.5
  8.4 0.0 copy-done.7
  8.4 0.7 copy-done.6
  9.1 0.0 copy-done.5
  9.1 0.7 info_rows.1
  9.8 0.0 copy-start.2
  9.8 0.0 copy-start.4
  9.8 4.9 %all-to-all-start = ((f32[32,8,128]{2,1,0:T(8,128)}), f32[32,8,128]{2,1,0:T(8,128)S(1)}, u32[]{:S(2)}, u32[]{:S(2)}) async-start(f32[32,8,128]{2,1,0:T(8,128)} %info_rows.1), calls=%async_computation | async-start | bytes 262144 | tf_op jit(solution)/shard_map/all_to_all | solution.py:727
  14.7 0.0 collective-permute-done.halo_ref
  14.8 0.0 copy-done.2
  14.8 0.0 copy-done.4
  14.8 11.7 %forecast.1 = (s16[16,128,128]{2,1,0:T(8,128)(2,1)S(1)}, f32[16,8,8,128]{3,2,1,0:T(8,128)S(1)}) custom-call(s32[2]{0:T(128)S(1)} %pad_add_fusion.flags_ref, f32[4,64,8,128]{3,2,1,0:T(8,128)S(1)} %stage.1.own_ref.sent_ref, f32[20,32,128]{2,1,0:T(8,128)S(1)} %collective-permute-done.halo_ref, bf16[64,256]{1,0:T(8,128)(2,1)S(1)} %copy-done.2, ...), custom_call_target="tpu_custom_call" | custom-call | bytes 36000000 | tf_op jit(solution)/shard_map/forecast/pallas_call | solution.py:732
  26.4 0.0 all-to-all-done.table_ref
  26.4 1.2 %observe.1 = s16[16,144,128]{2,1,0:T(8,128)(2,1)S(1)} custom-call(s32[2]{0:T(128)S(1)} %pad_add_fusion.flags_ref, f32[16,8,8,128]{3,2,1,0:T(8,128)S(1)} %get-tuple-element.7.edges_ref, s16[16,128,128]{2,1,0:T(8,128)(2,1)S(1)} %get-tuple-element.8.coded_ref, f32[32,8,128]{2,1,0:T(8,128)S(1)} %all-to-all-done.table_ref), custom_call_target="tpu_custom_call" | custom-call | bytes 3000000 | tf_op jit(solution)/shard_map/observe/pallas_call | solution.py:745
  27.6 23.0 %all_to_all.15.got_ref = s16[16,144,128]{2,1,0:T(8,128)(2,1)S(1)} all-to-all(s16[16,144,128]{2,1,0:T(8,128)(2,1)S(1)} %observe.1), channel_id=1, replica_groups=mesh['mem'=16,'lat'=2] {'mem'}, dimensions={0} | all-to-all | bytes 1179648 | tf_op jit(solution)/shard_map/all_to_all | solution.py:754
  50.6 8.1 %analysis.1 = bf16[16,128,128]{2,1,0:T(8,128)(2,1)S(1)} custom-call(s32[2]{0:T(128)S(1)} %pad_add_fusion.flags_ref, s16[16,144,128]{2,1,0:T(8,128)(2,1)S(1)} %all_to_all.15.got_ref, f32[32,8,128]{2,1,0:T(8,128)S(1)} %all-to-all-done.table_ref, s32[4,128]{1,0:T(4,128)S(1)} %bitcast.18, f32[4,128]{1,0:T(4,128)S(1)} %bitcast.20, f32[4,128]{1,0:T(4,128)S(1)} %bitcast.22), custom_call_target="tpu_custom_call" | custom-call | bytes 36000000 | tf_op jit(solution)/shard_map/analysis/pallas_call | solution.py:756
  58.7 17.3 %all_to_all.16.got_ref = bf16[16,128,128]{2,1,0:T(8,128)(2,1)S(1)} all-to-all(bf16[16,128,128]{2,1,0:T(8,128)(2,1)S(1)} %analysis.1), channel_id=1, replica_groups=mesh['mem'=16,'lat'=2] {'mem'}, dimensions={0} | all-to-all | bytes 1048576 | tf_op jit(solution)/shard_map/all_to_all | solution.py:766
  76.0 2.7 %unpack.1 = f32[64,32,128]{2,1,0:T(8,128)} custom-call(s32[2]{0:T(128)S(1)} %pad_add_fusion.flags_ref, bf16[16,128,128]{2,1,0:T(8,128)(2,1)S(1)} %all_to_all.16.got_ref), custom_call_target="tpu_custom_call" | custom-call | bytes 6000000 | tf_op jit(solution)/shard_map/unpack/pallas_call | solution.py:767
Async XLA Ops:
  0.1 1.2 %copy-start = (f32[64,8,2,256]{3,2,1,0:T(2,128)S(1)}, f32[64,8,2,256]{3,2,1,0:T(2,128)}, u32[]{:S(2)}) copy-start(f32[64,8,2,256]{3,2,1,0:T(2,128)} %param.6) | copy-start | bytes 3145732
  1.3 0.8 copy-start.1
  2.1 0.8 copy-start.3
  3.5 11.2 %collective-permute-start = (f32[20,32,128]{2,1,0:T(8,128)S(1)}, f32[20,32,128]{2,1,0:T(8,128)S(1)}, u32[]{:S(2)}, u32[]{:S(2)}) collective-permute-start(f32[20,32,128]{2,1,0:T(8,128)S(1)} %halo_rows.1), channel_id=1, source_target_pairs={{0,1},{1,0},{2,3},{3,2},{4,5},{5,4},{6,7},{7,6},{8,9},{9,8},{10,11... | collective-permute-start | bytes 983048 | tf_op jit(solution)/shard_map/ppermute | solution.py:697
  6.6 1.9 %copy-start.7 = (f32[1,4,1,128]{3,2,1,0:T(1,128)S(1)}, f32[1,4,1,128]{3,2,1,0:T(1,128)}, u32[]{:S(2)}) copy-start(f32[1,4,1,128]{3,2,1,0:T(1,128)} %param.11) | copy-start | bytes 6148
  8.4 0.7 copy-start.6
  8.4 0.7 copy-start.5
  9.8 4.9 %copy-start.2 = (bf16[64,256]{1,0:T(8,128)(2,1)S(1)}, bf16[64,256]{1,0:T(8,128)(2,1)}, u32[]{:S(2)}) copy-start(bf16[64,256]{1,0:T(8,128)(2,1)} %east_ref.3) | copy-start | bytes 98308
  9.8 4.9 %copy-start.4 = (bf16[64,256]{1,0:T(8,128)(2,1)S(1)}, bf16[64,256]{1,0:T(8,128)(2,1)}, u32[]{:S(2)}) copy-start(bf16[64,256]{1,0:T(8,128)(2,1)} %north_ref.3) | copy-start | bytes 98308
  9.8 16.6 %all-to-all-start = ((f32[32,8,128]{2,1,0:T(8,128)}), f32[32,8,128]{2,1,0:T(8,128)S(1)}, u32[]{:S(2)}, u32[]{:S(2)}) async-start(f32[32,8,128]{2,1,0:T(8,128)} %info_rows.1), calls=%async_computation | async-start | bytes 262144 | tf_op jit(solution)/shard_map/all_to_all | solution.py:727

commit v3 on v2

--- a/solution.py
+++ b/solution.py
@@ -152,9 +152,13 @@
 
 
 PAD = 8
-BLOCK = 20
+TURNS = 4
 FINEST = 0.05
 LARGEST = 16.0 * sum(1.8**power / math.factorial(power) for power in range(5)) ** STEPS
+STATE_LEVELS = 2047.0
+WIND_LEVELS = 32767.0
+VALUE_LEVELS = 8191.0
+SCALE_LEVELS = 4095.0
 STEEPNESS = 32766.0 / math.log(1.0 + LARGEST / FINEST)
 
 
@@ -177,14 +181,27 @@
     return jnp.where(band == 0, group, sizes[2] - 1 - group)
 
 
-def beside_info(table_ref, sizes, band, group, is_after, kind):
+def beside_rows(table_ref, sizes, band, group, is_after):
     devices = sizes[2]
     near = group + 1 if is_after else jnp.maximum(group - 1, 0)
     over = near == devices
     place = jnp.where(over, jnp.where(band == 0, 0, devices - 1), group_place(sizes, band, near))
     near_band = jnp.where(over, 1 - band, band)
     last = jnp.where(band == 0, 0, 1) if is_after else jnp.where(band == 0, 1, 0)
-    return table_ref[near_band * devices + place, pl.ds(2 * kind + last, 1), :]
+    return near_band * devices + place, last
+
+
+def beside_index(table_ref, sizes, band, group, is_after):
+    place, last = beside_rows(table_ref, sizes, band, group, is_after)
+    return jnp.bitwise_and(table_ref[place, pl.ds(last, 1), :], 65535)
+
+
+def beside_observation(table_ref, sizes, band, group, is_after):
+    place, last = beside_rows(table_ref, sizes, band, group, is_after)
+    value = jnp.right_shift(table_ref[place, pl.ds(last, 1), :], 16)
+    scales = table_ref[place, 2:3, :]
+    scale = jnp.where(last == 1, jnp.right_shift(scales, 16), jnp.bitwise_and(scales, 65535))
+    return value.astype(F32) * F32(1.0 / VALUE_LEVELS), scale.astype(F32) * F32(1.0 / SCALE_LEVELS)
 
 
 def parts_matrix(from_parts=False):
@@ -298,55 +315,64 @@
     return jnp.concatenate([low, high], axis=0).astype(jnp.int32).astype(jnp.int16)
 
 
-def halo_kernel(
-    sizes, flags_ref, own_ref, east_ref, north_ref, sent_ref, winds_ref, copied, winds_copied
+def tell_kernel(
+    sizes,
+    own_ref,
+    east_ref,
+    north_ref,
+    index_ref,
+    value_ref,
+    scale_ref,
+    sent_ref,
+    told_ref,
+    edge_ref,
+    winds_ref,
+    ints_ref,
+    floats_ref,
+    copied,
 ):
     rows, members, devices = sizes
-    band = flags_ref[0]
+    own_rows = rows // devices
+    band = lax.axis_index("lat")
     wind_halo = -(-HALO // CHUNK) * CHUNK
     begin = jnp.where(band == 0, rows - HALO, 0)
+    pairs = (
+        (own_ref.at[pl.ds(begin, HALO)], edge_ref),
+        (east_ref, winds_ref.at[0]),
+        (north_ref, winds_ref.at[1]),
+        (index_ref, ints_ref),
+        (value_ref, floats_ref.at[0]),
+        (scale_ref, floats_ref.at[1]),
+    )
     copies = [
-        pltpu.make_async_copy(ref, winds_ref.at[side], winds_copied.at[side])
-        for side, ref in enumerate((east_ref, north_ref))
-    ]
-    copies.append(
-        pltpu.make_async_copy(own_ref.at[pl.ds(begin, HALO)], sent_ref.at[:HALO], copied)
-    )
-    for copy in copies:
-        copy.start()
-    winds = []
-    for side in range(2):
-        copies[side].wait()
-        wind = winds_ref[side].astype(F32)
-        wind = jnp.where(band == 0, wind[rows - wind_halo :], wind[:wind_halo])
-        winds += [wind[:, :LANES], wind[:, LANES:]]
-    sent_ref[HALO:] = jnp.concatenate(winds, axis=0).reshape(-1, sent_ref.shape[1], LANES)
-    copies[2].wait()
-
-
-def info_kernel(sizes, sent_ref, index_ref, value_ref, scale_ref, info_ref, ints_ref, floats_ref, copied):
-    rows, members, devices = sizes
-    own_rows = rows // devices
-    copies = [
-        pltpu.make_async_copy(index_ref, ints_ref, copied.at[0]),
-        pltpu.make_async_copy(value_ref, floats_ref.at[0], copied.at[1]),
-        pltpu.make_async_copy(scale_ref, floats_ref.at[1], copied.at[2]),
+        pltpu.make_async_copy(source, target, copied.at[turn])
+        for turn, (source, target) in enumerate(pairs)
     ]
     for copy in copies:
         copy.start()
-    for copy in copies:
+    for copy in copies[1:]:
         copy.wait()
-    edges = []
-    for array in (ints_ref[...].astype(F32), floats_ref[0], floats_ref[1]):
-        edges += [array[:1], array[own_rows - 1 :]]
-    edges.append(jnp.zeros((info_ref.shape[1] - len(edges), LANES), F32))
-    told = jnp.concatenate(edges, axis=0)
-    info_ref[...] = jnp.broadcast_to(told[None], info_ref.shape)
-
-
-def stage_kernel(sizes, flags_ref, own_ref, parts_ref):
+    winds = []
+    for side in range(2):
+        wind = winds_ref[side].astype(F32) * F32(WIND_LEVELS)
+        wind = jnp.where(band == 0, wind[rows - wind_halo :], wind[:wind_halo])
+        winds += [wind[:, :LANES], wind[:, LANES:]]
+    winds = jnp.round(jnp.concatenate(winds, axis=0)).astype(jnp.int32).astype(jnp.int16)
+    sent_ref[HALO:] = winds.reshape(-1, sent_ref.shape[1], LANES)
+    values = jnp.round(floats_ref[0] * F32(VALUE_LEVELS)).astype(jnp.int32)
+    scales = jnp.round(floats_ref[1] * F32(SCALE_LEVELS)).astype(jnp.int32)
+    pairs = ints_ref[...] + values * 65536
+    ends = [row[end : end + 1] for row in (pairs, scales) for end in (0, own_rows - 1)]
+    told = jnp.concatenate(ends[:2] + [ends[2] + ends[3] * 65536, jnp.zeros_like(ends[0])], axis=0)
+    told_ref[...] = jnp.broadcast_to(told[None], told_ref.shape)
+    copies[0].wait()
+    edge = jnp.round(edge_ref[...] * F32(STATE_LEVELS))
+    sent_ref[:HALO] = edge.astype(jnp.int32).astype(jnp.int16)
+
+
+def stage_kernel(sizes, own_ref, parts_ref):
     rows, members, devices = sizes
-    band = flags_ref[0]
+    band = lax.axis_index("lat")
     matrix = parts_matrix()
     block = 4 * CHUNK
 
@@ -367,20 +393,20 @@
 
 def forecast_kernel(
     sizes,
-    flags_ref,
     own_ref,
     halo_ref,
     east_ref,
     north_ref,
     out_ref,
     edges_ref,
+    edge_ref,
     w_ref,
     q_ref,
     *stage_refs,
 ):
     rows, members, devices = sizes
     own_rows = rows // devices
-    band = flags_ref[0]
+    band = lax.axis_index("lat")
     matrix = parts_matrix()
     north_sign = jnp.where(band == 0, F32(-0.25), F32(0.25))
     wind_halo = -(-HALO // CHUNK) * CHUNK
@@ -397,7 +423,9 @@
         w_ref,
         jnp.where(band == 0, 0, wind_halo),
     )
-    halo_winds = halo_ref[HALO:].reshape(4 * wind_halo, LANES).astype(BF16)
+    edge_ref[...] = halo_ref[:HALO].astype(jnp.int32).astype(F32) * F32(1.0 / STATE_LEVELS)
+    halo_winds = halo_ref[HALO:].astype(jnp.int32).astype(F32).reshape(4 * wind_halo, LANES)
+    halo_winds = (halo_winds * F32(1.0 / WIND_LEVELS)).astype(BF16)
     halo_winds = [halo_winds[k * wind_halo : (k + 1) * wind_halo] for k in range(4)]
     stage_winds(
         jnp.concatenate(halo_winds[:2], axis=1),
@@ -415,18 +443,16 @@
         return jnp.where(band == 0, row, HALO - 1 - row)
 
     def load(row, lane):
-        return halo_ref[row, pl.ds(lane, members, stride=4), :]
+        return edge_ref[row, pl.ds(lane, members, stride=4), :]
 
     stage_states(load, row_of, wind_halo, members, matrix, q_ref, PAD + rows)
 
     def wind_row(row):
         return jnp.where(band == 0, row, rows + wind_halo - 1 - row)
 
-    def step(_, carry):
-        rk_passes(q_ref, stage_refs, PAD, w_ref, wind_row, 0, rows + HALO - 1, BLOCK)
-        return carry
-
-    lax.fori_loop(0, STEPS, step, 0)
+    for step in range(STEPS):
+        count = rows + HALO - 1 - 4 * step
+        rk_passes(q_ref, stage_refs, PAD, w_ref, wind_row, 0, count, -(-count // TURNS))
 
     def state(row):
         return [q_ref[part, PAD + row] for part in range(4)]
@@ -449,9 +475,9 @@
     lax.fori_loop(0, devices, emit, 0)
 
 
-def observe_kernel(sizes, flags_ref, edges_ref, coded_ref, table_ref, out_ref):
+def observe_kernel(sizes, edges_ref, coded_ref, table_ref, out_ref):
     rows, members, devices = sizes
-    band = flags_ref[0]
+    band = lax.axis_index("lat")
     coded_rows = coded_ref.shape[1]
     out_ref[:, :coded_rows] = coded_ref[...]
 
@@ -459,8 +485,8 @@
         place = group_place(sizes, band, group)
         values = []
         for side in range(2):
-            index = beside_info(table_ref, sizes, band, group, side == 1, 0)
-            index = jnp.broadcast_to(index, (members, LANES)).astype(jnp.int32)
+            index = beside_index(table_ref, sizes, band, group, side == 1)
+            index = jnp.broadcast_to(index, (members, LANES))
             states = [edges_ref[place, 4 * side + part] for part in range(4)]
             values.append(encode(pick_lanes(states, index)))
         out_ref[place, pl.ds(coded_rows, 2 * members), :] = pack_pair(*values)
@@ -493,7 +519,6 @@
 
 def analysis_kernel(
     sizes,
-    flags_ref,
     got_ref,
     table_ref,
     index_ref,
@@ -509,8 +534,8 @@
     rows, members, devices = sizes
     own_rows = rows // devices
     total = members * devices
-    band = flags_ref[0]
-    group = group_place(sizes, band, flags_ref[1])
+    band = lax.axis_index("lat")
+    group = group_place(sizes, band, lax.axis_index("mem"))
     pair = 2 * members
     beside_start = 4 * own_rows * members
 
@@ -537,9 +562,7 @@
         if 0 <= j < own_rows:
             value, scale = info(value_ref, j), info(scale_ref, j)
         else:
-            value, scale = [
-                beside_info(table_ref, sizes, band, group, j == own_rows, kind) for kind in (1, 2)
-            ]
+            value, scale = beside_observation(table_ref, sizes, band, group, j == own_rows)
         if j == -1:
             scale = jnp.where(group == 0, 0.0, scale)
         picked = picked_rows[j + 1]
@@ -618,13 +641,13 @@
             out_ref[:, pl.ds(place, pair), :] = jnp.concatenate(moved, axis=1).astype(BF16)
 
 
-def unpack_kernel(sizes, flags_ref, got_ref, out_ref):
+def unpack_kernel(sizes, got_ref, out_ref):
     rows, members, devices = sizes
     own_rows = rows // devices
-    band = flags_ref[0]
+    band = lax.axis_index("lat")
     matrix = parts_matrix(from_parts=True)
 
-    batch = 4
+    batch = devices
 
     def place(index, _):
         device = index * batch
@@ -666,11 +689,9 @@
     own_rows = rows // devices
     total = members * devices
     sizes = (rows, members, devices)
-    band = lax.axis_index("lat")
-    flags = jnp.stack([band, lax.axis_index("mem")]).astype(jnp.int32)
-    smem = pl.BlockSpec(memory_space=pltpu.SMEM)
     vmem = pl.BlockSpec(memory_space=pltpu.VMEM)
     params = pltpu.CompilerParams(vmem_limit_bytes=40 * 1024 * 1024)
+    whole = pltpu.CompilerParams(vmem_limit_bytes=127 * 512 * 1024)
 
     def cost(microseconds):
         return pl.CostEstimate(
@@ -684,47 +705,40 @@
     wind_halo = -(-HALO // CHUNK) * CHUNK
     hbm = pl.BlockSpec(memory_space=pltpu.HBM)
     dma = pltpu.SemaphoreType.DMA
-    sent = pl.pallas_call(
-        functools.partial(halo_kernel, sizes),
-        out_shape=jax.ShapeDtypeStruct((HALO + 4 * wind_halo // grouped, grouped, LANES), F32),
-        in_specs=[smem, hbm, hbm, hbm],
-        out_specs=vmem,
-        scratch_shapes=[pltpu.VMEM((2, rows, width), BF16), dma, dma((2,))],
-        compiler_params=params,
+    observations = [
+        array.reshape(own_rows, NOBS) for array in (obs_index, obs_value, obs_scale)
+    ]
+    edge_rows = pltpu.VMEM((HALO, grouped, LANES), F32)
+    sent, told = pl.pallas_call(
+        functools.partial(tell_kernel, sizes),
+        out_shape=(
+            jax.ShapeDtypeStruct((HALO + 4 * wind_halo // grouped, grouped, LANES), jnp.int16),
+            jax.ShapeDtypeStruct((bands * devices, 4, LANES), jnp.int32),
+        ),
+        in_specs=[hbm] * 6,
+        out_specs=(vmem, vmem),
+        scratch_shapes=[
+            edge_rows,
+            pltpu.VMEM((2, rows, width), BF16),
+            pltpu.VMEM((own_rows, LANES), jnp.int32),
+            pltpu.VMEM((2, own_rows, LANES), F32),
+            dma((6,)),
+        ],
+        compiler_params=whole,
         cost_estimate=cost(1),
-        name="halo_rows",
-    )(flags, own, wind_east, wind_north)
+        name="tell",
+    )(own, wind_east, wind_north, *observations)
     halo = lax.ppermute(sent, "lat", [(0, 1), (1, 0)])
+    table = lax.all_to_all(told, ("lat", "mem"), split_axis=0, concat_axis=0, tiled=True)
     staged = pl.pallas_call(
         functools.partial(stage_kernel, sizes),
         out_shape=jax.ShapeDtypeStruct((4, rows, members, LANES), F32),
-        in_specs=[smem, vmem],
+        in_specs=[vmem],
         out_specs=vmem,
         compiler_params=params,
         cost_estimate=cost(2),
         name="stage",
-    )(flags, own)
-    observations = [
-        array.reshape(own_rows, NOBS) for array in (obs_index, obs_value, obs_scale)
-    ]
-    info = pl.pallas_call(
-        functools.partial(info_kernel, sizes),
-        out_shape=jax.ShapeDtypeStruct((bands * devices, CHUNK, LANES), F32),
-        in_specs=[pl.BlockSpec(memory_space=pl.ANY)] + [hbm] * 3,
-        out_specs=vmem,
-        scratch_shapes=[
-            pltpu.VMEM((own_rows, LANES), jnp.int32),
-            pltpu.VMEM((2, own_rows, LANES), F32),
-            dma((3,)),
-        ],
-        compiler_params=params,
-        cost_estimate=cost(1),
-        name="info_rows",
-    )(
-        staged,
-        *observations,
-    )
-    table = lax.all_to_all(info, ("lat", "mem"), split_axis=0, concat_axis=0, tiled=True)
+    )(own)
 
     per_target = (4 * own_rows + 2) * members
     wind_rows = pltpu.VMEM((8, rows + wind_halo, members, LANES), F32)
@@ -735,44 +749,44 @@
             jax.ShapeDtypeStruct((devices, 4 * own_rows * members, LANES), jnp.int16),
             jax.ShapeDtypeStruct((devices, 8, members, LANES), F32),
         ),
-        in_specs=[smem] + [vmem] * 4,
+        in_specs=[vmem] * 4,
         out_specs=(vmem, vmem),
-        scratch_shapes=[wind_rows] + [field_rows] * 4,
+        scratch_shapes=[edge_rows, wind_rows] + [field_rows] * 4,
         compiler_params=params,
         cost_estimate=cost(12),
         name="forecast",
-    )(flags, staged, halo, wind_east, wind_north)
+    )(staged, halo, wind_east, wind_north)
     packed = pl.pallas_call(
         functools.partial(observe_kernel, sizes),
         out_shape=jax.ShapeDtypeStruct((devices, per_target, LANES), jnp.int16),
-        in_specs=[smem] + [vmem] * 3,
+        in_specs=[vmem] * 3,
         out_specs=vmem,
         compiler_params=params,
         cost_estimate=cost(1),
         name="observe",
-    )(flags, edges, coded, table)
+    )(edges, coded, table)
     got = lax.all_to_all(packed, "mem", split_axis=0, concat_axis=0, tiled=True)
     half_matrix = pltpu.VMEM((own_rows, total, total), BF16)
     back = pl.pallas_call(
         functools.partial(analysis_kernel, sizes),
         out_shape=jax.ShapeDtypeStruct((devices, 4 * own_rows * members, LANES), BF16),
-        in_specs=[smem] + [vmem] * 5,
+        in_specs=[vmem] * 5,
         out_specs=vmem,
         scratch_shapes=[pltpu.VMEM((own_rows, total, 4 * LANES), F32)] + [half_matrix] * 4,
         compiler_params=params,
         cost_estimate=cost(12),
         name="analysis",
-    )(flags, got, table, *observations)
+    )(got, table, *observations)
     returned = lax.all_to_all(back, "mem", split_axis=0, concat_axis=0, tiled=True)
     result = pl.pallas_call(
         functools.partial(unpack_kernel, sizes),
         out_shape=jax.ShapeDtypeStruct((rows, grouped, LANES), F32),
-        in_specs=[smem, vmem],
+        in_specs=[vmem],
         out_specs=vmem,
         compiler_params=params,
         cost_estimate=cost(2),
         name="unpack",
-    )(flags, returned)
+    )(returned)
     result = result.reshape(rows, members, 2, fields, LANES).transpose(0, 1, 3, 2, 4)
     return result.reshape(rows, members, fields, width)
 
@@ -788,7 +802,6 @@
         and width == 2 * LANES == PW
         and obs_index.shape[2:] == (1, LANES)
         and rows % (4 * CHUNK) == 0
-        and devices % 4 == 0
         and 4 * STEPS % (rows // devices) == 0
         and (rows // devices) % 2 == 0
         and rows >= 8 * STEPS

time: 79.1 us -> 73.3 us (0.927)
  Pallas kernels: 26.8 us -> 23.3 us
  local copies, waits for them, and re-layouts: 3.43 us -> 1.25 us
    unnamed x16 -> x12, local copies, waits for them, and re-layouts: 3.43 us -> 1.25 us
    pallas_call x1, Pallas kernels: 2.68 us -> 1.44 us  [per_device_pair(): pl.pallas_call(functools.partial(unpack_kernel, sizes), out_shape=jax.Sha...]
    pallas_call x1, Pallas kernels: 11.7 us -> 10.7 us  [per_device_pair(): pl.pallas_call(functools.partial(forecast_kernel, sizes), out_shape=(jax....]
    pallas_call x2 -> x1, Pallas kernels: 1.41 us -> 1.71 us  [per_device_pair(): pl.pallas_call(functools.partial(tell_kernel, sizes), out_shape=(jax.Shap...]
  transfers between devices with their start and end apart: 2 -> 2, of which waited for: 0 -> 0; matrix products, arithmetic and copies ran while one was open for 0% -> 0% of each run, Pallas kernels for 18% -> 16%
where the time goes in v3:
time: 73.3 us; the launch traced here: 73 us
  blocking collectives  40.4 us (55%)
  Pallas kernels  23.3 us (32%)
  starting transfers between devices  7.93 us (11%)
  local copies, waits for them, and re-layouts  1.25 us (2%)
    all_to_all x1, blocking collectives, per_device_pair(): got = lax.all_to_all(packed, 'mem', split_axis=0, concat_axis=0, tiled=True)  23.1 us
    all_to_all x1, blocking collectives, per_device_pair(): lax.all_to_all(back, 'mem', split_axis=0, concat_axis=0, tiled=True)  17.3 us
    pallas_call x1, Pallas kernels, per_device_pair(): pl.pallas_call(functools.partial(forecast_kernel, sizes), out_shape=(jax....  10.7 us
    pallas_call x1, Pallas kernels, per_device_pair(): pl.pallas_call(functools.partial(analysis_kernel, sizes), out_shape=jax.S...  7.55 us
    all_to_all x1, starting transfers between devices, per_device_pair(): lax.all_to_all(told, ('lat', 'mem'), split_axis=0, concat_axis=0, tiled=T...  4.89 us
    ppermute x1, starting transfers between devices, per_device_pair(): halo = lax.ppermute(sent, 'lat', [(0, 1), (1, 0)])  3.03 us
    pallas_call x1, Pallas kernels, per_device_pair(): pl.pallas_call(functools.partial(tell_kernel, sizes), out_shape=(jax.Shap...  1.71 us
  transfers between devices with their start and end apart: 2, of which 0 were waited for; matrix products, arithmetic and copies ran while one was open for 0% of the time, Pallas kernels for 16%

profile of v3, /device:TPU:0, one launch (start us, length us, event | category | flops | bytes accessed | tf_op | source)
XLA Modules:
  0.0 73.0 jit_solution(2852284160438243832)
XLA Ops:
  0.0 1.7 %tell.1 = (s16[20,32,128]{2,1,0:T(8,128)(2,1)}, s32[32,4,128]{2,1,0:T(4,128)}) custom-call(f32[64,32,128]{2,1,0:T(8,128)} %bitcast.13, bf16[64,256]{1,0:T(8,128)(2,1)} %east_ref.3, bf16[64,256]{1,0:T(8,128)(2,1)} %north_ref.3, s32[4,128]{1,0:T(4,128)} %bitcast.15, f32[4,128]{1,0:T(4,128)} %bitcast.17, f32[4,128]{1,0:T(4,128)} %bitcast.19), custom_call_target="tpu_custom_call" | custom-call | bytes 3000000 | tf_op jit(solution)/shard_map/tell/pallas_call | solution.py:712
  1.7 3.0 %collective-permute-start = (s16[20,32,128]{2,1,0:T(8,128)(2,1)}, s16[20,32,128]{2,1,0:T(8,128)(2,1)S(1)}, u32[]{:S(2)}, u32[]{:S(2)}) collective-permute-start(s16[20,32,128]{2,1,0:T(8,128)(2,1)} %get-tuple-element.9), channel_id=1, source_target_pairs={{0,1},{1,0},{2,3},{3,2},{4,5},{5,4},{6,7},{7,6},{8,9},{9,8},{10,11... | collective-permute-start | bytes 491528 | tf_op jit(solution)/shard_map/ppermute | solution.py:731
  4.7 4.9 %all-to-all-start = ((s32[32,4,128]{2,1,0:T(4,128)}), s32[32,4,128]{2,1,0:T(4,128)S(1)}, u32[]{:S(2)}, u32[]{:S(2)}) async-start(s32[32,4,128]{2,1,0:T(4,128)} %get-tuple-element.12), calls=%async_computation | async-start | bytes 131072 | tf_op jit(solution)/shard_map/all_to_all | solution.py:732
  9.6 0.0 copy-start
  9.7 1.2 %copy-done = f32[64,8,2,256]{3,2,1,0:T(2,128)S(1)} copy-done((f32[64,8,2,256]{3,2,1,0:T(2,128)S(1)}, f32[64,8,2,256]{3,2,1,0:T(2,128)}, u32[]{:S(2)}) %copy-start) | copy-done | bytes 1048600
  10.9 0.0 copy-start.1
  10.9 0.0 copy-start.2
  10.9 1.3 %stage.1.own_ref = f32[4,64,8,128]{3,2,1,0:T(8,128)S(1)} custom-call(f32[64,32,128]{2,1,0:T(8,128)S(1)} %bitcast.14), custom_call_target="tpu_custom_call" | custom-call | bytes 6000000 | tf_op jit(solution)/shard_map/stage/pallas_call | solution.py:733
  12.2 0.0 collective-permute-done.halo_ref
  12.2 0.0 copy-done.1
  12.2 0.0 copy-done.2
  12.2 10.7 %forecast.1 = (s16[16,128,128]{2,1,0:T(8,128)(2,1)S(1)}, f32[16,8,8,128]{3,2,1,0:T(8,128)S(1)}) custom-call(f32[4,64,8,128]{3,2,1,0:T(8,128)S(1)} %stage.1.own_ref, s16[20,32,128]{2,1,0:T(8,128)(2,1)S(1)} %collective-permute-done.halo_ref, bf16[64,256]{1,0:T(8,128)(2,1)S(1)} %copy-done.1, bf16[64,256]{1,0:T(8,128)(2,1)S(1)} %copy-done.2), custom_call_target="tpu_custom_call" | custom-call | bytes 36000000 | tf_op jit(solution)/shard_map/forecast/pallas_call | solution.py:746
  22.9 0.0 all-to-all-done.table_ref
  22.9 0.6 observe.1
  23.5 0.0 copy-start.3
  23.6 0.0 copy-start.4
  23.6 0.0 copy-start.5
  23.6 23.1 %all_to_all.15.got_ref = s16[16,144,128]{2,1,0:T(8,128)(2,1)S(1)} all-to-all(s16[16,144,128]{2,1,0:T(8,128)(2,1)S(1)} %observe.1), channel_id=1, replica_groups=mesh['mem'=16,'lat'=2] {'mem'}, dimensions={0} | all-to-all | bytes 1179648 | tf_op jit(solution)/shard_map/all_to_all | solution.py:768
  46.7 0.0 copy-done.3
  46.7 0.0 copy-done.4
  46.7 0.0 copy-done.5
  46.7 7.6 %analysis.1 = bf16[16,128,128]{2,1,0:T(8,128)(2,1)S(1)} custom-call(s16[16,144,128]{2,1,0:T(8,128)(2,1)S(1)} %all_to_all.15.got_ref, s32[32,4,128]{2,1,0:T(4,128)S(1)} %all-to-all-done.table_ref, s32[4,128]{1,0:T(4,128)S(1)} %bitcast.16, f32[4,128]{1,0:T(4,128)S(1)} %bitcast.18, f32[4,128]{1,0:T(4,128)S(1)} %bitcast.20), custom_call_target="tpu_custom_call" | custom-call | bytes 36000000 | tf_op jit(solution)/shard_map/analysis/pallas_call | solution.py:770
  54.3 17.3 %all_to_all.16.got_ref = bf16[16,128,128]{2,1,0:T(8,128)(2,1)S(1)} all-to-all(bf16[16,128,128]{2,1,0:T(8,128)(2,1)S(1)} %analysis.1), channel_id=1, replica_groups=mesh['mem'=16,'lat'=2] {'mem'}, dimensions={0} | all-to-all | bytes 1048576 | tf_op jit(solution)/shard_map/all_to_all | solution.py:780
  71.5 1.4 %unpack.1 = f32[64,32,128]{2,1,0:T(8,128)} custom-call(bf16[16,128,128]{2,1,0:T(8,128)(2,1)S(1)} %all_to_all.16.got_ref), custom_call_target="tpu_custom_call" | custom-call | bytes 6000000 | tf_op jit(solution)/shard_map/unpack/pallas_call | solution.py:781
Async XLA Ops:
  1.7 10.5 %collective-permute-start = (s16[20,32,128]{2,1,0:T(8,128)(2,1)}, s16[20,32,128]{2,1,0:T(8,128)(2,1)S(1)}, u32[]{:S(2)}, u32[]{:S(2)}) collective-permute-start(s16[20,32,128]{2,1,0:T(8,128)(2,1)} %get-tuple-element.9), channel_id=1, source_target_pairs={{0,1},{1,0},{2,3},{3,2},{4,5},{5,4},{6,7},{7,6},{8,9},{9,8},{10,11... | collective-permute-start | bytes 491528 | tf_op jit(solution)/shard_map/ppermute | solution.py:731
  4.7 18.2 %all-to-all-start = ((s32[32,4,128]{2,1,0:T(4,128)}), s32[32,4,128]{2,1,0:T(4,128)S(1)}, u32[]{:S(2)}, u32[]{:S(2)}) async-start(s32[32,4,128]{2,1,0:T(4,128)} %get-tuple-element.12), calls=%async_computation | async-start | bytes 131072 | tf_op jit(solution)/shard_map/all_to_all | solution.py:732
  9.6 1.2 %copy-start = (f32[64,8,2,256]{3,2,1,0:T(2,128)S(1)}, f32[64,8,2,256]{3,2,1,0:T(2,128)}, u32[]{:S(2)}) copy-start(f32[64,8,2,256]{3,2,1,0:T(2,128)} %param.6) | copy-start | bytes 3145732
  10.9 1.3 %copy-start.1 = (bf16[64,256]{1,0:T(8,128)(2,1)S(1)}, bf16[64,256]{1,0:T(8,128)(2,1)}, u32[]{:S(2)}) copy-start(bf16[64,256]{1,0:T(8,128)(2,1)} %east_ref.3) | copy-start | bytes 98308
  10.9 1.3 %copy-start.2 = (bf16[64,256]{1,0:T(8,128)(2,1)S(1)}, bf16[64,256]{1,0:T(8,128)(2,1)}, u32[]{:S(2)}) copy-start(bf16[64,256]{1,0:T(8,128)(2,1)} %north_ref.3) | copy-start | bytes 98308
  23.5 23.2 %copy-start.3 = (s32[1,4,1,128]{3,2,1,0:T(1,128)S(1)}, s32[1,4,1,128]{3,2,1,0:T(1,128)}, u32[]{:S(2)}) copy-start(s32[1,4,1,128]{3,2,1,0:T(1,128)} %param.9) | copy-start | bytes 6148
  23.6 23.2 %copy-start.4 = (f32[1,4,1,128]{3,2,1,0:T(1,128)S(1)}, f32[1,4,1,128]{3,2,1,0:T(1,128)}, u32[]{:S(2)}) copy-start(f32[1,4,1,128]{3,2,1,0:T(1,128)} %param.10) | copy-start | bytes 6148
  23.6 23.2 %copy-start.5 = (f32[1,4,1,128]{3,2,1,0:T(1,128)S(1)}, f32[1,4,1,128]{3,2,1,0:T(1,128)}, u32[]{:S(2)}) copy-start(f32[1,4,1,128]{3,2,1,0:T(1,128)} %param.11) | copy-start | bytes 6148

commit v4 on v3

--- a/solution.py
+++ b/solution.py
@@ -152,7 +152,7 @@
 
 
 PAD = 8
-TURNS = 4
+TURNS = 2
 FINEST = 0.05
 LARGEST = 16.0 * sum(1.8**power / math.factorial(power) for power in range(5)) ** STEPS
 STATE_LEVELS = 2047.0
@@ -278,10 +278,14 @@
 
         def turn(index, _):
             base = first + index * block + offset
-            states = [[stage[part, base + k - 1] for k in range(block + 2)] for part in range(4)]
+
+            def load(k):
+                return [stage[part, base + k - 1] for part in range(4)]
+
+            before, here = load(0), load(1)
             for k in range(1, block + 1):
+                after = load(k + 1)
                 place = wind_row(base - offset + k - 1)
-                here = [states[part][k] for part in range(4)]
                 along = (
                     here[1] - pltpu.roll(here[3], 2, 1),
                     here[2] - here[0],
@@ -289,9 +293,10 @@
                     pltpu.roll(here[0], LANES - 2, 1) - here[2],
                 )
                 for part in range(4):
-                    across = states[part][k + 1] - states[part][k - 1]
+                    across = after[part] - before[part]
                     half = w_ref[part, place] * along[part] + w_ref[4 + part, place] * across
                     finish(part, base + k - 1, half)
+                before, here = here, after
             return 0
 
         turns = -(-count // block)
@@ -472,7 +477,7 @@
                 edges_ref[place, 4 * side + part] = values
         return 0
 
-    lax.fori_loop(0, devices, emit, 0)
+    lax.fori_loop(0, devices, emit, 0, unroll=4)
 
 
 def observe_kernel(sizes, edges_ref, coded_ref, table_ref, out_ref):
@@ -526,10 +531,10 @@
     scale_ref,
     out_ref,
     states_ref,
-    upper_ref,
-    upper_low_ref,
-    lower_ref,
-    lower_low_ref,
+    center_ref,
+    high_ref,
+    low_ref,
+    *iterates,
 ):
     rows, members, devices = sizes
     own_rows = rows // devices
@@ -552,7 +557,8 @@
     for j in range(0, own_rows, 2):
         parts = [pair_at((part * own_rows + j) * members) for part in range(4)]
         for k in range(2):
-            states_ref[j + k] = jnp.concatenate([part[k] for part in parts], axis=1)
+            for part in range(4):
+                states_ref[4 * (j + k) + part] = parts[part][k]
             index = jnp.broadcast_to(info(index_ref, j + k), (total, LANES)).astype(jnp.int32)
             picked_rows[j + k + 1] = pick_lanes([part[k] for part in parts], index)
 
@@ -580,9 +586,10 @@
     diagonal = row_ids == column_ids
     identity = jnp.where(diagonal, F32(1.0), F32(0.0))
 
-    def put(high_ref, low_ref, j, value):
-        high_ref[j], low_ref[j] = split_value(value)
-
+    def put(refs, j, value):
+        refs[0][j], refs[1][j] = split_value(value)
+
+    upper_refs, lower_refs = iterates[:2], iterates[2:]
     traces = []
     for j in range(own_rows):
         system = identity + 3.0 * grams[j + 1] + grams[j] + grams[j + 2]
@@ -593,52 +600,70 @@
         )
         traces.append(trace)
         scaled = system / trace
-        factor = split_value(1.5 * identity - 0.5 * scaled)
-        put(upper_ref, upper_low_ref, j, product(split_value(scaled), factor))
-        lower_ref[j], lower_low_ref[j] = factor
+        factor = 1.5 * identity - 0.5 * scaled
+        put(upper_refs, j, product(split_value(scaled), split_value(factor)))
+        put(lower_refs, j, factor)
 
     def factor_of(j):
-        lower = lower_ref[j], lower_low_ref[j]
-        upper = upper_ref[j], upper_low_ref[j]
+        lower, upper = lower_refs, upper_refs
+        lower, upper = (lower[0][j], lower[1][j]), (upper[0][j], upper[1][j])
         return lower, upper, split_value(1.5 * identity - 0.5 * product(lower, upper))
 
+    per_turn = -(-4 * own_rows // (ITERS - 2))
+
     def newton(turn, _):
+        for k in range(per_turn):
+            entry = jnp.minimum(turn * per_turn + k, 4 * own_rows - 1)
+            state = states_ref[entry]
+            center = jnp.mean(state, axis=0, keepdims=True)
+            center_ref[entry] = jnp.broadcast_to(center, (8, LANES))
+            high_ref[entry], low_ref[entry] = split_value(state - center)
         parts = [factor_of(j) for j in range(own_rows)]
         for j in range(own_rows):
             lower, upper, factor = parts[j]
-            put(upper_ref, upper_low_ref, j, product(upper, factor))
-            put(lower_ref, lower_low_ref, j, product(factor, lower))
+            put(upper_refs, j, product(upper, factor))
+            put(lower_refs, j, product(factor, lower))
         return 0
 
     lax.fori_loop(0, ITERS - 2, newton, 0)
 
+    def joined(ref, j):
+        return jnp.concatenate([ref[4 * j + part] for part in range(4)], axis=1)
+
     parts = [factor_of(j) for j in range(own_rows)]
-    weights = []
+    roots = [
+        split_value(product(parts[j][2], parts[j][0]) / jnp.sqrt(traces[j]))
+        for j in range(own_rows)
+    ]
+    half_steps = []
     for j in range(own_rows):
-        lower, upper, factor = parts[j]
-        inv_root = product(factor, lower) / jnp.sqrt(traces[j])
         coupling = 3.0 * couplings[j + 1] + couplings[j] + couplings[j + 2]
-        root_parts = split_value(inv_root)
-        half_step = product(split_value(coupling), root_parts)
-        mean_weight = product(split_value(half_step), root_parts)[:1] / math.sqrt(total - 1)
-        weights.append(split_value(inv_root + mean_weight))
-
+        half_steps.append(product(split_value(coupling), roots[j]))
+    spreads = [
+        jnp.dot(roots[j][0], joined(high_ref, j), preferred_element_type=F32)
+        for j in range(own_rows)
+    ]
+    results = []
+    for j in range(own_rows):
+        mean_weight = product(split_value(half_steps[j]), roots[j]) / math.sqrt(total - 1)
+        high, low = split_value(mean_weight[:8])
+        moved = jnp.dot(
+            jnp.concatenate([high, low], axis=0), joined(high_ref, j), preferred_element_type=F32
+        )
+        rest = jnp.dot(
+            jnp.concatenate([high, low], axis=0), joined(low_ref, j), preferred_element_type=F32
+        )
+        center = joined(center_ref, j)[:1]
+        results.append(spreads[j] + (center + (moved[:1] + moved[8:9]) + rest[:1]))
     for j in range(0, own_rows, 2):
         for part in range(4):
-            place = (part * own_rows + j) * members
-            moved = []
-            for k in range(2):
-                state = states_ref[j + k, :, part * LANES : (part + 1) * LANES]
-                center = jnp.mean(state, axis=0, keepdims=True)
-                high, low = split_value(state - center)
-                weights_high, weights_low = weights[j + k]
-                result = center + (
-                    jnp.dot(weights_high, high, preferred_element_type=F32)
-                    + jnp.dot(weights_high, low, preferred_element_type=F32)
-                    + jnp.dot(weights_low, high, preferred_element_type=F32)
-                )
-                moved.append(result.reshape(devices, members, LANES))
-            out_ref[:, pl.ds(place, pair), :] = jnp.concatenate(moved, axis=1).astype(BF16)
+            both = [
+                results[k][:, part * LANES : (part + 1) * LANES].reshape(devices, members, LANES)
+                for k in (j, j + 1)
+            ]
+            out_ref[:, pl.ds((part * own_rows + j) * members, pair), :] = jnp.concatenate(
+                both, axis=1
+            ).astype(BF16)
 
 
 def unpack_kernel(sizes, got_ref, out_ref):
@@ -766,13 +791,19 @@
         name="observe",
     )(edges, coded, table)
     got = lax.all_to_all(packed, "mem", split_axis=0, concat_axis=0, tiled=True)
-    half_matrix = pltpu.VMEM((own_rows, total, total), BF16)
+    iterate = pltpu.VMEM((own_rows, total, total), BF16)
     back = pl.pallas_call(
         functools.partial(analysis_kernel, sizes),
         out_shape=jax.ShapeDtypeStruct((devices, 4 * own_rows * members, LANES), BF16),
         in_specs=[vmem] * 5,
         out_specs=vmem,
-        scratch_shapes=[pltpu.VMEM((own_rows, total, 4 * LANES), F32)] + [half_matrix] * 4,
+        scratch_shapes=[
+            pltpu.VMEM((4 * own_rows, total, LANES), F32),
+            pltpu.VMEM((4 * own_rows, 8, LANES), F32),
+            pltpu.VMEM((4 * own_rows, total, LANES), BF16),
+            pltpu.VMEM((4 * own_rows, total, LANES), BF16),
+        ]
+        + [iterate] * 4,
         compiler_params=params,
         cost_estimate=cost(12),
         name="analysis",

time: 73.3 us -> 72.6 us (level)
  no operation moved by 1% of the time
where the time goes in v4:
time: 72.6 us; the launch traced here: 72.3 us
  blocking collectives  40.4 us (56%)
  Pallas kernels  22.6 us (31%)
  starting transfers between devices  7.93 us (11%)
  local copies, waits for them, and re-layouts  1.25 us (2%)
    all_to_all x1, blocking collectives, per_device_pair(): got = lax.all_to_all(packed, 'mem', split_axis=0, concat_axis=0, tiled=True)  23.1 us
    all_to_all x1, blocking collectives, per_device_pair(): lax.all_to_all(back, 'mem', split_axis=0, concat_axis=0, tiled=True)  17.3 us
    pallas_call x1, Pallas kernels, per_device_pair(): pl.pallas_call(functools.partial(forecast_kernel, sizes), out_shape=(jax....  10.5 us
    pallas_call x1, Pallas kernels, per_device_pair(): pl.pallas_call(functools.partial(analysis_kernel, sizes), out_shape=jax.S...  7.08 us
    all_to_all x1, starting transfers between devices, per_device_pair(): lax.all_to_all(told, ('lat', 'mem'), split_axis=0, concat_axis=0, tiled=T...  4.89 us
    ppermute x1, starting transfers between devices, per_device_pair(): halo = lax.ppermute(sent, 'lat', [(0, 1), (1, 0)])  3.03 us
    pallas_call x1, Pallas kernels, per_device_pair(): pl.pallas_call(functools.partial(tell_kernel, sizes), out_shape=(jax.Shap...  1.71 us
  transfers between devices with their start and end apart: 2, of which 0 were waited for; matrix products, arithmetic and copies ran while one was open for 0% of the time, Pallas kernels for 16%

profile of v4, /device:TPU:0, one launch (start us, length us, event | category | flops | bytes accessed | tf_op | source)
XLA Modules:
  0.0 72.3 jit_solution(15766518857676254810)
XLA Ops:
  0.0 1.7 %tell.1 = (s16[20,32,128]{2,1,0:T(8,128)(2,1)}, s32[32,4,128]{2,1,0:T(4,128)}) custom-call(f32[64,32,128]{2,1,0:T(8,128)} %bitcast.13, bf16[64,256]{1,0:T(8,128)(2,1)} %east_ref.3, bf16[64,256]{1,0:T(8,128)(2,1)} %north_ref.3, s32[4,128]{1,0:T(4,128)} %bitcast.15, f32[4,128]{1,0:T(4,128)} %bitcast.17, f32[4,128]{1,0:T(4,128)} %bitcast.19), custom_call_target="tpu_custom_call" | custom-call | bytes 3000000 | tf_op jit(solution)/shard_map/tell/pallas_call | solution.py:737
  1.7 3.0 %collective-permute-start = (s16[20,32,128]{2,1,0:T(8,128)(2,1)}, s16[20,32,128]{2,1,0:T(8,128)(2,1)S(1)}, u32[]{:S(2)}, u32[]{:S(2)}) collective-permute-start(s16[20,32,128]{2,1,0:T(8,128)(2,1)} %get-tuple-element.9), channel_id=1, source_target_pairs={{0,1},{1,0},{2,3},{3,2},{4,5},{5,4},{6,7},{7,6},{8,9},{9,8},{10,11... | collective-permute-start | bytes 491528 | tf_op jit(solution)/shard_map/ppermute | solution.py:756
  4.7 4.9 %all-to-all-start = ((s32[32,4,128]{2,1,0:T(4,128)}), s32[32,4,128]{2,1,0:T(4,128)S(1)}, u32[]{:S(2)}, u32[]{:S(2)}) async-start(s32[32,4,128]{2,1,0:T(4,128)} %get-tuple-element.12), calls=%async_computation | async-start | bytes 131072 | tf_op jit(solution)/shard_map/all_to_all | solution.py:757
  9.6 0.0 copy-start
  9.7 1.2 %copy-done = f32[64,8,2,256]{3,2,1,0:T(2,128)S(1)} copy-done((f32[64,8,2,256]{3,2,1,0:T(2,128)S(1)}, f32[64,8,2,256]{3,2,1,0:T(2,128)}, u32[]{:S(2)}) %copy-start) | copy-done | bytes 1048600
  10.9 0.0 copy-start.1
  10.9 0.0 copy-start.2
  10.9 1.3 %stage.1.own_ref = f32[4,64,8,128]{3,2,1,0:T(8,128)S(1)} custom-call(f32[64,32,128]{2,1,0:T(8,128)S(1)} %bitcast.14), custom_call_target="tpu_custom_call" | custom-call | bytes 6000000 | tf_op jit(solution)/shard_map/stage/pallas_call | solution.py:758
  12.2 0.0 collective-permute-done.halo_ref
  12.2 0.0 copy-done.1
  12.2 0.0 copy-done.2
  12.2 10.5 %forecast.1 = (s16[16,128,128]{2,1,0:T(8,128)(2,1)S(1)}, f32[16,8,8,128]{3,2,1,0:T(8,128)S(1)}) custom-call(f32[4,64,8,128]{3,2,1,0:T(8,128)S(1)} %stage.1.own_ref, s16[20,32,128]{2,1,0:T(8,128)(2,1)S(1)} %collective-permute-done.halo_ref, bf16[64,256]{1,0:T(8,128)(2,1)S(1)} %copy-done.1, bf16[64,256]{1,0:T(8,128)(2,1)S(1)} %copy-done.2), custom_call_target="tpu_custom_call" | custom-call | bytes 36000000 | tf_op jit(solution)/shard_map/forecast/pallas_call | solution.py:771
  22.7 0.0 all-to-all-done.table_ref
  22.7 0.6 observe.1
  23.3 0.0 copy-start.3
  23.3 0.0 copy-start.4
  23.3 0.0 copy-start.5
  23.3 23.1 %all_to_all.15.got_ref = s16[16,144,128]{2,1,0:T(8,128)(2,1)S(1)} all-to-all(s16[16,144,128]{2,1,0:T(8,128)(2,1)S(1)} %observe.1), channel_id=1, replica_groups=mesh['mem'=16,'lat'=2] {'mem'}, dimensions={0} | all-to-all | bytes 1179648 | tf_op jit(solution)/shard_map/all_to_all | solution.py:793
  46.5 0.0 copy-done.3
  46.5 0.0 copy-done.4
  46.5 0.0 copy-done.5
  46.5 7.1 %analysis.1 = bf16[16,128,128]{2,1,0:T(8,128)(2,1)S(1)} custom-call(s16[16,144,128]{2,1,0:T(8,128)(2,1)S(1)} %all_to_all.15.got_ref, s32[32,4,128]{2,1,0:T(4,128)S(1)} %all-to-all-done.table_ref, s32[4,128]{1,0:T(4,128)S(1)} %bitcast.16, f32[4,128]{1,0:T(4,128)S(1)} %bitcast.18, f32[4,128]{1,0:T(4,128)S(1)} %bitcast.20), custom_call_target="tpu_custom_call" | custom-call | bytes 36000000 | tf_op jit(solution)/shard_map/analysis/pallas_call | solution.py:795
  53.6 17.3 %all_to_all.16.got_ref = bf16[16,128,128]{2,1,0:T(8,128)(2,1)S(1)} all-to-all(bf16[16,128,128]{2,1,0:T(8,128)(2,1)S(1)} %analysis.1), channel_id=1, replica_groups=mesh['mem'=16,'lat'=2] {'mem'}, dimensions={0} | all-to-all | bytes 1048576 | tf_op jit(solution)/shard_map/all_to_all | solution.py:811
  70.8 1.4 %unpack.1 = f32[64,32,128]{2,1,0:T(8,128)} custom-call(bf16[16,128,128]{2,1,0:T(8,128)(2,1)S(1)} %all_to_all.16.got_ref), custom_call_target="tpu_custom_call" | custom-call | bytes 6000000 | tf_op jit(solution)/shard_map/unpack/pallas_call | solution.py:812
Async XLA Ops:
  1.7 10.5 %collective-permute-start = (s16[20,32,128]{2,1,0:T(8,128)(2,1)}, s16[20,32,128]{2,1,0:T(8,128)(2,1)S(1)}, u32[]{:S(2)}, u32[]{:S(2)}) collective-permute-start(s16[20,32,128]{2,1,0:T(8,128)(2,1)} %get-tuple-element.9), channel_id=1, source_target_pairs={{0,1},{1,0},{2,3},{3,2},{4,5},{5,4},{6,7},{7,6},{8,9},{9,8},{10,11... | collective-permute-start | bytes 491528 | tf_op jit(solution)/shard_map/ppermute | solution.py:756
  4.7 17.9 %all-to-all-start = ((s32[32,4,128]{2,1,0:T(4,128)}), s32[32,4,128]{2,1,0:T(4,128)S(1)}, u32[]{:S(2)}, u32[]{:S(2)}) async-start(s32[32,4,128]{2,1,0:T(4,128)} %get-tuple-element.12), calls=%async_computation | async-start | bytes 131072 | tf_op jit(solution)/shard_map/all_to_all | solution.py:757
  9.6 1.2 %copy-start = (f32[64,8,2,256]{3,2,1,0:T(2,128)S(1)}, f32[64,8,2,256]{3,2,1,0:T(2,128)}, u32[]{:S(2)}) copy-start(f32[64,8,2,256]{3,2,1,0:T(2,128)} %param.6) | copy-start | bytes 3145732
  10.9 1.3 %copy-start.1 = (bf16[64,256]{1,0:T(8,128)(2,1)S(1)}, bf16[64,256]{1,0:T(8,128)(2,1)}, u32[]{:S(2)}) copy-start(bf16[64,256]{1,0:T(8,128)(2,1)} %east_ref.3) | copy-start | bytes 98308
  10.9 1.3 %copy-start.2 = (bf16[64,256]{1,0:T(8,128)(2,1)S(1)}, bf16[64,256]{1,0:T(8,128)(2,1)}, u32[]{:S(2)}) copy-start(bf16[64,256]{1,0:T(8,128)(2,1)} %north_ref.3) | copy-start | bytes 98308
  23.3 23.2 %copy-start.3 = (s32[1,4,1,128]{3,2,1,0:T(1,128)S(1)}, s32[1,4,1,128]{3,2,1,0:T(1,128)}, u32[]{:S(2)}) copy-start(s32[1,4,1,128]{3,2,1,0:T(1,128)} %param.9) | copy-start | bytes 6148
  23.3 23.2 %copy-start.4 = (f32[1,4,1,128]{3,2,1,0:T(1,128)S(1)}, f32[1,4,1,128]{3,2,1,0:T(1,128)}, u32[]{:S(2)}) copy-start(f32[1,4,1,128]{3,2,1,0:T(1,128)} %param.10) | copy-start | bytes 6148
  23.3 23.2 %copy-start.5 = (f32[1,4,1,128]{3,2,1,0:T(1,128)S(1)}, f32[1,4,1,128]{3,2,1,0:T(1,128)}, u32[]{:S(2)}) copy-start(f32[1,4,1,128]{3,2,1,0:T(1,128)} %param.11) | copy-start | bytes 6148

commit v5 on v4

--- a/solution.py
+++ b/solution.py
@@ -241,18 +241,18 @@
         q_ref[part, pl.ds(start, count)] = values.reshape(count, members, LANES)
 
 
-def stage_winds(east, north, north_sign, matrix, w_ref, start):
-    count = east.shape[0]
+def stage_winds(east, north, north_sign, matrix, w_ref, row_of):
+    count, members = east.shape[0], w_ref.shape[2]
     for side, (wind, sign) in enumerate(((east, F32(-0.25)), (north, north_sign))):
         both = jnp.concatenate([wind, wind], axis=1)
         split = jnp.dot(both, matrix, preferred_element_type=F32) * sign
-        for part in range(4):
-            lanes = split[:, part * LANES : (part + 1) * LANES]
-            wide = jnp.broadcast_to(lanes[:, None, :], (count, w_ref.shape[2], LANES))
-            w_ref[4 * side + part, pl.ds(start, count)] = wide
-
-
-def rk_passes(q_ref, stage_refs, offset, w_ref, wind_row, first, count, block):
+        for k in range(count):
+            for part in range(4):
+                lanes = split[k : k + 1, part * LANES : (part + 1) * LANES]
+                w_ref[4 * side + part, row_of(k)] = jnp.broadcast_to(lanes, (members, LANES))
+
+
+def rk_passes(q_ref, stage_refs, w_ref, count, block):
     a_ref, b_ref, c_ref = stage_refs
 
     def finish_one(part, at, half):
@@ -277,7 +277,7 @@
     ):
 
         def turn(index, _):
-            base = first + index * block + offset
+            base = PAD + index * block
 
             def load(k):
                 return [stage[part, base + k - 1] for part in range(4)]
@@ -285,7 +285,7 @@
             before, here = load(0), load(1)
             for k in range(1, block + 1):
                 after = load(k + 1)
-                place = wind_row(base - offset + k - 1)
+                place = index * block + k - 1
                 along = (
                     here[1] - pltpu.roll(here[3], 2, 1),
                     here[2] - here[0],
@@ -426,7 +426,7 @@
         north_sign,
         matrix,
         w_ref,
-        jnp.where(band == 0, 0, wind_halo),
+        lambda k: jnp.where(band == 0, k, rows - 1 - k),
     )
     edge_ref[...] = halo_ref[:HALO].astype(jnp.int32).astype(F32) * F32(1.0 / STATE_LEVELS)
     halo_winds = halo_ref[HALO:].astype(jnp.int32).astype(F32).reshape(4 * wind_halo, LANES)
@@ -438,7 +438,7 @@
         north_sign,
         matrix,
         w_ref,
-        jnp.where(band == 0, rows, 0),
+        lambda k: rows + jnp.where(band == 0, k, wind_halo - 1 - k),
     )
 
     q_ref[:, PAD : PAD + rows] = own_ref[...]
@@ -452,12 +452,9 @@
 
     stage_states(load, row_of, wind_halo, members, matrix, q_ref, PAD + rows)
 
-    def wind_row(row):
-        return jnp.where(band == 0, row, rows + wind_halo - 1 - row)
-
     for step in range(STEPS):
         count = rows + HALO - 1 - 4 * step
-        rk_passes(q_ref, stage_refs, PAD, w_ref, wind_row, 0, count, -(-count // TURNS))
+        rk_passes(q_ref, stage_refs, w_ref, count, -(-count // TURNS))
 
     def state(row):
         return [q_ref[part, PAD + row] for part in range(4)]

time: 72.6 us -> 70 us (0.964)
  Pallas kernels: 22.6 us -> 20.1 us
    pallas_call x1, Pallas kernels: 10.5 us -> 7.92 us  [per_device_pair(): pl.pallas_call(functools.partial(forecast_kernel, sizes), out_shape=(jax....]
  transfers between devices with their start and end apart: 2 -> 2, of which waited for: 0 -> 0; matrix products, arithmetic and copies ran while one was open for 0% -> 0% of each run, Pallas kernels for 16% -> 13%
where the time goes in v5:
time: 70 us; the launch traced here: 69.7 us
  blocking collectives  40.4 us (58%)
  Pallas kernels  20.1 us (29%)
  starting transfers between devices  7.93 us (11%)
  local copies, waits for them, and re-layouts  1.25 us (2%)
    all_to_all x1, blocking collectives, per_device_pair(): got = lax.all_to_all(packed, 'mem', split_axis=0, concat_axis=0, tiled=True)  23.1 us
    all_to_all x1, blocking collectives, per_device_pair(): lax.all_to_all(back, 'mem', split_axis=0, concat_axis=0, tiled=True)  17.3 us
    pallas_call x1, Pallas kernels, per_device_pair(): pl.pallas_call(functools.partial(forecast_kernel, sizes), out_shape=(jax....  7.92 us
    pallas_call x1, Pallas kernels, per_device_pair(): pl.pallas_call(functools.partial(analysis_kernel, sizes), out_shape=jax.S...  7.08 us
    all_to_all x1, starting transfers between devices, per_device_pair(): lax.all_to_all(told, ('lat', 'mem'), split_axis=0, concat_axis=0, tiled=T...  4.89 us
    ppermute x1, starting transfers between devices, per_device_pair(): halo = lax.ppermute(sent, 'lat', [(0, 1), (1, 0)])  3.03 us
    pallas_call x1, Pallas kernels, per_device_pair(): pl.pallas_call(functools.partial(tell_kernel, sizes), out_shape=(jax.Shap...  1.71 us
    pallas_call x1, Pallas kernels, per_device_pair(): pl.pallas_call(functools.partial(unpack_kernel, sizes), out_shape=jax.Sha...  1.44 us
  transfers between devices with their start and end apart: 2, of which 0 were waited for; matrix products, arithmetic and copies ran while one was open for 0% of the time, Pallas kernels for 13%

profile of v5, /device:TPU:0, one launch (start us, length us, event | category | flops | bytes accessed | tf_op | source)
XLA Modules:
  0.0 69.7 jit_solution(17567964415594269110)
XLA Ops:
  0.0 1.7 %tell.1 = (s16[20,32,128]{2,1,0:T(8,128)(2,1)}, s32[32,4,128]{2,1,0:T(4,128)}) custom-call(f32[64,32,128]{2,1,0:T(8,128)} %bitcast.13, bf16[64,256]{1,0:T(8,128)(2,1)} %east_ref.3, bf16[64,256]{1,0:T(8,128)(2,1)} %north_ref.3, s32[4,128]{1,0:T(4,128)} %bitcast.15, f32[4,128]{1,0:T(4,128)} %bitcast.17, f32[4,128]{1,0:T(4,128)} %bitcast.19), custom_call_target="tpu_custom_call" | custom-call | bytes 3000000 | tf_op jit(solution)/shard_map/tell/pallas_call | solution.py:734
  1.7 3.0 %collective-permute-start = (s16[20,32,128]{2,1,0:T(8,128)(2,1)}, s16[20,32,128]{2,1,0:T(8,128)(2,1)S(1)}, u32[]{:S(2)}, u32[]{:S(2)}) collective-permute-start(s16[20,32,128]{2,1,0:T(8,128)(2,1)} %get-tuple-element.9), channel_id=1, source_target_pairs={{0,1},{1,0},{2,3},{3,2},{4,5},{5,4},{6,7},{7,6},{8,9},{9,8},{10,11... | collective-permute-start | bytes 491528 | tf_op jit(solution)/shard_map/ppermute | solution.py:753
  4.7 4.9 %all-to-all-start = ((s32[32,4,128]{2,1,0:T(4,128)}), s32[32,4,128]{2,1,0:T(4,128)S(1)}, u32[]{:S(2)}, u32[]{:S(2)}) async-start(s32[32,4,128]{2,1,0:T(4,128)} %get-tuple-element.12), calls=%async_computation | async-start | bytes 131072 | tf_op jit(solution)/shard_map/all_to_all | solution.py:754
  9.6 0.0 copy-start
  9.7 1.2 %copy-done = f32[64,8,2,256]{3,2,1,0:T(2,128)S(1)} copy-done((f32[64,8,2,256]{3,2,1,0:T(2,128)S(1)}, f32[64,8,2,256]{3,2,1,0:T(2,128)}, u32[]{:S(2)}) %copy-start) | copy-done | bytes 1048600
  10.9 0.0 copy-start.1
  10.9 0.0 copy-start.2
  10.9 1.3 %stage.1.own_ref = f32[4,64,8,128]{3,2,1,0:T(8,128)S(1)} custom-call(f32[64,32,128]{2,1,0:T(8,128)S(1)} %bitcast.14), custom_call_target="tpu_custom_call" | custom-call | bytes 6000000 | tf_op jit(solution)/shard_map/stage/pallas_call | solution.py:755
  12.2 0.0 collective-permute-done.halo_ref
  12.2 0.0 copy-done.1
  12.2 0.0 copy-done.2
  12.2 7.9 %forecast.1 = (s16[16,128,128]{2,1,0:T(8,128)(2,1)S(1)}, f32[16,8,8,128]{3,2,1,0:T(8,128)S(1)}) custom-call(f32[4,64,8,128]{3,2,1,0:T(8,128)S(1)} %stage.1.own_ref, s16[20,32,128]{2,1,0:T(8,128)(2,1)S(1)} %collective-permute-done.halo_ref, bf16[64,256]{1,0:T(8,128)(2,1)S(1)} %copy-done.1, bf16[64,256]{1,0:T(8,128)(2,1)S(1)} %copy-done.2), custom_call_target="tpu_custom_call" | custom-call | bytes 36000000 | tf_op jit(solution)/shard_map/forecast/pallas_call | solution.py:768
  20.1 0.0 all-to-all-done.table_ref
  20.1 0.6 observe.1
  20.8 0.0 copy-start.3
  20.8 0.0 copy-start.4
  20.8 0.0 copy-start.5
  20.8 23.1 %all_to_all.15.got_ref = s16[16,144,128]{2,1,0:T(8,128)(2,1)S(1)} all-to-all(s16[16,144,128]{2,1,0:T(8,128)(2,1)S(1)} %observe.1), channel_id=1, replica_groups=mesh['mem'=16,'lat'=2] {'mem'}, dimensions={0} | all-to-all | bytes 1179648 | tf_op jit(solution)/shard_map/all_to_all | solution.py:790
  43.9 0.0 copy-done.3
  43.9 0.0 copy-done.4
  44.0 0.0 copy-done.5
  44.0 7.1 %analysis.1 = bf16[16,128,128]{2,1,0:T(8,128)(2,1)S(1)} custom-call(s16[16,144,128]{2,1,0:T(8,128)(2,1)S(1)} %all_to_all.15.got_ref, s32[32,4,128]{2,1,0:T(4,128)S(1)} %all-to-all-done.table_ref, s32[4,128]{1,0:T(4,128)S(1)} %bitcast.16, f32[4,128]{1,0:T(4,128)S(1)} %bitcast.18, f32[4,128]{1,0:T(4,128)S(1)} %bitcast.20), custom_call_target="tpu_custom_call" | custom-call | bytes 36000000 | tf_op jit(solution)/shard_map/analysis/pallas_call | solution.py:792
  51.0 17.3 %all_to_all.16.got_ref = bf16[16,128,128]{2,1,0:T(8,128)(2,1)S(1)} all-to-all(bf16[16,128,128]{2,1,0:T(8,128)(2,1)S(1)} %analysis.1), channel_id=1, replica_groups=mesh['mem'=16,'lat'=2] {'mem'}, dimensions={0} | all-to-all | bytes 1048576 | tf_op jit(solution)/shard_map/all_to_all | solution.py:808
  68.3 1.4 %unpack.1 = f32[64,32,128]{2,1,0:T(8,128)} custom-call(bf16[16,128,128]{2,1,0:T(8,128)(2,1)S(1)} %all_to_all.16.got_ref), custom_call_target="tpu_custom_call" | custom-call | bytes 6000000 | tf_op jit(solution)/shard_map/unpack/pallas_call | solution.py:809
Async XLA Ops:
  1.7 10.5 %collective-permute-start = (s16[20,32,128]{2,1,0:T(8,128)(2,1)}, s16[20,32,128]{2,1,0:T(8,128)(2,1)S(1)}, u32[]{:S(2)}, u32[]{:S(2)}) collective-permute-start(s16[20,32,128]{2,1,0:T(8,128)(2,1)} %get-tuple-element.9), channel_id=1, source_target_pairs={{0,1},{1,0},{2,3},{3,2},{4,5},{5,4},{6,7},{7,6},{8,9},{9,8},{10,11... | collective-permute-start | bytes 491528 | tf_op jit(solution)/shard_map/ppermute | solution.py:753
  4.7 15.4 %all-to-all-start = ((s32[32,4,128]{2,1,0:T(4,128)}), s32[32,4,128]{2,1,0:T(4,128)S(1)}, u32[]{:S(2)}, u32[]{:S(2)}) async-start(s32[32,4,128]{2,1,0:T(4,128)} %get-tuple-element.12), calls=%async_computation | async-start | bytes 131072 | tf_op jit(solution)/shard_map/all_to_all | solution.py:754
  9.6 1.2 %copy-start = (f32[64,8,2,256]{3,2,1,0:T(2,128)S(1)}, f32[64,8,2,256]{3,2,1,0:T(2,128)}, u32[]{:S(2)}) copy-start(f32[64,8,2,256]{3,2,1,0:T(2,128)} %param.6) | copy-start | bytes 3145732
  10.9 1.3 %copy-start.1 = (bf16[64,256]{1,0:T(8,128)(2,1)S(1)}, bf16[64,256]{1,0:T(8,128)(2,1)}, u32[]{:S(2)}) copy-start(bf16[64,256]{1,0:T(8,128)(2,1)} %east_ref.3) | copy-start | bytes 98308
  10.9 1.3 %copy-start.2 = (bf16[64,256]{1,0:T(8,128)(2,1)S(1)}, bf16[64,256]{1,0:T(8,128)(2,1)}, u32[]{:S(2)}) copy-start(bf16[64,256]{1,0:T(8,128)(2,1)} %north_ref.3) | copy-start | bytes 98308
  20.8 23.2 %copy-start.3 = (s32[1,4,1,128]{3,2,1,0:T(1,128)S(1)}, s32[1,4,1,128]{3,2,1,0:T(1,128)}, u32[]{:S(2)}) copy-start(s32[1,4,1,128]{3,2,1,0:T(1,128)} %param.9) | copy-start | bytes 6148
  20.8 23.2 %copy-start.4 = (f32[1,4,1,128]{3,2,1,0:T(1,128)S(1)}, f32[1,4,1,128]{3,2,1,0:T(1,128)}, u32[]{:S(2)}) copy-start(f32[1,4,1,128]{3,2,1,0:T(1,128)} %param.10) | copy-start | bytes 6148
  20.8 23.2 %copy-start.5 = (f32[1,4,1,128]{3,2,1,0:T(1,128)S(1)}, f32[1,4,1,128]{3,2,1,0:T(1,128)}, u32[]{:S(2)}) copy-start(f32[1,4,1,128]{3,2,1,0:T(1,128)} %param.11) | copy-start | bytes 6148

commit v6 on v5

--- a/solution.py
+++ b/solution.py
@@ -255,19 +255,19 @@
 def rk_passes(q_ref, stage_refs, w_ref, count, block):
     a_ref, b_ref, c_ref = stage_refs
 
-    def finish_one(part, at, half):
-        a_ref[part, at] = q_ref[part, at] + half
-
-    def finish_two(part, at, half):
+    def finish_one(part, at, half, here):
+        a_ref[part, at] = here + half
+
+    def finish_two(part, at, half, here):
         b_ref[part, at] = q_ref[part, at] + half
 
-    def finish_three(part, at, half):
-        c_ref[part, at] = q_ref[part, at] + (half + half)
-
-    def finish_four(part, at, half):
-        doubled = b_ref[part, at]
-        gathered = (a_ref[part, at] + c_ref[part, at] - q_ref[part, at]) + (doubled + doubled)
-        q_ref[part, at] = (gathered + half) * F32(1.0 / 3.0)
+    def finish_three(part, at, half, here):
+        moved = half + half
+        c_ref[part, at] = q_ref[part, at] + moved
+        a_ref[part, at] = (a_ref[part, at] + moved) + (here + here)
+
+    def finish_four(part, at, half, here):
+        q_ref[part, at] = (a_ref[part, at] + half) * F32(1.0 / 3.0)
 
     for stage, finish in (
         (q_ref, finish_one),
@@ -295,7 +295,7 @@
                 for part in range(4):
                     across = after[part] - before[part]
                     half = w_ref[part, place] * along[part] + w_ref[4 + part, place] * across
-                    finish(part, base + k - 1, half)
+                    finish(part, base + k - 1, half, here[part])
                 before, here = here, after
             return 0
 
@@ -375,27 +375,6 @@
     sent_ref[:HALO] = edge.astype(jnp.int32).astype(jnp.int16)
 
 
-def stage_kernel(sizes, own_ref, parts_ref):
-    rows, members, devices = sizes
-    band = lax.axis_index("lat")
-    matrix = parts_matrix()
-    block = 4 * CHUNK
-
-    def stage(index, _):
-        base = index * block
-
-        def row_of(k):
-            return jnp.where(band == 0, base + k, rows - 1 - base - k)
-
-        def load(row, lane):
-            return own_ref[row, pl.ds(lane, members, stride=4), :]
-
-        stage_states(load, row_of, block, members, matrix, parts_ref, base)
-        return 0
-
-    lax.fori_loop(0, rows // block, stage, 0)
-
-
 def forecast_kernel(
     sizes,
     own_ref,
@@ -441,8 +420,6 @@
         lambda k: rows + jnp.where(band == 0, k, wind_halo - 1 - k),
     )
 
-    q_ref[:, PAD : PAD + rows] = own_ref[...]
-
     def row_of(k):
         row = min(k, HALO - 1)
         return jnp.where(band == 0, row, HALO - 1 - row)
@@ -451,6 +428,22 @@
         return edge_ref[row, pl.ds(lane, members, stride=4), :]
 
     stage_states(load, row_of, wind_halo, members, matrix, q_ref, PAD + rows)
+
+    def load_own(row, lane):
+        return own_ref[row, pl.ds(lane, members, stride=4), :]
+
+    block = 4 * CHUNK
+    for start in range(0, rows, block):
+        place = PAD + jnp.where(band == 0, start, rows - block - start)
+        stage_states(
+            load_own,
+            lambda k: start + jnp.where(band == 0, k, block - 1 - k),
+            block,
+            members,
+            matrix,
+            q_ref,
+            place,
+        )
 
     for step in range(STEPS):
         count = rows + HALO - 1 - 4 * step
@@ -622,7 +615,7 @@
             put(lower_refs, j, product(factor, lower))
         return 0
 
-    lax.fori_loop(0, ITERS - 2, newton, 0)
+    lax.fori_loop(0, ITERS - 2, newton, 0, unroll=2)
 
     def joined(ref, j):
         return jnp.concatenate([ref[4 * j + part] for part in range(4)], axis=1)
@@ -663,45 +656,45 @@
             ).astype(BF16)
 
 
-def unpack_kernel(sizes, got_ref, out_ref):
+def unpack_kernel(sizes, got_ref, out_ref, rows_ref, copied):
     rows, members, devices = sizes
     own_rows = rows // devices
     band = lax.axis_index("lat")
     matrix = parts_matrix(from_parts=True)
-
-    batch = devices
-
-    def place(index, _):
-        device = index * batch
+    share = devices // 2
+    copies = []
+    for start in range(0, devices, share):
         parts = jnp.concatenate(
             [
-                jnp.concatenate(
-                    [
-                        got_ref[device + d, pl.ds(part * own_rows * members, own_rows * members), :]
-                        for d in range(batch)
-                    ],
-                    axis=0,
-                )
+                got_ref[
+                    start : start + share,
+                    part * own_rows * members : (part + 1) * own_rows * members,
+                ].reshape(share * own_rows * members, LANES)
                 for part in range(4)
             ],
             axis=1,
         )
         joined = jnp.dot(parts, matrix, preferred_element_type=F32)
-        for k in range(batch * own_rows):
-            row = device * own_rows + k
-            if own_rows > 1:
-                flipped = (device + k // own_rows) * own_rows + own_rows - 1 - k % own_rows
-                row = jnp.where(band == 0, row, flipped)
+        for k in range(share * own_rows):
+            row = start * own_rows + k
+            flipped = (start + k // own_rows) * own_rows + own_rows - 1 - k % own_rows
+            row = jnp.where(band == 0, row, flipped)
             values = joined[k * members : (k + 1) * members]
             for field in range(2):
                 for half in range(2):
                     first = (2 * field + half) * LANES
-                    out_ref[row, pl.ds(2 * half + field, members, stride=4), :] = values[
+                    rows_ref[row, pl.ds(2 * half + field, members, stride=4), :] = values[
                         :, first : first + LANES
                     ]
-        return 0
-
-    lax.fori_loop(0, devices // batch, place, 0)
+        part_rows = pl.ds(start * own_rows, share * own_rows)
+        copies.append(
+            pltpu.make_async_copy(
+                rows_ref.at[part_rows], out_ref.at[part_rows], copied.at[start // share]
+            )
+        )
+        copies[-1].start()
+    for copy in copies:
+        copy.wait()
 
 
 def per_device_pair(background, wind_east, wind_north, obs_index, obs_value, obs_scale):
@@ -752,16 +745,6 @@
     )(own, wind_east, wind_north, *observations)
     halo = lax.ppermute(sent, "lat", [(0, 1), (1, 0)])
     table = lax.all_to_all(told, ("lat", "mem"), split_axis=0, concat_axis=0, tiled=True)
-    staged = pl.pallas_call(
-        functools.partial(stage_kernel, sizes),
-        out_shape=jax.ShapeDtypeStruct((4, rows, members, LANES), F32),
-        in_specs=[vmem],
-        out_specs=vmem,
-        compiler_params=params,
-        cost_estimate=cost(2),
-        name="stage",
-    )(own)
-
     per_target = (4 * own_rows + 2) * members
     wind_rows = pltpu.VMEM((8, rows + wind_halo, members, LANES), F32)
     field_rows = pltpu.VMEM((4, PAD + rows + wind_halo, members, LANES), F32)
@@ -777,7 +760,7 @@
         compiler_params=params,
         cost_estimate=cost(12),
         name="forecast",
-    )(staged, halo, wind_east, wind_north)
+    )(own, halo, wind_east, wind_north)
     packed = pl.pallas_call(
         functools.partial(observe_kernel, sizes),
         out_shape=jax.ShapeDtypeStruct((devices, per_target, LANES), jnp.int16),
@@ -810,7 +793,8 @@
         functools.partial(unpack_kernel, sizes),
         out_shape=jax.ShapeDtypeStruct((rows, grouped, LANES), F32),
         in_specs=[vmem],
-        out_specs=vmem,
+        out_specs=hbm,
+        scratch_shapes=[pltpu.VMEM((rows, grouped, LANES), F32), dma((2,))],
         compiler_params=params,
         cost_estimate=cost(2),
         name="unpack",

time: 70 us -> 68.8 us (0.983)
  Pallas kernels: 20.1 us -> 18.8 us
    pallas_call x1 -> x0, Pallas kernels: 1.28 us -> none  [per_device_pair(): pl.pallas_call(functools.partial(stage_kernel, sizes), out_shape=jax.Shap...]
  transfers between devices with their start and end apart: 2 -> 2, of which waited for: 0 -> 0; matrix products, arithmetic and copies ran while one was open for 0% -> 0% of each run, Pallas kernels for 13% -> 12%
where the time goes in v6:
time: 68.8 us; the launch traced here: 68.5 us
  blocking collectives  40.4 us (59%)
  Pallas kernels  18.8 us (27%)
  starting transfers between devices  7.93 us (12%)
  local copies, waits for them, and re-layouts  1.25 us (2%)
    all_to_all x1, blocking collectives, per_device_pair(): got = lax.all_to_all(packed, 'mem', split_axis=0, concat_axis=0, tiled=True)  23.1 us
    all_to_all x1, blocking collectives, per_device_pair(): lax.all_to_all(back, 'mem', split_axis=0, concat_axis=0, tiled=True)  17.3 us
    pallas_call x1, Pallas kernels, per_device_pair(): pl.pallas_call(functools.partial(forecast_kernel, sizes), out_shape=(jax....  8.36 us
    pallas_call x1, Pallas kernels, per_device_pair(): pl.pallas_call(functools.partial(analysis_kernel, sizes), out_shape=jax.S...  6.73 us
    all_to_all x1, starting transfers between devices, per_device_pair(): lax.all_to_all(told, ('lat', 'mem'), split_axis=0, concat_axis=0, tiled=T...  4.89 us
    ppermute x1, starting transfers between devices, per_device_pair(): halo = lax.ppermute(sent, 'lat', [(0, 1), (1, 0)])  3.03 us
    pallas_call x1, Pallas kernels, per_device_pair(): pl.pallas_call(functools.partial(tell_kernel, sizes), out_shape=(jax.Shap...  1.71 us
    pallas_call x1, Pallas kernels, per_device_pair(): pl.pallas_call(functools.partial(unpack_kernel, sizes), out_shape=jax.Sha...  1.38 us
  transfers between devices with their start and end apart: 2, of which 0 were waited for; matrix products, arithmetic and copies ran while one was open for 0% of the time, Pallas kernels for 12%

profile of v6, /device:TPU:0, one launch (start us, length us, event | category | flops | bytes accessed | tf_op | source)
XLA Modules:
  0.0 68.5 jit_solution(6919917224398545516)
XLA Ops:
  0.0 1.7 %tell.1 = (s16[20,32,128]{2,1,0:T(8,128)(2,1)}, s32[32,4,128]{2,1,0:T(4,128)}) custom-call(f32[64,32,128]{2,1,0:T(8,128)} %bitcast.13, bf16[64,256]{1,0:T(8,128)(2,1)} %east_ref.3, bf16[64,256]{1,0:T(8,128)(2,1)} %north_ref.3, s32[4,128]{1,0:T(4,128)} %bitcast.15, f32[4,128]{1,0:T(4,128)} %bitcast.17, f32[4,128]{1,0:T(4,128)} %bitcast.19), custom_call_target="tpu_custom_call" | custom-call | bytes 3000000 | tf_op jit(solution)/shard_map/tell/pallas_call | solution.py:727
  1.7 3.0 %collective-permute-start = (s16[20,32,128]{2,1,0:T(8,128)(2,1)}, s16[20,32,128]{2,1,0:T(8,128)(2,1)S(1)}, u32[]{:S(2)}, u32[]{:S(2)}) collective-permute-start(s16[20,32,128]{2,1,0:T(8,128)(2,1)} %get-tuple-element.9), channel_id=1, source_target_pairs={{0,1},{1,0},{2,3},{3,2},{4,5},{5,4},{6,7},{7,6},{8,9},{9,8},{10,11... | collective-permute-start | bytes 491528 | tf_op jit(solution)/shard_map/ppermute | solution.py:746
  4.7 0.0 copy-start.1
  4.7 0.0 copy-start.2
  4.8 4.9 %all-to-all-start = ((s32[32,4,128]{2,1,0:T(4,128)}), s32[32,4,128]{2,1,0:T(4,128)S(1)}, u32[]{:S(2)}, u32[]{:S(2)}) async-start(s32[32,4,128]{2,1,0:T(4,128)} %get-tuple-element.12), calls=%async_computation | async-start | bytes 131072 | tf_op jit(solution)/shard_map/all_to_all | solution.py:747
  9.7 0.0 collective-permute-done.halo_ref
  9.7 0.0 copy-done.1
  9.7 0.0 copy-done.2
  9.7 0.0 copy-start
  9.7 1.2 %copy-done = f32[64,8,2,256]{3,2,1,0:T(2,128)S(1)} copy-done((f32[64,8,2,256]{3,2,1,0:T(2,128)S(1)}, f32[64,8,2,256]{3,2,1,0:T(2,128)}, u32[]{:S(2)}) %copy-start) | copy-done | bytes 1048600
  10.9 8.4 %forecast.1 = (s16[16,128,128]{2,1,0:T(8,128)(2,1)S(1)}, f32[16,8,8,128]{3,2,1,0:T(8,128)S(1)}) custom-call(f32[64,32,128]{2,1,0:T(8,128)S(1)} %bitcast.14, s16[20,32,128]{2,1,0:T(8,128)(2,1)S(1)} %collective-permute-done.halo_ref, bf16[64,256]{1,0:T(8,128)(2,1)S(1)} %copy-done.1, bf16[64,256]{1,0:T(8,128)(2,1)S(1)} %copy-done.2), custom_call_target="tpu_custom_call" | custom-call | bytes 36000000 | tf_op jit(solution)/shard_map/forecast/pallas_call | solution.py:751
  19.3 0.0 all-to-all-done.table_ref
  19.3 0.6 observe.1
  19.9 0.0 copy-start.3
  19.9 0.0 copy-start.4
  20.0 0.0 copy-start.5
  20.0 23.1 %all_to_all.15.got_ref = s16[16,144,128]{2,1,0:T(8,128)(2,1)S(1)} all-to-all(s16[16,144,128]{2,1,0:T(8,128)(2,1)S(1)} %observe.1), channel_id=1, replica_groups=mesh['mem'=16,'lat'=2] {'mem'}, dimensions={0} | all-to-all | bytes 1179648 | tf_op jit(solution)/shard_map/all_to_all | solution.py:773
  43.1 0.0 copy-done.3
  43.1 0.0 copy-done.4
  43.1 0.0 copy-done.5
  43.1 6.7 %analysis.1 = bf16[16,128,128]{2,1,0:T(8,128)(2,1)S(1)} custom-call(s16[16,144,128]{2,1,0:T(8,128)(2,1)S(1)} %all_to_all.15.got_ref, s32[32,4,128]{2,1,0:T(4,128)S(1)} %all-to-all-done.table_ref, s32[4,128]{1,0:T(4,128)S(1)} %bitcast.16, f32[4,128]{1,0:T(4,128)S(1)} %bitcast.18, f32[4,128]{1,0:T(4,128)S(1)} %bitcast.20), custom_call_target="tpu_custom_call" | custom-call | bytes 36000000 | tf_op jit(solution)/shard_map/analysis/pallas_call | solution.py:775
  49.8 17.3 %all_to_all.16.got_ref = bf16[16,128,128]{2,1,0:T(8,128)(2,1)S(1)} all-to-all(bf16[16,128,128]{2,1,0:T(8,128)(2,1)S(1)} %analysis.1), channel_id=1, replica_groups=mesh['mem'=16,'lat'=2] {'mem'}, dimensions={0} | all-to-all | bytes 1048576 | tf_op jit(solution)/shard_map/all_to_all | solution.py:791
  67.1 1.4 %unpack.1 = f32[64,32,128]{2,1,0:T(8,128)} custom-call(bf16[16,128,128]{2,1,0:T(8,128)(2,1)S(1)} %all_to_all.16.got_ref), custom_call_target="tpu_custom_call" | custom-call | bytes 6000000 | tf_op jit(solution)/shard_map/unpack/pallas_call | solution.py:792
Async XLA Ops:
  1.7 7.9 %collective-permute-start = (s16[20,32,128]{2,1,0:T(8,128)(2,1)}, s16[20,32,128]{2,1,0:T(8,128)(2,1)S(1)}, u32[]{:S(2)}, u32[]{:S(2)}) collective-permute-start(s16[20,32,128]{2,1,0:T(8,128)(2,1)} %get-tuple-element.9), channel_id=1, source_target_pairs={{0,1},{1,0},{2,3},{3,2},{4,5},{5,4},{6,7},{7,6},{8,9},{9,8},{10,11... | collective-permute-start | bytes 491528 | tf_op jit(solution)/shard_map/ppermute | solution.py:746
  4.7 4.9 %copy-start.1 = (bf16[64,256]{1,0:T(8,128)(2,1)S(1)}, bf16[64,256]{1,0:T(8,128)(2,1)}, u32[]{:S(2)}) copy-start(bf16[64,256]{1,0:T(8,128)(2,1)} %east_ref.3) | copy-start | bytes 98308
  4.7 4.9 %copy-start.2 = (bf16[64,256]{1,0:T(8,128)(2,1)S(1)}, bf16[64,256]{1,0:T(8,128)(2,1)}, u32[]{:S(2)}) copy-start(bf16[64,256]{1,0:T(8,128)(2,1)} %north_ref.3) | copy-start | bytes 98308
  4.8 14.5 %all-to-all-start = ((s32[32,4,128]{2,1,0:T(4,128)}), s32[32,4,128]{2,1,0:T(4,128)S(1)}, u32[]{:S(2)}, u32[]{:S(2)}) async-start(s32[32,4,128]{2,1,0:T(4,128)} %get-tuple-element.12), calls=%async_computation | async-start | bytes 131072 | tf_op jit(solution)/shard_map/all_to_all | solution.py:747
  9.7 1.2 %copy-start = (f32[64,8,2,256]{3,2,1,0:T(2,128)S(1)}, f32[64,8,2,256]{3,2,1,0:T(2,128)}, u32[]{:S(2)}) copy-start(f32[64,8,2,256]{3,2,1,0:T(2,128)} %param.6) | copy-start | bytes 3145732
  19.9 23.2 %copy-start.3 = (s32[1,4,1,128]{3,2,1,0:T(1,128)S(1)}, s32[1,4,1,128]{3,2,1,0:T(1,128)}, u32[]{:S(2)}) copy-start(s32[1,4,1,128]{3,2,1,0:T(1,128)} %param.9) | copy-start | bytes 6148
  19.9 23.2 %copy-start.4 = (f32[1,4,1,128]{3,2,1,0:T(1,128)S(1)}, f32[1,4,1,128]{3,2,1,0:T(1,128)}, u32[]{:S(2)}) copy-start(f32[1,4,1,128]{3,2,1,0:T(1,128)} %param.10) | copy-start | bytes 6148
  20.0 23.2 %copy-start.5 = (f32[1,4,1,128]{3,2,1,0:T(1,128)S(1)}, f32[1,4,1,128]{3,2,1,0:T(1,128)}, u32[]{:S(2)}) copy-start(f32[1,4,1,128]{3,2,1,0:T(1,128)} %param.11) | copy-start | bytes 6148

commit v7 on v6

--- a/solution.py
+++ b/solution.py
@@ -432,18 +432,10 @@
     def load_own(row, lane):
         return own_ref[row, pl.ds(lane, members, stride=4), :]
 
-    block = 4 * CHUNK
-    for start in range(0, rows, block):
-        place = PAD + jnp.where(band == 0, start, rows - block - start)
-        stage_states(
-            load_own,
-            lambda k: start + jnp.where(band == 0, k, block - 1 - k),
-            block,
-            members,
-            matrix,
-            q_ref,
-            place,
-        )
+    def own_row(k):
+        return jnp.where(band == 0, k, rows - 1 - k)
+
+    stage_states(load_own, own_row, rows, members, matrix, q_ref, PAD)
 
     for step in range(STEPS):
         count = rows + HALO - 1 - 4 * step
@@ -615,7 +607,7 @@
             put(lower_refs, j, product(factor, lower))
         return 0
 
-    lax.fori_loop(0, ITERS - 2, newton, 0, unroll=2)
+    lax.fori_loop(0, ITERS - 2, newton, 0, unroll=5)
 
     def joined(ref, j):
         return jnp.concatenate([ref[4 * j + part] for part in range(4)], axis=1)

time: 68.8 us -> 68.6 us (level)
  no operation moved by 1% of the time
where the time goes in v7:
time: 68.6 us; the launch traced here: 68.3 us
  blocking collectives  40.4 us (59%)
  Pallas kernels  18.6 us (27%)
  starting transfers between devices  7.93 us (12%)
  local copies, waits for them, and re-layouts  1.25 us (2%)
    all_to_all x1, blocking collectives, per_device_pair(): got = lax.all_to_all(packed, 'mem', split_axis=0, concat_axis=0, tiled=True)  23.1 us
    all_to_all x1, blocking collectives, per_device_pair(): lax.all_to_all(back, 'mem', split_axis=0, concat_axis=0, tiled=True)  17.3 us
    pallas_call x1, Pallas kernels, per_device_pair(): pl.pallas_call(functools.partial(forecast_kernel, sizes), out_shape=(jax....  8.39 us
    pallas_call x1, Pallas kernels, per_device_pair(): pl.pallas_call(functools.partial(analysis_kernel, sizes), out_shape=jax.S...  6.51 us
    all_to_all x1, starting transfers between devices, per_device_pair(): lax.all_to_all(told, ('lat', 'mem'), split_axis=0, concat_axis=0, tiled=T...  4.89 us
    ppermute x1, starting transfers between devices, per_device_pair(): halo = lax.ppermute(sent, 'lat', [(0, 1), (1, 0)])  3.03 us
    pallas_call x1, Pallas kernels, per_device_pair(): pl.pallas_call(functools.partial(tell_kernel, sizes), out_shape=(jax.Shap...  1.71 us
    pallas_call x1, Pallas kernels, per_device_pair(): pl.pallas_call(functools.partial(unpack_kernel, sizes), out_shape=jax.Sha...  1.38 us
  transfers between devices with their start and end apart: 2, of which 0 were waited for; matrix products, arithmetic and copies ran while one was open for 0% of the time, Pallas kernels for 12%

profile of v7, /device:TPU:0, one launch (start us, length us, event | category | flops | bytes accessed | tf_op | source)
XLA Modules:
  0.0 68.3 jit_solution(9910770631224186268)
XLA Ops:
  0.0 1.7 %tell.1 = (s16[20,32,128]{2,1,0:T(8,128)(2,1)}, s32[32,4,128]{2,1,0:T(4,128)}) custom-call(f32[64,32,128]{2,1,0:T(8,128)} %bitcast.13, bf16[64,256]{1,0:T(8,128)(2,1)} %east_ref.3, bf16[64,256]{1,0:T(8,128)(2,1)} %north_ref.3, s32[4,128]{1,0:T(4,128)} %bitcast.15, f32[4,128]{1,0:T(4,128)} %bitcast.17, f32[4,128]{1,0:T(4,128)} %bitcast.19), custom_call_target="tpu_custom_call" | custom-call | bytes 3000000 | tf_op jit(solution)/shard_map/tell/pallas_call | solution.py:719
  1.7 3.0 %collective-permute-start = (s16[20,32,128]{2,1,0:T(8,128)(2,1)}, s16[20,32,128]{2,1,0:T(8,128)(2,1)S(1)}, u32[]{:S(2)}, u32[]{:S(2)}) collective-permute-start(s16[20,32,128]{2,1,0:T(8,128)(2,1)} %get-tuple-element.9), channel_id=1, source_target_pairs={{0,1},{1,0},{2,3},{3,2},{4,5},{5,4},{6,7},{7,6},{8,9},{9,8},{10,11... | collective-permute-start | bytes 491528 | tf_op jit(solution)/shard_map/ppermute | solution.py:738
  4.7 0.0 copy-start.1
  4.7 0.0 copy-start.2
  4.8 4.9 %all-to-all-start = ((s32[32,4,128]{2,1,0:T(4,128)}), s32[32,4,128]{2,1,0:T(4,128)S(1)}, u32[]{:S(2)}, u32[]{:S(2)}) async-start(s32[32,4,128]{2,1,0:T(4,128)} %get-tuple-element.12), calls=%async_computation | async-start | bytes 131072 | tf_op jit(solution)/shard_map/all_to_all | solution.py:739
  9.7 0.0 collective-permute-done.halo_ref
  9.7 0.0 copy-done.1
  9.7 0.0 copy-done.2
  9.7 0.0 copy-start
  9.7 1.2 %copy-done = f32[64,8,2,256]{3,2,1,0:T(2,128)S(1)} copy-done((f32[64,8,2,256]{3,2,1,0:T(2,128)S(1)}, f32[64,8,2,256]{3,2,1,0:T(2,128)}, u32[]{:S(2)}) %copy-start) | copy-done | bytes 1048600
  10.9 8.4 %forecast.1 = (s16[16,128,128]{2,1,0:T(8,128)(2,1)S(1)}, f32[16,8,8,128]{3,2,1,0:T(8,128)S(1)}) custom-call(f32[64,32,128]{2,1,0:T(8,128)S(1)} %bitcast.14, s16[20,32,128]{2,1,0:T(8,128)(2,1)S(1)} %collective-permute-done.halo_ref, bf16[64,256]{1,0:T(8,128)(2,1)S(1)} %copy-done.1, bf16[64,256]{1,0:T(8,128)(2,1)S(1)} %copy-done.2), custom_call_target="tpu_custom_call" | custom-call | bytes 36000000 | tf_op jit(solution)/shard_map/forecast/pallas_call | solution.py:743
  19.3 0.0 all-to-all-done.table_ref
  19.3 0.6 observe.1
  20.0 0.0 copy-start.3
  20.0 0.0 copy-start.4
  20.0 0.0 copy-start.5
  20.0 23.1 %all_to_all.15.got_ref = s16[16,144,128]{2,1,0:T(8,128)(2,1)S(1)} all-to-all(s16[16,144,128]{2,1,0:T(8,128)(2,1)S(1)} %observe.1), channel_id=1, replica_groups=mesh['mem'=16,'lat'=2] {'mem'}, dimensions={0} | all-to-all | bytes 1179648 | tf_op jit(solution)/shard_map/all_to_all | solution.py:765
  43.1 0.0 copy-done.3
  43.1 0.0 copy-done.4
  43.1 0.0 copy-done.5
  43.1 6.5 %analysis.1 = bf16[16,128,128]{2,1,0:T(8,128)(2,1)S(1)} custom-call(s16[16,144,128]{2,1,0:T(8,128)(2,1)S(1)} %all_to_all.15.got_ref, s32[32,4,128]{2,1,0:T(4,128)S(1)} %all-to-all-done.table_ref, s32[4,128]{1,0:T(4,128)S(1)} %bitcast.16, f32[4,128]{1,0:T(4,128)S(1)} %bitcast.18, f32[4,128]{1,0:T(4,128)S(1)} %bitcast.20), custom_call_target="tpu_custom_call" | custom-call | bytes 36000000 | tf_op jit(solution)/shard_map/analysis/pallas_call | solution.py:767
  49.7 17.3 %all_to_all.16.got_ref = bf16[16,128,128]{2,1,0:T(8,128)(2,1)S(1)} all-to-all(bf16[16,128,128]{2,1,0:T(8,128)(2,1)S(1)} %analysis.1), channel_id=1, replica_groups=mesh['mem'=16,'lat'=2] {'mem'}, dimensions={0} | all-to-all | bytes 1048576 | tf_op jit(solution)/shard_map/all_to_all | solution.py:783
  66.9 1.4 %unpack.1 = f32[64,32,128]{2,1,0:T(8,128)} custom-call(bf16[16,128,128]{2,1,0:T(8,128)(2,1)S(1)} %all_to_all.16.got_ref), custom_call_target="tpu_custom_call" | custom-call | bytes 6000000 | tf_op jit(solution)/shard_map/unpack/pallas_call | solution.py:784
Async XLA Ops:
  1.7 7.9 %collective-permute-start = (s16[20,32,128]{2,1,0:T(8,128)(2,1)}, s16[20,32,128]{2,1,0:T(8,128)(2,1)S(1)}, u32[]{:S(2)}, u32[]{:S(2)}) collective-permute-start(s16[20,32,128]{2,1,0:T(8,128)(2,1)} %get-tuple-element.9), channel_id=1, source_target_pairs={{0,1},{1,0},{2,3},{3,2},{4,5},{5,4},{6,7},{7,6},{8,9},{9,8},{10,11... | collective-permute-start | bytes 491528 | tf_op jit(solution)/shard_map/ppermute | solution.py:738
  4.7 4.9 %copy-start.1 = (bf16[64,256]{1,0:T(8,128)(2,1)S(1)}, bf16[64,256]{1,0:T(8,128)(2,1)}, u32[]{:S(2)}) copy-start(bf16[64,256]{1,0:T(8,128)(2,1)} %east_ref.3) | copy-start | bytes 98308
  4.7 4.9 %copy-start.2 = (bf16[64,256]{1,0:T(8,128)(2,1)S(1)}, bf16[64,256]{1,0:T(8,128)(2,1)}, u32[]{:S(2)}) copy-start(bf16[64,256]{1,0:T(8,128)(2,1)} %north_ref.3) | copy-start | bytes 98308
  4.8 14.6 %all-to-all-start = ((s32[32,4,128]{2,1,0:T(4,128)}), s32[32,4,128]{2,1,0:T(4,128)S(1)}, u32[]{:S(2)}, u32[]{:S(2)}) async-start(s32[32,4,128]{2,1,0:T(4,128)} %get-tuple-element.12), calls=%async_computation | async-start | bytes 131072 | tf_op jit(solution)/shard_map/all_to_all | solution.py:739
  9.7 1.2 %copy-start = (f32[64,8,2,256]{3,2,1,0:T(2,128)S(1)}, f32[64,8,2,256]{3,2,1,0:T(2,128)}, u32[]{:S(2)}) copy-start(f32[64,8,2,256]{3,2,1,0:T(2,128)} %param.6) | copy-start | bytes 3145732
  20.0 23.2 %copy-start.3 = (s32[1,4,1,128]{3,2,1,0:T(1,128)S(1)}, s32[1,4,1,128]{3,2,1,0:T(1,128)}, u32[]{:S(2)}) copy-start(s32[1,4,1,128]{3,2,1,0:T(1,128)} %param.9) | copy-start | bytes 6148
  20.0 23.2 %copy-start.4 = (f32[1,4,1,128]{3,2,1,0:T(1,128)S(1)}, f32[1,4,1,128]{3,2,1,0:T(1,128)}, u32[]{:S(2)}) copy-start(f32[1,4,1,128]{3,2,1,0:T(1,128)} %param.10) | copy-start | bytes 6148
  20.0 23.2 %copy-start.5 = (f32[1,4,1,128]{3,2,1,0:T(1,128)S(1)}, f32[1,4,1,128]{3,2,1,0:T(1,128)}, u32[]{:S(2)}) copy-start(f32[1,4,1,128]{3,2,1,0:T(1,128)} %param.11) | copy-start | bytes 6148
